TPU v7x, 256 devices: a whole 4x4x8 slice. The times are simulated.
256 devices in a mesh: row: 16 (over z, core), col: 16 (over x, y).
Axes of the slice: x: 4, y: 4, z: 8, core: 2. Of those that a mesh axis runs over, the one named last changes fastest.
Arguments:
- acts: bfloat16 [512, 16384], P('col', 'row'), may hold values from -6 to 6
- gate_weight: bfloat16 [16384, 26624], P('row', 'col'), may hold values from -0.046875 to 0.046875
- up_weight: bfloat16 [16384, 26624], P('row', 'col'), may hold values from -0.046875 to 0.046875
- down_weight: bfloat16 [26624, 16384], P('col', 'row'), may hold values from -0.0390625 to 0.0390625
Outputs:
- block_out: bfloat16 [512, 16384], P('col', 'row')
All inputs are finite; a program needn't handle non-finite values.
Results may differ from a plain program's by a relative error of at most 0.019.
Values may be sent and summed in bfloat16 or wider, within the bound.
No kernel may reach another device: no remote copies, remote signals or barrier semaphores. Data moves between devices by JAX's collectives and lax.ppermute only.
A program may use at most 64 MiB of HBM per device.

v0:
```python
import jax
import jax.numpy as jnp
from jax import lax
from jax.sharding import PartitionSpec as P


def on_device(acts, gate_weight, up_weight, down_weight):
    width = gate_weight.shape[1]
    piece = lax.all_gather(acts, "col", axis=0, tiled=True)
    partial_value = jnp.concatenate(
        [
            jnp.dot(piece, gate_weight, preferred_element_type=jnp.float32),
            jnp.dot(piece, up_weight, preferred_element_type=jnp.float32),
        ],
        axis=1,
    )
    summed = lax.psum_scatter(partial_value, "row", scatter_dimension=0, tiled=True)
    hidden = (jax.nn.silu(summed[:, :width]) * summed[:, width:]).astype(jnp.bfloat16)
    terms = jnp.dot(
        lax.all_gather(hidden, "row", axis=0, tiled=True),
        down_weight,
        preferred_element_type=jnp.float32,
    )
    result = lax.psum_scatter(terms.astype(jnp.bfloat16), "col", scatter_dimension=0, tiled=True)
    return result


def solution(mesh):
    in_specs = (P("col", "row"), P("row", "col"), P("row", "col"), P("col", "row"))
    out_specs = P("col", "row")
    return jax.shard_map(
        on_device, mesh=mesh, in_specs=in_specs, out_specs=out_specs, check_vma=False
    )
```

profile of v0, /device:TPU:1, one launch (start us, length us, event | category | flops | bytes accessed | tf_op | source)
XLA Modules:
  0.0 264.3 jit_solution(4808323874564527482)
XLA Ops:
  6.5 0.0 copy-start
  6.5 0.0 all-gather.3.cloned.1.call-start
  6.5 0.7 all-gather.3.cloned.1.call-update
  7.3 0.0 reduce-scatter.3.cloned.1.call-start
  7.3 52.6 %all-gather.3.cloned.1.call-done = bf16[512,1024]{1,0:T(8,128)(2,1)} async-done(((bf16[32,1024]{1,0:T(8,128)(2,1)}), bf16[512,1024]{1,0:T(8,128)(2,1)}) %all-gather.3.cloned.1.call-update) | async-done | bytes 1048592 | tf_op jit(solution)/shard_map/all_gather | solution.py:9
  59.9 0.0 copy-done
  59.9 0.0 copy-start.1
  59.9 0.0 copy-start.2
  59.9 3.4 %fusion.2 = f32[512,1664]{1,0:T(8,128)S(1)} fusion(bf16[512,1024]{1,0:T(8,128)(2,1)} %all-gather.3.cloned.1.call-done, bf16[1024,1664]{1,0:T(8,128)(2,1)S(1)} %copy-done), kind=kOutput, calls=%fused_computation.5 | convolution fusion | flops 1744830464 | bytes 7864320 | tf_op jit(solution)/shard_map/dot_general | solution.py:13
  63.4 0.0 copy-done.1
  63.4 0.0 copy-done.2
  63.4 2.1 fusion.1
  65.5 3.3 %pad_maximum_fusion = f32[512,3328]{1,0:T(8,128)} fusion(f32[512,1664]{1,0:T(8,128)S(1)} %fusion.2, f32[512,1664]{1,0:T(8,128)S(1)} %fusion.1), kind=kLoop, calls=%fused_computation | loop fusion | flops 1703936 | bytes 13631488 | tf_op jit(solution)/shard_map/concatenate | solution.py:10
  68.8 0.0 reduce-scatter.3.cloned.1.call-update
  68.8 0.0 all-gather.5.cloned.1.call-start
  68.8 65.3 %reduce-scatter.3.cloned.1.call-done = f32[32,3328]{1,0:T(8,128)} async-done(((f32[512,3328]{1,0:T(8,128)}), f32[32,3328]{1,0:T(8,128)}) %reduce-scatter.3.cloned.1.call-update) | async-done | bytes 426000 | tf_op jit(solution)/shard_map/reduce_scatter | solution.py:17
  134.1 1.7 fusion
  135.9 0.0 all-gather.5.cloned.1.call-update
  135.9 0.0 reduce-scatter.5.cloned.1.call-start
  135.9 41.5 %all-gather.5.cloned.1.call-done = bf16[512,1664]{1,0:T(8,128)(2,1)} async-done(((bf16[32,1664]{1,0:T(8,128)(2,1)}), bf16[512,1664]{1,0:T(8,128)(2,1)}) %all-gather.5.cloned.1.call-update) | async-done | bytes 1703952 | tf_op jit(solution)/shard_map/all_gather | solution.py:20
  177.4 5.5 %convolution_convert_fusion = bf16[512,1024]{1,0:T(8,128)(2,1)} fusion(bf16[512,1664]{1,0:T(8,128)(2,1)} %all-gather.5.cloned.1.call-done, bf16[1664,1024]{1,0:T(8,128)(2,1)} %param.7), kind=kOutput, calls=%fused_computation.1 | convolution fusion | flops 1745354752 | bytes 6160384 | tf_op jit(solution)/shard_map/dot_general | solution.py:19
  182.9 0.0 reduce-scatter.5.cloned.1.call-update
  183.0 74.8 %reduce-scatter.5.cloned.1.call-done = bf16[32,1024]{1,0:T(8,128)(2,1)} async-done(((bf16[512,1024]{1,0:T(8,128)(2,1)}), bf16[32,1024]{1,0:T(8,128)(2,1)}) %reduce-scatter.5.cloned.1.call-update) | async-done | bytes 65552 | tf_op jit(solution)/shard_map/reduce_scatter | solution.py:24
Async XLA Ops:
  6.5 53.4 %copy-start = (bf16[1024,1664]{1,0:T(8,128)(2,1)S(1)}, bf16[1024,1664]{1,0:T(8,128)(2,1)}, u32[]{:S(2)}) copy-start(bf16[1024,1664]{1,0:T(8,128)(2,1)} %param.6) | copy-start | bytes 10223620
  6.5 53.4 %all-gather.3.cloned.1.call-start = ((), (), s32[]{:S(2)}) async-start(), calls=%async_computation.2 | async-start | bytes 1114112 | tf_op jit(solution)/shard_map/all_gather | solution.py:9
  7.3 126.9 %reduce-scatter.3.cloned.1.call-start = ((), (), s32[]{:S(2)}) async-start(), calls=%async_computation.3 | async-start | bytes 7241728 | tf_op jit(solution)/shard_map/reduce_scatter | solution.py:17
  59.9 3.4 %copy-start.1 = (bf16[1024,1664]{1,0:T(8,128)(2,1)S(1)}, bf16[1024,1664]{1,0:T(8,128)(2,1)}, u32[]{:S(2)}) copy-start(bf16[1024,1664]{1,0:T(8,128)(2,1)} %param.5) | copy-start | bytes 10223620
  59.9 3.5 %copy-start.2 = (bf16[512,1024]{1,0:T(8,128)(2,1)S(1)}, bf16[512,1024]{1,0:T(8,128)(2,1)}, u32[]{:S(2)}) copy-start(bf16[512,1024]{1,0:T(8,128)(2,1)} %all-gather.3.cloned.1.call-done) | copy-start | bytes 3145732
  68.8 108.6 %all-gather.5.cloned.1.call-start = ((), (), s32[]{:S(2)}) async-start(), calls=%async_computation.4 | async-start | bytes 1810432 | tf_op jit(solution)/shard_map/all_gather | solution.py:20
  135.9 121.8 %reduce-scatter.5.cloned.1.call-start = ((), (), s32[]{:S(2)}) async-start(), calls=%async_computation.5 | async-start | bytes 1114112 | tf_op jit(solution)/shard_map/reduce_scatter | solution.py:24
Sparse Core Ops, SparseCore 0:
  9.8 50.0 all-gather.2
  68.9 65.1 reduce-scatter.2
  136.0 41.3 all-gather.4
  183.1 74.5 reduce-scatter.4
where the time goes:
time: 265 us; the launch traced here: 264 us
  waiting for transfers between devices  235 us (89%)
  between operations  13.2 us (5%)
  matrix products  11.1 us (4%)
  other arithmetic  5.04 us (2%)
    reduce_scatter x1, waiting for transfers between devices, on_device(): lax.psum_scatter(terms.astype(jnp.bfloat16), 'col', scatter_dimension=0,...  74.8 us
    reduce_scatter x1, waiting for transfers between devices, on_device(): lax.psum_scatter(partial_value, 'row', scatter_dimension=0, tiled=True)  65.3 us
    all_gather x1, waiting for transfers between devices, on_device(): piece = lax.all_gather(acts, 'col', axis=0, tiled=True)  52.6 us
    all_gather x1, waiting for transfers between devices, on_device(): lax.all_gather(hidden, 'row', axis=0, tiled=True)  41.5 us
    dot_general x1, matrix products, on_device(): jnp.dot(lax.all_gather(hidden, 'row', axis=0, tiled=True), down_weight, p...  5.54 us
  transfers between devices with their start and end apart: 4, of which 4 were waited for; matrix products, arithmetic and copies ran while one was open for 0% of the time, Pallas kernels for 0%

commit v1 on v0

v1 whole, which is shorter than its diff:
```python
import jax
import jax.numpy as jnp
from jax import lax
from jax.sharding import Mesh, PartitionSpec as P

BF = jnp.bfloat16
F32 = jnp.float32


def shift(v, axis, n, s):
    return lax.ppermute(v, axis, [(i, (i + s) % n) for i in range(n)])


def block(x, i):
    return lax.dynamic_index_in_dim(x, i, 0, keepdims=False)


def gather_near(v, axis, n):
    return jnp.concatenate([v] + [shift(v, axis, n, s) for s in range(1, n)], 0)


def unrotate(v, axis, n):
    me = lax.axis_index(axis)
    v = jnp.flip(v, 0)
    return jnp.roll(v, me + 1, 0)


def reduce_ring(x, axis, n):
    me, h, c = lax.axis_index(axis), n // 2, x.shape[2]
    cut = c // 256 * 128
    far = block(x, (me + h) % n)
    right, left = shift(far[:, :cut], axis, n, 1), shift(far[:, cut:], axis, n, -1)
    for k in range(h - 1, 0, -1):
        ours_r, ours_l = block(x, (me + k) % n), block(x, (me - k) % n)
        if k == h - 1:
            right = jnp.concatenate([ours_r[:, :cut] + right, ours_r[:, cut:]], 1)
            left = jnp.concatenate([ours_l[:, :cut], ours_l[:, cut:] + left], 1)
        else:
            right, left = ours_r + right, ours_l + left
        right, left = shift(right, axis, n, 1), shift(left, axis, n, -1)
    return block(x, me).astype(F32) + right.astype(F32) + left.astype(F32)


def on_device(acts, gate_weight, up_weight, down_weight):
    width = gate_weight.shape[1]
    nz, nx, ny = lax.axis_size("z"), lax.axis_size("x"), lax.axis_size("y")
    core = lax.axis_index("core")
    piece = gather_near(acts, "x", nx).reshape(nx, -1, acts.shape[1])
    piece = unrotate(piece, "x", nx).reshape(-1, acts.shape[1])
    piece = gather_near(piece, "y", ny).reshape(ny, nx, -1, acts.shape[1])
    piece = unrotate(piece, "y", ny).swapaxes(0, 1).reshape(-1, acts.shape[1])
    half = piece.shape[0] // 2

    def both(rows):
        return jnp.concatenate(
            [jnp.dot(rows, w, preferred_element_type=F32) for w in (gate_weight, up_weight)], 1
        )

    theirs = both(lax.dynamic_slice_in_dim(piece, (1 - core) * half, half)).astype(BF)
    theirs = shift(theirs, "core", 2, 1)
    ours = both(lax.dynamic_slice_in_dim(piece, core * half, half))
    ours = (ours + theirs.astype(F32)).astype(BF).reshape(nz, half // nz, 2 * width)
    summed = reduce_ring(ours, "z", nz)
    hidden = (jax.nn.silu(summed[:, :width]) * summed[:, width:]).astype(BF)
    hidden = gather_near(hidden, "z", nz).reshape(nz, -1, width)
    hidden = unrotate(hidden, "z", nz).reshape(half, width)
    other = shift(hidden, "core", 2, 1)
    low = jnp.where(core == 0, hidden, other)
    high = jnp.where(core == 0, other, hidden)
    terms = jnp.dot(jnp.concatenate([low, high], 0), down_weight, preferred_element_type=F32)
    terms = terms.astype(BF).reshape(nx * ny, -1, down_weight.shape[1])
    terms = lax.all_to_all(terms, ("x", "y"), 0, 0, tiled=True)
    return jnp.sum(terms.astype(F32), 0).astype(BF)


def solution(mesh):
    grid = Mesh(mesh.devices.reshape(8, 2, 4, 4), ("z", "core", "x", "y"))
    row, col = ("z", "core"), ("x", "y")
    in_specs = (P(col, row), P(row, col), P(row, col), P(col, row))
    return jax.shard_map(
        on_device, mesh=grid, in_specs=in_specs, out_specs=P(col, row), check_vma=False
    )
```

time: 265 us -> 154 us (0.58)
  waiting for transfers between devices: 235 us -> 42 us
  starting transfers between devices: 0.12 us -> 40.6 us
  other arithmetic: 5.04 us -> 26.6 us
  blocking collectives: 0 us -> 21.5 us
  local copies, waits for them, and re-layouts: 0.01 us -> 14.9 us
  between operations: 13.2 us -> 0.17 us
  matrix products: 11.1 us -> 7.74 us
    reduce_scatter x2 -> x0, waiting for transfers between devices: 140 us -> none  [the longest x1 74.8 us: on_device(): lax.psum_scatter(terms.astype(jnp.bfloat16), 'col', scatter_dimension=0,...]
    all_gather x2 -> x0, waiting for transfers between devices: 94.1 us -> none  [the longest x1 52.6 us: on_device(): piece = lax.all_gather(acts, 'col', axis=0, tiled=True)]
    ppermute x0 -> x23, waiting for transfers between devices: none -> 42 us  [shift(): return lax.ppermute(v, axis, [(i, (i + s) % n) for i in range(n)])]
    ppermute x0 -> x23, starting transfers between devices: none -> 40.6 us  [shift(): return lax.ppermute(v, axis, [(i, (i + s) % n) for i in range(n)])]
    all_to_all x0 -> x1, blocking collectives: none -> 21.5 us  [on_device(): terms = lax.all_to_all(terms, ('x', 'y'), 0, 0, tiled=True)]
    add x0 -> x5, other arithmetic: none -> 7.64 us  [the longest x3 5.46 us: reduce_ring(): right, left = (ours_r + right, ours_l + left)]
    concatenate x1 -> x7, other arithmetic: 3.29 us -> 10.1 us  [the longest x2 4.2 us: unrotate(): return jnp.roll(v, me + 1, 0)]
    unnamed x6 -> x20, local copies, waits for them, and re-layouts: 0.01 us -> 6.56 us
  transfers between devices with their start and end apart: 4 -> 23, of which waited for: 4 -> 12; matrix products, arithmetic and copies ran while one was open for 0% -> 9% of each run, Pallas kernels for 0% -> 0%
where the time goes in v1:
time: 154 us; the launch traced here: 153 us
  waiting for transfers between devices  42 us (27%)
  starting transfers between devices  40.6 us (26%)
  other arithmetic  26.6 us (17%)
  blocking collectives  21.5 us (14%)
  local copies, waits for them, and re-layouts  14.9 us (10%)
  matrix products  7.74 us (5%)
    ppermute x23, waiting for transfers between devices, shift(): return lax.ppermute(v, axis, [(i, (i + s) % n) for i in range(n)])  42 us
    ppermute x23, starting transfers between devices, shift(): return lax.ppermute(v, axis, [(i, (i + s) % n) for i in range(n)])  40.6 us
    all_to_all x1, blocking collectives, on_device(): terms = lax.all_to_all(terms, ('x', 'y'), 0, 0, tiled=True)  21.5 us
    unnamed x20, local copies, waits for them, and re-layouts  6.56 us
    rev x3, local copies, waits for them, and re-layouts, unrotate(): v = jnp.flip(v, 0)  6.08 us
    dot_general x4, matrix products, both(): jnp.dot(rows, w, preferred_element_type=F32)  5.68 us
    add x3, other arithmetic, reduce_ring(): right, left = (ours_r + right, ours_l + left)  5.46 us
    concatenate x2, other arithmetic, unrotate(): return jnp.roll(v, me + 1, 0)  4.2 us
  transfers between devices with their start and end apart: 23, of which 12 were waited for; matrix products, arithmetic and copies ran while one was open for 9% of the time, Pallas kernels for 0%

profile of v1, /device:TPU:1, one launch (start us, length us, event | category | flops | bytes accessed | tf_op | source)
XLA Modules:
  0.0 153.4 jit_solution(14189083881980669592)
XLA Ops:
  0.0 2.0 %collective-permute-start = (bf16[32,1024]{1,0:T(8,128)(2,1)}, bf16[32,1024]{1,0:T(8,128)(2,1)S(1)}, u32[]{:S(2)}, u32[]{:S(2)}) collective-permute-start(bf16[32,1024]{1,0:T(8,128)(2,1)} %param.4), channel_id=1, source_target_pairs={{0,4},{4,8},{8,12},{12,0},{1,5},{5,9},{9,13},{13,1},{2,6},{6,10},{... | collective-permute-start | bytes 196616 | tf_op jit(solution)/shard_map/ppermute | solution.py:11
  2.0 2.5 %collective-permute-start.1 = (bf16[32,1024]{1,0:T(8,128)(2,1)}, bf16[32,1024]{1,0:T(8,128)(2,1)S(1)}, u32[]{:S(2)}, u32[]{:S(2)}) collective-permute-start(bf16[32,1024]{1,0:T(8,128)(2,1)} %param.4), channel_id=1, source_target_pairs={{0,8},{4,12},{8,0},{12,4},{1,9},{5,13},{9,1},{13,5},{2,10},{6,14},... | collective-permute-start | bytes 196616 | tf_op jit(solution)/shard_map/ppermute | solution.py:11
  4.5 1.2 collective-permute-start.2
  5.7 1.7 %collective-permute-done.1 = bf16[32,1024]{1,0:T(8,128)(2,1)S(1)} collective-permute-done((bf16[32,1024]{1,0:T(8,128)(2,1)}, bf16[32,1024]{1,0:T(8,128)(2,1)S(1)}, u32[]{:S(2)}, u32[]{:S(2)}) %collective-permute-start.1) | collective-permute-done | bytes 65568 | tf_op jit(solution)/shard_map/ppermute | solution.py:11
  7.3 0.8 collective-permute-done.2
  8.1 1.6 %pad_maximum_fusion.2 = bf16[128,1024]{1,0:T(8,128)(2,1)} fusion(bf16[32,1024]{1,0:T(8,128)(2,1)} %collective-permute-done.2, bf16[32,1024]{1,0:T(8,128)(2,1)S(1)} %collective-permute-done.1, bf16[32,1024]{1,0:T(8,128)(2,1)S(1)} %collective-permute-done, bf16[32,1024]{1,0:T(8,128)(2,1)} %param.4), kind=kLoop, calls=%fused_computation.31 | loop fusion | flops 1048576 | bytes 524288 | tf_op jit(solution)/shard_map/concatenate | solution.py:19
  9.7 1.7 %rev.12 = bf16[4,32,1024]{2,1,0:T(8,128)(2,1)} reverse(bf16[4,32,1024]{2,1,0:T(8,128)(2,1)} %bitcast.46), dimensions={0} | reverse | bytes 524288 | tf_op jit(solution)/shard_map/jit(_flip)/rev | solution.py:24
  11.4 1.8 %fusion.18 = bf16[4,32,1024]{2,1,0:T(8,128)(2,1)} fusion(s32[]{:T(128)S(6)} %select_n.106, bf16[4,32,1024]{2,1,0:T(8,128)(2,1)} %rev.12), kind=kLoop, calls=%fused_computation.30 | loop fusion | flops 131072 | bytes 524292 | tf_op jit(solution)/shard_map/jit(_roll_dynamic)/concatenate | solution.py:25
  13.1 1.5 %collective-permute-start.3 = (bf16[128,1024]{1,0:T(8,128)(2,1)}, bf16[128,1024]{1,0:T(8,128)(2,1)}, u32[]{:S(2)}, u32[]{:S(2)}) collective-permute-start(bf16[128,1024]{1,0:T(8,128)(2,1)} %bitcast.1), channel_id=1, source_target_pairs={{0,1},{1,2},{2,3},{3,0},{4,5},{5,6},{6,7},{7,4},{8,9},{9,10},{10,1... | collective-permute-start | bytes 786440 | tf_op jit(solution)/shard_map/ppermute | solution.py:11
  14.7 2.6 %collective-permute-start.4 = (bf16[128,1024]{1,0:T(8,128)(2,1)}, bf16[128,1024]{1,0:T(8,128)(2,1)}, u32[]{:S(2)}, u32[]{:S(2)}) collective-permute-start(bf16[128,1024]{1,0:T(8,128)(2,1)} %bitcast.1), channel_id=1, source_target_pairs={{0,2},{1,3},{2,0},{3,1},{4,6},{5,7},{6,4},{7,5},{8,10},{9,11},{10,... | collective-permute-start | bytes 786440 | tf_op jit(solution)/shard_map/ppermute | solution.py:11
  17.3 1.1 collective-permute-start.5
  18.4 2.2 %collective-permute-done.3 = bf16[128,1024]{1,0:T(8,128)(2,1)} collective-permute-done((bf16[128,1024]{1,0:T(8,128)(2,1)}, bf16[128,1024]{1,0:T(8,128)(2,1)}, u32[]{:S(2)}, u32[]{:S(2)}) %collective-permute-start.3) | collective-permute-done | bytes 262176 | tf_op jit(solution)/shard_map/ppermute | solution.py:11
  20.6 7.0 %collective-permute-done.4 = bf16[128,1024]{1,0:T(8,128)(2,1)} collective-permute-done((bf16[128,1024]{1,0:T(8,128)(2,1)}, bf16[128,1024]{1,0:T(8,128)(2,1)}, u32[]{:S(2)}, u32[]{:S(2)}) %collective-permute-start.4) | collective-permute-done | bytes 262176 | tf_op jit(solution)/shard_map/ppermute | solution.py:11
  27.6 2.2 %pad_maximum_fusion.1 = bf16[512,1024]{1,0:T(8,128)(2,1)} fusion(bf16[128,1024]{1,0:T(8,128)(2,1)} %collective-permute-done.5, bf16[128,1024]{1,0:T(8,128)(2,1)} %collective-permute-done.4, bf16[128,1024]{1,0:T(8,128)(2,1)} %collective-permute-done.3, bf16[128,1024]{1,0:T(8,128)(2,1)} %bitcast.1), kind=kLoop, calls=%fused_computation.16 | loop fusion | flops 4194304 | bytes 2097152 | tf_op jit(solution)/shard_map/concatenate | solution.py:19
  29.8 2.3 %rev.13 = bf16[4,4,32,1024]{3,2,1,0:T(8,128)(2,1)} reverse(bf16[4,4,32,1024]{3,2,1,0:T(8,128)(2,1)} %bitcast.39), dimensions={0} | reverse | bytes 2097152 | tf_op jit(solution)/shard_map/jit(_flip)/rev | solution.py:24
  32.1 1.7 %fusion.9 = bf16[4,4,32,1024]{3,2,0,1:T(8,128)(2,1)S(1)} fusion(s32[]{:T(128)S(6)} %select_n.108, bf16[4,4,32,1024]{3,2,1,0:T(8,128)(2,1)} %rev.13), kind=kLoop, calls=%fused_computation.15 | loop fusion | flops 524288 | bytes 2097156 | tf_op jit(solution)/shard_map/transpose | solution.py:51
  34.4 1.1 convolution_convert_fusion
  35.6 1.1 convolution_convert_fusion.1
  36.7 1.3 pad_maximum_fusion
  38.0 2.9 %collective-permute-start.6 = (bf16[256,3328]{1,0:T(8,128)(2,1)}, bf16[256,3328]{1,0:T(8,128)(2,1)}, u32[]{:S(2)}, u32[]{:S(2)}) collective-permute-start(bf16[256,3328]{1,0:T(8,128)(2,1)} %pad_maximum_fusion), channel_id=1, source_target_pairs={{0,16},{16,0},{1,17},{17,1},{2,18},{18,2},{3,19},{19,3},{4,20},{20... | collective-permute-start | bytes 5111816 | tf_op jit(solution)/shard_map/ppermute | solution.py:11
  40.9 2.3 %fusion.15 = f32[256,1664]{1,0:T(8,128)S(1)} fusion(bf16[1024,1664]{1,0:T(8,128)(2,1)S(1)} %copy-done, bf16[512,1024]{1,0:T(8,128)(2,1)} %bitcast.43, s32[]{:T(128)S(6)} %select_n.109), kind=kOutput, calls=%fused_computation.26 | convolution fusion | flops 872415232 | bytes 5636100 | tf_op jit(solution)/shard_map/dot_general | solution.py:56
  43.4 1.1 fusion.13
  44.5 1.8 %fusion = bf16[256,3328]{1,0:T(8,128)(2,1)S(1)} fusion(f32[256,1664]{1,0:T(8,128)S(1)} %fusion.13, f32[256,1664]{1,0:T(8,128)S(1)} %fusion.15, bf16[256,3328]{1,0:T(8,128)(2,1)} %collective-permute-done.6), kind=kLoop, calls=%fused_computation.1 | loop fusion | flops 3407872 | bytes 6815744 | tf_op jit(solution)/shard_map/convert_element_type | solution.py:62
  46.3 1.2 copy-done.1
  47.5 0.8 dynamic-slice_bitcast_fusion.2
  48.3 0.7 fusion.26
  49.0 1.6 %collective-permute-start.7 = (bf16[32,1664]{1,0:T(8,128)(2,1)}, bf16[32,1664]{1,0:T(8,128)(2,1)S(1)}, u32[]{:S(2)}, u32[]{:S(2)}) collective-permute-start(bf16[32,1664]{1,0:T(8,128)(2,1)} %get-tuple-element.16), channel_id=1, source_target_pairs={{0,32},{32,64},{64,96},{96,128},{128,160},{160,192},{192,224},{224... | collective-permute-start | bytes 319496 | tf_op jit(solution)/shard_map/ppermute | solution.py:11
  50.7 3.9 %collective-permute-start.11 = (bf16[32,1664]{1,0:T(8,128)(2,1)}, bf16[32,1664]{1,0:T(8,128)(2,1)S(1)}, u32[]{:S(2)}, u32[]{:S(2)}) collective-permute-start(bf16[32,1664]{1,0:T(8,128)(2,1)} %get-tuple-element.17), channel_id=1, source_target_pairs={{0,224},{32,0},{64,32},{96,64},{128,96},{160,128},{192,160},{224,1... | collective-permute-start | bytes 319496 | tf_op jit(solution)/shard_map/ppermute | solution.py:11
  54.6 3.3 %collective-permute-done.7 = bf16[32,1664]{1,0:T(8,128)(2,1)S(1)} collective-permute-done((bf16[32,1664]{1,0:T(8,128)(2,1)}, bf16[32,1664]{1,0:T(8,128)(2,1)S(1)}, u32[]{:S(2)}, u32[]{:S(2)}) %collective-permute-start.7) | collective-permute-done | bytes 106528 | tf_op jit(solution)/shard_map/ppermute | solution.py:11
  57.9 1.0 slice_add_fusion.1
  59.0 1.0 fusion.27
  59.9 0.7 pad_maximum_fusion.4
  60.6 2.7 %collective-permute-start.12 = (bf16[32,3328]{1,0:T(8,128)(2,1)}, bf16[32,3328]{1,0:T(8,128)(2,1)}, u32[]{:S(2)}, u32[]{:S(2)}) collective-permute-start(bf16[32,3328]{1,0:T(8,128)(2,1)} %pad_maximum_fusion.4), channel_id=1, source_target_pairs={{0,224},{32,0},{64,32},{96,64},{128,96},{160,128},{192,160},{224,1... | collective-permute-start | bytes 638984 | tf_op jit(solution)/shard_map/ppermute | solution.py:11
  63.3 2.7 %collective-permute-done.8 = bf16[32,3328]{1,0:T(8,128)(2,1)S(1)} collective-permute-done((bf16[32,3328]{1,0:T(8,128)(2,1)S(1)}, bf16[32,3328]{1,0:T(8,128)(2,1)S(1)}, u32[]{:S(2)}, u32[]{:S(2)}) %collective-permute-start.8) | collective-permute-done | bytes 213024 | tf_op jit(solution)/shard_map/ppermute | solution.py:11
  66.0 1.7 %bitcast_add_fusion.2 = bf16[32,3328]{1,0:T(8,128)(2,1)} fusion(bf16[32,3328]{1,0:T(8,128)(2,1)S(1)} %collective-permute-done.8, bf16[8,32,3328]{2,1,0:T(8,128)(2,1)} %bitcast.35, s32[]{:T(128)S(6)} %select_n.115), kind=kLoop, calls=%fused_computation.38 | loop fusion | flops 106496 | bytes 638980 | tf_op jit(solution)/shard_map/add | solution.py:39
  67.7 6.2 %collective-permute-done.9 = bf16[32,3328]{1,0:T(8,128)(2,1)} collective-permute-done((bf16[32,3328]{1,0:T(8,128)(2,1)}, bf16[32,3328]{1,0:T(8,128)(2,1)}, u32[]{:S(2)}, u32[]{:S(2)}) %collective-permute-start.9) | collective-permute-done | bytes 213024 | tf_op jit(solution)/shard_map/ppermute | solution.py:11
  73.9 2.1 %bitcast_add_fusion.3 = (bf16[32,3328]{1,0:T(8,128)(2,1)}, bf16[32,3328]{1,0:T(8,128)(2,1)}) fusion(bf16[32,3328]{1,0:T(8,128)(2,1)} %collective-permute-done.9, bf16[8,32,3328]{2,1,0:T(8,128)(2,1)} %bitcast.36, s32[]{:T(128)S(6)} %select_n.113, bf16[32,3328]{1,0:T(8,128)(2,1)} %collective-permute-done.12, s32[]{:T(128)S(6)} %select_n.123), kind=kLoop, calls=%fused_computation.39 | loop fusion | flops 212992 | bytes 1277960 | tf_op jit(solution)/shard_map/add | solution.py:39
  76.0 1.5 collective-permute-start.10
  77.4 3.5 %collective-permute-done.13 = bf16[32,3328]{1,0:T(8,128)(2,1)} collective-permute-done((bf16[32,3328]{1,0:T(8,128)(2,1)}, bf16[32,3328]{1,0:T(8,128)(2,1)}, u32[]{:S(2)}, u32[]{:S(2)}) %collective-permute-start.13) | collective-permute-done | bytes 213024 | tf_op jit(solution)/shard_map/ppermute | solution.py:11
  81.0 1.7 %bitcast_add_fusion.1 = bf16[32,3328]{1,0:T(8,128)(2,1)} fusion(bf16[32,3328]{1,0:T(8,128)(2,1)} %collective-permute-done.13, bf16[8,32,3328]{2,1,0:T(8,128)(2,1)} %bitcast.37, s32[]{:T(128)S(6)} %select_n.121), kind=kLoop, calls=%fused_computation.37 | loop fusion | flops 106496 | bytes 638980 | tf_op jit(solution)/shard_map/add | solution.py:39
  82.7 1.2 collective-permute-start.14
  84.0 3.8 %collective-permute-done.14 = bf16[32,3328]{1,0:T(8,128)(2,1)} collective-permute-done((bf16[32,3328]{1,0:T(8,128)(2,1)}, bf16[32,3328]{1,0:T(8,128)(2,1)}, u32[]{:S(2)}, u32[]{:S(2)}) %collective-permute-start.14) | collective-permute-done | bytes 213024 | tf_op jit(solution)/shard_map/ppermute | solution.py:11
  87.8 1.2 fusion.17
  89.0 0.7 constant_dynamic-update-slice_fusion.7
  89.7 3.7 %collective-permute-start.16 = (bf16[32,1664]{1,0:T(8,128)(2,1)S(1)}, bf16[32,1664]{1,0:T(8,128)(2,1)S(1)}, u32[]{:S(2)}, u32[]{:S(2)}) collective-permute-start(bf16[32,1664]{1,0:T(8,128)(2,1)S(1)} %get-tuple-element.6), channel_id=1, source_target_pairs={{0,64},{32,96},{64,128},{96,160},{128,192},{160,224},{192,0},{224,... | collective-permute-start | bytes 319496 | tf_op jit(solution)/shard_map/ppermute | solution.py:11
  93.3 3.0 %collective-permute-start.18 = (bf16[32,1664]{1,0:T(8,128)(2,1)S(1)}, bf16[32,1664]{1,0:T(8,128)(2,1)S(1)}, u32[]{:S(2)}, u32[]{:S(2)}) collective-permute-start(bf16[32,1664]{1,0:T(8,128)(2,1)S(1)} %get-tuple-element.6), channel_id=1, source_target_pairs={{0,128},{32,160},{64,192},{96,224},{128,0},{160,32},{192,64},{224,... | collective-permute-start | bytes 319496 | tf_op jit(solution)/shard_map/ppermute | solution.py:11
  96.3 3.5 %collective-permute-start.19 = (bf16[32,1664]{1,0:T(8,128)(2,1)S(1)}, bf16[32,1664]{1,0:T(8,128)(2,1)S(1)}, u32[]{:S(2)}, u32[]{:S(2)}) collective-permute-start(bf16[32,1664]{1,0:T(8,128)(2,1)S(1)} %get-tuple-element.6), channel_id=1, source_target_pairs={{0,160},{32,192},{64,224},{96,0},{128,32},{160,64},{192,96},{224,1... | collective-permute-start | bytes 319496 | tf_op jit(solution)/shard_map/ppermute | solution.py:11
  99.8 1.3 collective-permute-start.20
  101.1 1.5 %constant_dynamic-update-slice_fusion.6 = bf16[256,1664]{1,0:T(8,128)(2,1)} fusion(bf16[256,1664]{1,0:T(8,128)(2,1)} %get-tuple-element.5, bf16[32,1664]{1,0:T(8,128)(2,1)} %collective-permute-done.15), kind=kLoop, calls=%fused_computation.51 | loop fusion | bytes 212992
  102.7 1.4 collective-permute-start.21
  104.1 0.7 constant_dynamic-update-slice_fusion.5
  104.7 0.6 constant_dynamic-update-slice_fusion.4
  105.4 3.3 %collective-permute-done.18 = bf16[32,1664]{1,0:T(8,128)(2,1)S(1)} collective-permute-done((bf16[32,1664]{1,0:T(8,128)(2,1)S(1)}, bf16[32,1664]{1,0:T(8,128)(2,1)S(1)}, u32[]{:S(2)}, u32[]{:S(2)}) %collective-permute-start.18) | collective-permute-done | bytes 106528 | tf_op jit(solution)/shard_map/ppermute | solution.py:11
  110.0 0.7 constant_dynamic-update-slice_fusion.1
  110.7 5.0 %collective-permute-done.21 = bf16[32,1664]{1,0:T(8,128)(2,1)S(1)} collective-permute-done((bf16[32,1664]{1,0:T(8,128)(2,1)S(1)}, bf16[32,1664]{1,0:T(8,128)(2,1)S(1)}, u32[]{:S(2)}, u32[]{:S(2)}) %collective-permute-start.21) | collective-permute-done | bytes 106528 | tf_op jit(solution)/shard_map/ppermute | solution.py:11
  115.7 0.7 constant_dynamic-update-slice_fusion
  116.3 2.1 %rev.14 = bf16[8,32,1664]{2,1,0:T(8,128)(2,1)} reverse(bf16[8,32,1664]{2,1,0:T(8,128)(2,1)} %bitcast.40), dimensions={0} | reverse | bytes 1703936 | tf_op jit(solution)/shard_map/jit(_flip)/rev | solution.py:24
  118.5 2.4 %fusion.10 = bf16[8,32,1664]{2,1,0:T(8,128)(2,1)} fusion(s32[]{:T(128)S(6)} %select_n.126, bf16[8,32,1664]{2,1,0:T(8,128)(2,1)} %rev.14), kind=kLoop, calls=%fused_computation.17 | loop fusion | flops 425984 | bytes 1703940 | tf_op jit(solution)/shard_map/jit(_roll_dynamic)/concatenate | solution.py:25
  120.9 3.0 %collective-permute-start.22 = (bf16[256,1664]{1,0:T(8,128)(2,1)}, bf16[256,1664]{1,0:T(8,128)(2,1)}, u32[]{:S(2)}, u32[]{:S(2)}) collective-permute-start(bf16[256,1664]{1,0:T(8,128)(2,1)} %bitcast.15), channel_id=1, source_target_pairs={{0,16},{16,0},{1,17},{17,1},{2,18},{18,2},{3,19},{19,3},{4,20},{20... | collective-permute-start | bytes 2555912 | tf_op jit(solution)/shard_map/ppermute | solution.py:11
  123.9 2.3 %collective-permute-done.22 = bf16[256,1664]{1,0:T(8,128)(2,1)} collective-permute-done((bf16[256,1664]{1,0:T(8,128)(2,1)}, bf16[256,1664]{1,0:T(8,128)(2,1)}, u32[]{:S(2)}, u32[]{:S(2)}) %collective-permute-start.22) | collective-permute-done | bytes 852000 | tf_op jit(solution)/shard_map/ppermute | solution.py:11
  126.2 1.6 %broadcast_select_fusion.1 = (bf16[256,1664]{1,0:T(8,128)(2,1)S(1)}, bf16[256,1664]{1,0:T(8,128)(2,1)S(1)}) fusion(bf16[256,1664]{1,0:T(8,128)(2,1)} %collective-permute-done.22, pred[]{:T(512)S(6)} %eq.19, bf16[8,32,1664]{2,1,0:T(8,128)(2,1)} %fusion.10), kind=kLoop, calls=%fused_computation.19 | loop fusion | flops 851968 | bytes 3407873 | tf_op jit(solution)/shard_map/jit(_where)/select_n | solution.py:68
  127.8 2.1 %fusion.5 = bf16[512,1024]{1,0:T(8,128)(2,1)S(1)} fusion(bf16[1664,1024]{1,0:T(8,128)(2,1)S(1)} %copy-done.6, bf16[256,1664]{1,0:T(8,128)(2,1)S(1)} %get-tuple-element.8, bf16[256,1664]{1,0:T(8,128)(2,1)S(1)} %get-tuple-element.7), kind=kOutput, calls=%fused_computation.13 | convolution fusion | flops 1748762624 | bytes 6160384 | tf_op jit(solution)/shard_map/dot_general | solution.py:70
  129.9 21.5 %all_to_all.5 = bf16[16,32,1024]{2,1,0:T(8,128)(2,1)} all-to-all(bf16[16,32,1024]{2,1,0:T(8,128)(2,1)S(1)} %bitcast.45), channel_id=1, replica_groups=mesh['z'=8,'core'=2,'x'=4,'y'=4] {'x','y'}, dimensions={0} | all-to-all | bytes 2097152 | tf_op jit(solution)/shard_map/all_to_all | solution.py:72
  151.3 2.1 %reduce_sum.12 = bf16[32,1024]{1,0:T(8,128)(2,1)} reduce(bf16[16,32,1024]{2,1,0:T(8,128)(2,1)} %all_to_all.5, bf16[]{:T(256)} %constant.142.clone.1), dimensions={0}, to_apply=%region_0.1 | reduce | flops 491520 | bytes 1114114 | tf_op jit(solution)/shard_map/reduce_sum | solution.py:73
  (33 shorter events, 2.1 us)
Async XLA Ops:
  0.0 35.6 %copy-start = (bf16[1024,1664]{1,0:T(8,128)(2,1)S(1)}, bf16[1024,1664]{1,0:T(8,128)(2,1)}, u32[]{:S(2)}) copy-start(bf16[1024,1664]{1,0:T(8,128)(2,1)} %param.5) | copy-start | bytes 10223620
  0.0 5.6 %collective-permute-start = (bf16[32,1024]{1,0:T(8,128)(2,1)}, bf16[32,1024]{1,0:T(8,128)(2,1)S(1)}, u32[]{:S(2)}, u32[]{:S(2)}) collective-permute-start(bf16[32,1024]{1,0:T(8,128)(2,1)} %param.4), channel_id=1, source_target_pairs={{0,4},{4,8},{8,12},{12,0},{1,5},{5,9},{9,13},{13,1},{2,6},{6,10},{... | collective-permute-start | bytes 196616 | tf_op jit(solution)/shard_map/ppermute | solution.py:11
  2.0 5.3 %collective-permute-start.1 = (bf16[32,1024]{1,0:T(8,128)(2,1)}, bf16[32,1024]{1,0:T(8,128)(2,1)S(1)}, u32[]{:S(2)}, u32[]{:S(2)}) collective-permute-start(bf16[32,1024]{1,0:T(8,128)(2,1)} %param.4), channel_id=1, source_target_pairs={{0,8},{4,12},{8,0},{12,4},{1,9},{5,13},{9,1},{13,5},{2,10},{6,14},... | collective-permute-start | bytes 196616 | tf_op jit(solution)/shard_map/ppermute | solution.py:11
  4.5 3.6 %collective-permute-start.2 = (bf16[32,1024]{1,0:T(8,128)(2,1)}, bf16[32,1024]{1,0:T(8,128)(2,1)}, u32[]{:S(2)}, u32[]{:S(2)}) collective-permute-start(bf16[32,1024]{1,0:T(8,128)(2,1)} %param.4), channel_id=1, source_target_pairs={{0,12},{4,0},{8,4},{12,8},{1,13},{5,1},{9,5},{13,9},{2,14},{6,2},{... | collective-permute-start | bytes 196616 | tf_op jit(solution)/shard_map/ppermute | solution.py:11
  13.1 7.5 %collective-permute-start.3 = (bf16[128,1024]{1,0:T(8,128)(2,1)}, bf16[128,1024]{1,0:T(8,128)(2,1)}, u32[]{:S(2)}, u32[]{:S(2)}) collective-permute-start(bf16[128,1024]{1,0:T(8,128)(2,1)} %bitcast.1), channel_id=1, source_target_pairs={{0,1},{1,2},{2,3},{3,0},{4,5},{5,6},{6,7},{7,4},{8,9},{9,10},{10,1... | collective-permute-start | bytes 786440 | tf_op jit(solution)/shard_map/ppermute | solution.py:11
  14.7 12.9 %collective-permute-start.4 = (bf16[128,1024]{1,0:T(8,128)(2,1)}, bf16[128,1024]{1,0:T(8,128)(2,1)}, u32[]{:S(2)}, u32[]{:S(2)}) collective-permute-start(bf16[128,1024]{1,0:T(8,128)(2,1)} %bitcast.1), channel_id=1, source_target_pairs={{0,2},{1,3},{2,0},{3,1},{4,6},{5,7},{6,4},{7,5},{8,10},{9,11},{10,... | collective-permute-start | bytes 786440 | tf_op jit(solution)/shard_map/ppermute | solution.py:11
  17.3 10.3 %collective-permute-start.5 = (bf16[128,1024]{1,0:T(8,128)(2,1)}, bf16[128,1024]{1,0:T(8,128)(2,1)}, u32[]{:S(2)}, u32[]{:S(2)}) collective-permute-start(bf16[128,1024]{1,0:T(8,128)(2,1)} %bitcast.1), channel_id=1, source_target_pairs={{0,3},{1,0},{2,1},{3,2},{4,7},{5,4},{6,5},{7,6},{8,11},{9,8},{10,9... | collective-permute-start | bytes 786440 | tf_op jit(solution)/shard_map/ppermute | solution.py:11
  32.1 2.3 %copy-start.4 = (bf16[1024,1664]{1,0:T(8,128)(2,1)S(1)}, bf16[1024,1664]{1,0:T(8,128)(2,1)}, u32[]{:S(2)}) copy-start(bf16[1024,1664]{1,0:T(8,128)(2,1)} %param.6) | copy-start | bytes 10223620
  34.0 1.6 %copy-start.2 = (bf16[4,4,32,1024]{3,2,1,0:T(8,128)(2,1)}, bf16[4,4,32,1024]{3,2,1,0:T(8,128)(2,1)S(1)}, u32[]{:S(2)}) copy-start(bf16[4,4,32,1024]{3,2,1,0:T(8,128)(2,1)S(1)} %copy.5) | copy-start | bytes 3145732
  38.0 6.4 %collective-permute-start.6 = (bf16[256,3328]{1,0:T(8,128)(2,1)}, bf16[256,3328]{1,0:T(8,128)(2,1)}, u32[]{:S(2)}, u32[]{:S(2)}) collective-permute-start(bf16[256,3328]{1,0:T(8,128)(2,1)} %pad_maximum_fusion), channel_id=1, source_target_pairs={{0,16},{16,0},{1,17},{17,1},{2,18},{18,2},{3,19},{19,3},{4,20},{20... | collective-permute-start | bytes 5111816 | tf_op jit(solution)/shard_map/ppermute | solution.py:11
  40.9 2.3 %copy-start.3 = (bf16[4,4,32,1024]{3,2,1,0:T(8,128)(2,1)S(1)}, bf16[4,4,32,1024]{3,2,1,0:T(8,128)(2,1)}, u32[]{:S(2)}) copy-start(bf16[4,4,32,1024]{3,2,1,0:T(8,128)(2,1)} %copy-done.2) | copy-start | bytes 3145732
  40.9 2.4 %copy-start.5 = (bf16[1024,1664]{1,0:T(8,128)(2,1)S(1)}, bf16[1024,1664]{1,0:T(8,128)(2,1)}, u32[]{:S(2)}) copy-start(bf16[1024,1664]{1,0:T(8,128)(2,1)} %param.6) | copy-start | bytes 10223620
  46.3 1.2 copy-start.1
  49.0 8.8 %collective-permute-start.7 = (bf16[32,1664]{1,0:T(8,128)(2,1)}, bf16[32,1664]{1,0:T(8,128)(2,1)S(1)}, u32[]{:S(2)}, u32[]{:S(2)}) collective-permute-start(bf16[32,1664]{1,0:T(8,128)(2,1)} %get-tuple-element.16), channel_id=1, source_target_pairs={{0,32},{32,64},{64,96},{96,128},{128,160},{160,192},{192,224},{224... | collective-permute-start | bytes 319496 | tf_op jit(solution)/shard_map/ppermute | solution.py:11
  50.7 8.3 %collective-permute-start.11 = (bf16[32,1664]{1,0:T(8,128)(2,1)}, bf16[32,1664]{1,0:T(8,128)(2,1)S(1)}, u32[]{:S(2)}, u32[]{:S(2)}) collective-permute-start(bf16[32,1664]{1,0:T(8,128)(2,1)} %get-tuple-element.17), channel_id=1, source_target_pairs={{0,224},{32,0},{64,32},{96,64},{128,96},{160,128},{192,160},{224,1... | collective-permute-start | bytes 319496 | tf_op jit(solution)/shard_map/ppermute | solution.py:11
  58.9 7.2 %collective-permute-start.8 = (bf16[32,3328]{1,0:T(8,128)(2,1)S(1)}, bf16[32,3328]{1,0:T(8,128)(2,1)S(1)}, u32[]{:S(2)}, u32[]{:S(2)}) collective-permute-start(bf16[32,3328]{1,0:T(8,128)(2,1)S(1)} %pad_maximum_fusion.3), channel_id=1, source_target_pairs={{0,32},{32,64},{64,96},{96,128},{128,160},{160,192},{192,224},{224... | collective-permute-start | bytes 638984 | tf_op jit(solution)/shard_map/ppermute | solution.py:11
  60.6 7.1 %collective-permute-start.12 = (bf16[32,3328]{1,0:T(8,128)(2,1)}, bf16[32,3328]{1,0:T(8,128)(2,1)}, u32[]{:S(2)}, u32[]{:S(2)}) collective-permute-start(bf16[32,3328]{1,0:T(8,128)(2,1)} %pad_maximum_fusion.4), channel_id=1, source_target_pairs={{0,224},{32,0},{64,32},{96,64},{128,96},{160,128},{192,160},{224,1... | collective-permute-start | bytes 638984 | tf_op jit(solution)/shard_map/ppermute | solution.py:11
  67.7 6.2 %collective-permute-start.9 = (bf16[32,3328]{1,0:T(8,128)(2,1)}, bf16[32,3328]{1,0:T(8,128)(2,1)}, u32[]{:S(2)}, u32[]{:S(2)}) collective-permute-start(bf16[32,3328]{1,0:T(8,128)(2,1)} %bitcast_add_fusion.2), channel_id=1, source_target_pairs={{0,32},{32,64},{64,96},{96,128},{128,160},{160,192},{192,224},{224... | collective-permute-start | bytes 638984 | tf_op jit(solution)/shard_map/ppermute | solution.py:11
  76.0 5.0 %collective-permute-start.13 = (bf16[32,3328]{1,0:T(8,128)(2,1)}, bf16[32,3328]{1,0:T(8,128)(2,1)}, u32[]{:S(2)}, u32[]{:S(2)}) collective-permute-start(bf16[32,3328]{1,0:T(8,128)(2,1)} %get-tuple-element.10), channel_id=1, source_target_pairs={{0,224},{32,0},{64,32},{96,64},{128,96},{160,128},{192,160},{224,1... | collective-permute-start | bytes 638984 | tf_op jit(solution)/shard_map/ppermute | solution.py:11
  76.0 8.0 %collective-permute-start.10 = (bf16[32,3328]{1,0:T(8,128)(2,1)}, bf16[32,3328]{1,0:T(8,128)(2,1)}, u32[]{:S(2)}, u32[]{:S(2)}) collective-permute-start(bf16[32,3328]{1,0:T(8,128)(2,1)} %get-tuple-element.9), channel_id=1, source_target_pairs={{0,32},{32,64},{64,96},{96,128},{128,160},{160,192},{192,224},{224... | collective-permute-start | bytes 638984 | tf_op jit(solution)/shard_map/ppermute | solution.py:11
  82.7 5.0 %collective-permute-start.14 = (bf16[32,3328]{1,0:T(8,128)(2,1)}, bf16[32,3328]{1,0:T(8,128)(2,1)}, u32[]{:S(2)}, u32[]{:S(2)}) collective-permute-start(bf16[32,3328]{1,0:T(8,128)(2,1)} %bitcast_add_fusion.1), channel_id=1, source_target_pairs={{0,224},{32,0},{64,32},{96,64},{128,96},{160,128},{192,160},{224,1... | collective-permute-start | bytes 638984 | tf_op jit(solution)/shard_map/ppermute | solution.py:11
  89.7 10.2 %collective-permute-start.15 = (bf16[32,1664]{1,0:T(8,128)(2,1)S(1)}, bf16[32,1664]{1,0:T(8,128)(2,1)}, u32[]{:S(2)}, u32[]{:S(2)}) collective-permute-start(bf16[32,1664]{1,0:T(8,128)(2,1)S(1)} %get-tuple-element.6), channel_id=1, source_target_pairs={{0,32},{32,64},{64,96},{96,128},{128,160},{160,192},{192,224},{224... | collective-permute-start | bytes 319496 | tf_op jit(solution)/shard_map/ppermute | solution.py:11
  89.7 13.0 %collective-permute-start.16 = (bf16[32,1664]{1,0:T(8,128)(2,1)S(1)}, bf16[32,1664]{1,0:T(8,128)(2,1)S(1)}, u32[]{:S(2)}, u32[]{:S(2)}) collective-permute-start(bf16[32,1664]{1,0:T(8,128)(2,1)S(1)} %get-tuple-element.6), channel_id=1, source_target_pairs={{0,64},{32,96},{64,128},{96,160},{128,192},{160,224},{192,0},{224,... | collective-permute-start | bytes 319496 | tf_op jit(solution)/shard_map/ppermute | solution.py:11
  93.3 11.4 %collective-permute-start.17 = (bf16[32,1664]{1,0:T(8,128)(2,1)S(1)}, bf16[32,1664]{1,0:T(8,128)(2,1)S(1)}, u32[]{:S(2)}, u32[]{:S(2)}) collective-permute-start(bf16[32,1664]{1,0:T(8,128)(2,1)S(1)} %get-tuple-element.6), channel_id=1, source_target_pairs={{0,96},{32,128},{64,160},{96,192},{128,224},{160,0},{192,32},{224,... | collective-permute-start | bytes 319496 | tf_op jit(solution)/shard_map/ppermute | solution.py:11
  93.3 15.4 %collective-permute-start.18 = (bf16[32,1664]{1,0:T(8,128)(2,1)S(1)}, bf16[32,1664]{1,0:T(8,128)(2,1)S(1)}, u32[]{:S(2)}, u32[]{:S(2)}) collective-permute-start(bf16[32,1664]{1,0:T(8,128)(2,1)S(1)} %get-tuple-element.6), channel_id=1, source_target_pairs={{0,128},{32,160},{64,192},{96,224},{128,0},{160,32},{192,64},{224,... | collective-permute-start | bytes 319496 | tf_op jit(solution)/shard_map/ppermute | solution.py:11
  96.3 13.0 %collective-permute-start.19 = (bf16[32,1664]{1,0:T(8,128)(2,1)S(1)}, bf16[32,1664]{1,0:T(8,128)(2,1)S(1)}, u32[]{:S(2)}, u32[]{:S(2)}) collective-permute-start(bf16[32,1664]{1,0:T(8,128)(2,1)S(1)} %get-tuple-element.6), channel_id=1, source_target_pairs={{0,160},{32,192},{64,224},{96,0},{128,32},{160,64},{192,96},{224,1... | collective-permute-start | bytes 319496 | tf_op jit(solution)/shard_map/ppermute | solution.py:11
  99.8 10.2 %collective-permute-start.20 = (bf16[32,1664]{1,0:T(8,128)(2,1)S(1)}, bf16[32,1664]{1,0:T(8,128)(2,1)S(1)}, u32[]{:S(2)}, u32[]{:S(2)}) collective-permute-start(bf16[32,1664]{1,0:T(8,128)(2,1)S(1)} %get-tuple-element.6), channel_id=1, source_target_pairs={{0,192},{32,224},{64,0},{96,32},{128,64},{160,96},{192,128},{224,1... | collective-permute-start | bytes 319496 | tf_op jit(solution)/shard_map/ppermute | solution.py:11
  102.7 13.0 %collective-permute-start.21 = (bf16[32,1664]{1,0:T(8,128)(2,1)S(1)}, bf16[32,1664]{1,0:T(8,128)(2,1)S(1)}, u32[]{:S(2)}, u32[]{:S(2)}) collective-permute-start(bf16[32,1664]{1,0:T(8,128)(2,1)S(1)} %get-tuple-element.6), channel_id=1, source_target_pairs={{0,224},{32,0},{64,32},{96,64},{128,96},{160,128},{192,160},{224,1... | collective-permute-start | bytes 319496 | tf_op jit(solution)/shard_map/ppermute | solution.py:11
  120.9 5.3 %collective-permute-start.22 = (bf16[256,1664]{1,0:T(8,128)(2,1)}, bf16[256,1664]{1,0:T(8,128)(2,1)}, u32[]{:S(2)}, u32[]{:S(2)}) collective-permute-start(bf16[256,1664]{1,0:T(8,128)(2,1)} %bitcast.15), channel_id=1, source_target_pairs={{0,16},{16,0},{1,17},{17,1},{2,18},{18,2},{3,19},{19,3},{4,20},{20... | collective-permute-start | bytes 2555912 | tf_op jit(solution)/shard_map/ppermute | solution.py:11
  123.9 3.9 %copy-start.6 = (bf16[1664,1024]{1,0:T(8,128)(2,1)S(1)}, bf16[1664,1024]{1,0:T(8,128)(2,1)}, u32[]{:S(2)}) copy-start(bf16[1664,1024]{1,0:T(8,128)(2,1)} %param.7) | copy-start | bytes 10223620

commit v2 on v0

v2 whole, which is shorter than its diff:
```python
import jax
import jax.numpy as jnp
from jax import lax
from jax.experimental import pallas as pl
from jax.experimental.pallas import tpu as pltpu
from jax.sharding import Mesh, PartitionSpec as P

BF = jnp.bfloat16
F32 = jnp.float32
VMEM = pl.BlockSpec(memory_space=pltpu.VMEM)
ANY = pl.BlockSpec(memory_space=pl.ANY)
MIB = 2**20

OWNER = (0, 3, 4, 7, 1, 6, 2, 5)
POSITION = sum(t << (4 * z) for t, z in enumerate(OWNER))
STEPS = (1, -1, 3)


def partner(z, step):
    return (z + STEPS[step] * (1 - 2 * (z % 2)) + 8) % 8


def swap_z(v, step):
    pairs = []
    for z in range(8):
        pairs.append((2 * z, 2 * partner(z, step)))
        pairs.append((2 * z + 1, 2 * ((8 - partner((8 - z) % 8, step)) % 8) + 1))
    return lax.ppermute(v, ("z", "core"), pairs)


def swap_core(v):
    return lax.ppermute(v, "core", [(0, 1), (1, 0)])


def swap_grid(v, near, far):
    pairs = []
    for x in range(4):
        for y in range(4):
            pairs.append((4 * x + y, 4 * (x ^ near) + (y ^ far)))
            pairs.append((16 + 4 * x + y, 16 + 4 * (x ^ far) + (y ^ near)))
    return lax.ppermute(v, ("core", "x", "y"), pairs)


def own_z():
    z = lax.axis_index("z")
    return jnp.where(lax.axis_index("core") == 0, z, (8 - z) % 8)


def is_in(z, members):
    return ((sum(1 << m for m in members) >> z) & 1) == 1


def shape(*dims, dtype=BF):
    return jax.ShapeDtypeStruct(dims, dtype)


def call(body, outs, *ins, flops=0, specs=None, scratch=(), limit=16):
    size = sum(v.size * v.dtype.itemsize for v in (*ins, *outs))
    return pl.pallas_call(
        body,
        out_shape=outs,
        in_specs=specs or [VMEM] * len(ins),
        out_specs=[VMEM] * len(outs),
        scratch_shapes=list(scratch),
        cost_estimate=pl.CostEstimate(flops=flops, bytes_accessed=size, transcendentals=0),
        compiler_params=pltpu.CompilerParams(vmem_limit_bytes=limit * MIB),
    )(*ins)


def load(weight):
    def body(source, out, sem):
        copy = pltpu.make_async_copy(source, out, sem)
        copy.start()
        copy.wait()

    sems = [pltpu.SemaphoreType.DMA(())]
    return call(body, [shape(*weight.shape)], weight, specs=[ANY], scratch=sems, limit=48)[0]


def join(*parts):
    rows = [p.shape[0] for p in parts]

    def body(*refs):
        at = 0
        for ref, n in zip(refs, rows):
            refs[-1][at : at + n] = ref[...]
            at += n

    return call(body, [shape(sum(rows), *parts[0].shape[1:])], *parts)[0]


def tiles(width, tile):
    return [(at, min(tile, width - at)) for at in range(0, width, tile)]


def project(part, first, second, gate_weight, up_weight, after=()):
    _, rows, depth = first.shape
    width = gate_weight.shape[1]
    half = 4 * rows

    def body(first, second, gate, up, *refs):
        theirs, ours, left = refs[len(after) :]
        mine = 2 * (part ^ lax.axis_index("core"))
        for j, ref in enumerate((first, second)):
            for h in range(2):
                at = (2 * j + h) * rows
                left[at : at + rows] = ref[2 - mine + h]
                left[half + at : half + at + rows] = ref[mine + h]
        for at, n in tiles(width, 256):
            for i, weight in enumerate((gate, up)):
                out = jnp.dot(left[...], weight[:, at : at + n], preferred_element_type=F32).astype(BF)
                theirs[:, i, :, at : at + n] = out[:half].reshape(4, rows, n)
                ours[:, i, :, at : at + n] = out[half:].reshape(4, rows, n)

    return call(
        body, [shape(4, 2, rows, width)] * 2, first, second, gate_weight, up_weight, *after,
        specs=[VMEM] * 4 + [ANY] * len(after), flops=8 * half * depth * width, scratch=[pltpu.VMEM((2 * half, depth), BF)],
    )


def first_sums(ours, theirs):
    _, _, rows, width = ours[0].shape

    def body(o0, o1, t0, t1, send, keep):
        core = lax.axis_index("core")

        def total(t, i):
            p, j, k = t // 4, t // 2 % 2, t % 2
            o, r, s = ((o0, t0, t1), (o1, t1, t0))[p]
            got = jnp.where(core == 0, r[2 * k + j, i], s[2 * k + j, i])
            return o[t % 4, i].astype(F32) + got.astype(F32)

        def fill(kept, sent):
            for n in range(4):
                for i in range(2):
                    send[n, i] = total(sent + n, i).astype(BF)
                    keep[n, i] = total(kept + n, i)

        inside = is_in(own_z(), OWNER[:4])
        pl.when(inside)(lambda: fill(0, 4))
        pl.when(jnp.logical_not(inside))(lambda: fill(4, 0))

    outs = [shape(4, 2, rows, width), shape(4, 2, rows, width, dtype=F32)]
    return call(body, outs, *ours, *theirs)


def next_sums(got, kept, after=()):
    n, _, rows, width = got.shape
    m = n // 2
    firsts = OWNER[0:2] + OWNER[4:6] if m == 2 else OWNER[::2]

    def body(got, kept, *refs):
        send, keep = refs[len(after) :]
        at = jnp.where(is_in(own_z(), firsts), 0, m)
        for i in range(m):
            send[i] = (got[m - at + i].astype(F32) + kept[m - at + i]).astype(BF)
            keep[i] = got[at + i].astype(F32) + kept[at + i]

    outs = [shape(m, 2, rows, width), shape(m, 2, rows, width, dtype=F32)]
    return call(body, outs, got, kept, *after, specs=[VMEM] * 2 + [ANY] * len(after))


def activate(got, kept):
    _, _, rows, width = got.shape

    def body(got, kept, out):
        gate = got[0, 0].astype(F32) + kept[0, 0]
        up = got[0, 1].astype(F32) + kept[0, 1]
        out[0] = (gate / (1 + jnp.exp(-gate)) * up).astype(BF)

    return call(body, [shape(1, rows, width)], got, kept)[0]


def assemble(sent, got):
    _, rows, width = sent.shape

    def body(sent, got, out):
        me = own_z()
        for source, ref in ((me, sent), (partner(me, 0), got)):
            near = partner(source, 1)
            for i, owner in enumerate((source, partner(source, 2), near, partner(near, 2))):
                out[(POSITION >> (4 * owner)) & 7] = ref[i]

    return call(body, [shape(8, rows, width)], sent, got)[0]


def expand(own, other, weight):
    _, rows, depth = own.shape
    columns = weight.shape[1]

    def body(own, other, weight, *refs):
        outs, left = refs[:4], refs[4]
        core = lax.axis_index("core")
        for j in range(4):
            for q in range(4):
                at = (4 * j + q) * rows
                if q < 2:
                    left[at : at + rows] = own[2 * j + q]
                else:
                    left[at : at + rows] = other[4 * ((j >> 1) ^ 1 ^ core) + 2 * (q - 2) + (j & 1)]
        for at, n in tiles(columns, 256):
            out = jnp.dot(left[...], weight[:, at : at + n], preferred_element_type=F32).astype(BF)
            out = out.reshape(4, 4, rows, n)
            for j in range(4):
                outs[j][:, :, at : at + n] = out[j]

    return call(
        body, [shape(4, rows, columns)] * 4, own, other, weight,
        flops=32 * rows * depth * columns, scratch=[pltpu.VMEM((16 * rows, depth), BF)],
    )


def sum_far(*parts):
    _, rows, columns = parts[0].shape

    def body(a, b, c, d, keep, *sends):
        core = lax.axis_index("core")
        for k in range(4):
            low, high = k ^ (2 * core), k ^ 2 ^ (2 * core)
            total = (a[low].astype(F32) + b[low].astype(F32)) + (c[high].astype(F32) + d[high].astype(F32))
            if k == 0:
                keep[...] = total
            else:
                sends[k - 1][...] = total.astype(BF)

    outs = [shape(rows, columns, dtype=F32)] + [shape(rows, columns)] * 3
    return call(body, outs, *parts)


def sum_near(*parts):
    def body(a, b, c, d, out):
        total = (a[...] + b[...].astype(F32)) + (c[...].astype(F32) + d[...].astype(F32))
        out[...] = total.astype(BF)

    return call(body, [shape(*parts[0].shape)], *parts)[0]


def on_device(acts, gate_weight, up_weight, down_weight):
    own = acts[None]
    near = [swap_grid(own, k, 0) for k in (1, 2, 3)]
    gate_weight = load(gate_weight)
    piece = join(load(own), *near)
    far = [swap_grid(piece, 0, j) for j in (1, 2, 3)]
    up_weight = load(up_weight)
    theirs0, ours0 = project(0, piece, far[0], gate_weight, up_weight)
    theirs1, ours1 = project(1, far[1], far[2], gate_weight, up_weight, after=(theirs0,))
    send, keep = first_sums((ours0, ours1), (swap_core(theirs0), swap_core(theirs1)))
    down_weight = load(down_weight)
    send, keep = next_sums(swap_z(send, 0), keep, after=(down_weight,))
    send, keep = next_sums(swap_z(send, 1), keep)
    have = activate(swap_z(send, 2), keep)
    for step in (2, 1):
        have = join(have, swap_z(have, step))
    hidden = assemble(have, swap_z(have, 0))
    terms = expand(hidden, swap_core(hidden), down_weight)
    sums = sum_far(terms[0], *[swap_grid(terms[j], 0, j) for j in (1, 2, 3)])
    return sum_near(sums[0], *[swap_grid(sums[k], k, 0) for k in (1, 2, 3)])


def solution(mesh):
    grid = Mesh(mesh.devices.reshape(8, 2, 4, 4), ("z", "core", "x", "y"))
    row, col = ("z", "core"), ("x", "y")
    in_specs = (P(col, row), P(row, col), P(row, col), P(col, row))
    return jax.shard_map(
        on_device, mesh=grid, in_specs=in_specs, out_specs=P(col, row), check_vma=False
    )
```

time: 265 us -> 114 us (0.43)
  waiting for transfers between devices: 235 us -> 60.9 us
  starting transfers between devices: 0.12 us -> 36.7 us
  Pallas kernels: 0 us -> 13.8 us
  between operations: 13.2 us -> 0.16 us
  matrix products: 11.1 us -> 0 us
  other arithmetic: 5.04 us -> 0 us
    reduce_scatter x2 -> x0, waiting for transfers between devices: 140 us -> none  [the longest x1 74.8 us: on_device(): lax.psum_scatter(terms.astype(jnp.bfloat16), 'col', scatter_dimension=0,...]
    all_gather x2 -> x0, waiting for transfers between devices: 94.1 us -> none  [the longest x1 52.6 us: on_device(): piece = lax.all_gather(acts, 'col', axis=0, tiled=True)]
    ppermute x0 -> x21, waiting for transfers between devices: none -> 60.9 us  [the longest x6 44.4 us: swap_z(): return lax.ppermute(v, ('z', 'core'), pairs)]
    ppermute x0 -> x21, starting transfers between devices: none -> 36.7 us  [the longest x12 16.6 us: swap_grid(): return lax.ppermute(v, ('core', 'x', 'y'), pairs)]
    pallas_call x0 -> x17, Pallas kernels: none -> 13.8 us  [call(): pl.pallas_call(body, out_shape=outs, in_specs=specs or [VMEM] * len(ins),...]
    dot_general x3 -> x0, matrix products: 11.1 us -> none  [the longest x1 5.54 us: on_device(): jnp.dot(lax.all_gather(hidden, 'row', axis=0, tiled=True), down_weight, p...]
    concatenate x1 -> x0, other arithmetic: 3.29 us -> none  [on_device(): jnp.concatenate([jnp.dot(piece, gate_weight, preferred_element_type=jnp.f...]
  transfers between devices with their start and end apart: 4 -> 21, of which waited for: 4 -> 16; matrix products, arithmetic and copies ran while one was open for 0% -> 0% of each run, Pallas kernels for 0% -> 9%
where the time goes in v2:
time: 114 us; the launch traced here: 112 us
  waiting for transfers between devices  60.9 us (53%)
  starting transfers between devices  36.7 us (32%)
  Pallas kernels  13.8 us (12%)
    ppermute x6, waiting for transfers between devices, swap_z(): return lax.ppermute(v, ('z', 'core'), pairs)  44.4 us
    ppermute x12, starting transfers between devices, swap_grid(): return lax.ppermute(v, ('core', 'x', 'y'), pairs)  16.6 us
    pallas_call x17, Pallas kernels, call(): pl.pallas_call(body, out_shape=outs, in_specs=specs or [VMEM] * len(ins),...  13.8 us
    ppermute x12, waiting for transfers between devices, swap_grid(): return lax.ppermute(v, ('core', 'x', 'y'), pairs)  12.5 us
    ppermute x6, starting transfers between devices, swap_z(): return lax.ppermute(v, ('z', 'core'), pairs)  11 us
    ppermute x3, starting transfers between devices, swap_core(): return lax.ppermute(v, 'core', [(0, 1), (1, 0)])  9.15 us
    ppermute x3, waiting for transfers between devices, swap_core(): return lax.ppermute(v, 'core', [(0, 1), (1, 0)])  4.01 us
  transfers between devices with their start and end apart: 21, of which 16 were waited for; matrix products, arithmetic and copies ran while one was open for 0% of the time, Pallas kernels for 9%

profile of v2, /device:TPU:1, one launch (start us, length us, event | category | flops | bytes accessed | tf_op | source)
XLA Modules:
  0.0 112.4 jit_solution(5643023300891940526)
XLA Ops:
  0.0 2.1 %collective-permute-start = (bf16[1,32,1024]{2,1,0:T(8,128)(2,1)}, bf16[1,32,1024]{2,1,0:T(8,128)(2,1)S(1)}, u32[]{:S(2)}, u32[]{:S(2)}) collective-permute-start(bf16[1,32,1024]{2,1,0:T(8,128)(2,1)} %bitcast.1), channel_id=1, source_target_pairs={{0,4},{16,17},{1,5},{17,16},{2,6},{18,19},{3,7},{19,18},{4,0},{20,... | collective-permute-start | bytes 196616 | tf_op jit(solution)/shard_map/ppermute | solution.py:41
  2.1 2.6 %collective-permute-start.1 = (bf16[1,32,1024]{2,1,0:T(8,128)(2,1)}, bf16[1,32,1024]{2,1,0:T(8,128)(2,1)S(1)}, u32[]{:S(2)}, u32[]{:S(2)}) collective-permute-start(bf16[1,32,1024]{2,1,0:T(8,128)(2,1)} %bitcast.2), channel_id=1, source_target_pairs={{0,8},{16,18},{1,9},{17,19},{2,10},{18,16},{3,11},{19,17},{4,12},{... | collective-permute-start | bytes 196616 | tf_op jit(solution)/shard_map/ppermute | solution.py:41
  4.7 0.0 collective-permute-start.2
  4.8 0.0 copy-start
  4.8 0.9 copy-done
  5.7 0.1 shard_map.46.refs_0_
  5.7 0.0 collective-permute-done.refs_1_
  5.7 1.6 %collective-permute-done.1.refs_2_ = bf16[1,32,1024]{2,1,0:T(8,128)(2,1)S(1)} collective-permute-done((bf16[1,32,1024]{2,1,0:T(8,128)(2,1)}, bf16[1,32,1024]{2,1,0:T(8,128)(2,1)S(1)}, u32[]{:S(2)}, u32[]{:S(2)}) %collective-permute-start.1) | collective-permute-done | bytes 65568 | tf_op jit(solution)/shard_map/ppermute | solution.py:41
  7.3 2.0 %collective-permute-done.2.refs_3_ = bf16[1,32,1024]{2,1,0:T(8,128)(2,1)S(1)} collective-permute-done((bf16[1,32,1024]{2,1,0:T(8,128)(2,1)}, bf16[1,32,1024]{2,1,0:T(8,128)(2,1)S(1)}, u32[]{:S(2)}, u32[]{:S(2)}) %collective-permute-start.2) | collective-permute-done | bytes 65568 | tf_op jit(solution)/shard_map/ppermute | solution.py:41
  9.3 1.4 %collective-permute-start.3 = (bf16[4,32,1024]{2,1,0:T(8,128)(2,1)S(1)}, bf16[4,32,1024]{2,1,0:T(8,128)(2,1)S(1)}, u32[]{:S(2)}, u32[]{:S(2)}) collective-permute-start(bf16[4,32,1024]{2,1,0:T(8,128)(2,1)S(1)} %shard_map.47.first), channel_id=1, source_target_pairs={{0,1},{16,20},{1,0},{17,21},{2,3},{18,22},{3,2},{19,23},{4,5},{20,... | collective-permute-start | bytes 786440 | tf_op jit(solution)/shard_map/ppermute | solution.py:41
  10.7 2.4 %collective-permute-start.4 = (bf16[4,32,1024]{2,1,0:T(8,128)(2,1)S(1)}, bf16[4,32,1024]{2,1,0:T(8,128)(2,1)S(1)}, u32[]{:S(2)}, u32[]{:S(2)}) collective-permute-start(bf16[4,32,1024]{2,1,0:T(8,128)(2,1)S(1)} %shard_map.47.first), channel_id=1, source_target_pairs={{0,2},{16,24},{1,3},{17,25},{2,0},{18,26},{3,1},{19,27},{4,6},{20,... | collective-permute-start | bytes 786440 | tf_op jit(solution)/shard_map/ppermute | solution.py:41
  13.1 0.2 collective-permute-start.5
  13.3 2.0 %shard_map.48.gate = bf16[1024,1664]{1,0:T(8,128)(2,1)S(1)} custom-call(bf16[1024,1664]{1,0:T(8,128)(2,1)} %source.3), custom_call_target="tpu_custom_call" | custom-call | bytes 6815744 | tf_op jit(solution)/shard_map/pallas_call | solution.py:59
  15.2 2.0 %shard_map.49.up = bf16[1024,1664]{1,0:T(8,128)(2,1)S(1)} custom-call(bf16[1024,1664]{1,0:T(8,128)(2,1)} %source.4), custom_call_target="tpu_custom_call" | custom-call | bytes 6815744 | tf_op jit(solution)/shard_map/pallas_call | solution.py:59
  17.2 0.0 collective-permute-done.3.second
  17.2 2.1 %shard_map.50 = (bf16[4,2,32,1664]{3,2,1,0:T(8,128)(2,1)S(1)}, bf16[4,2,32,1664]{3,2,1,0:T(8,128)(2,1)S(1)}) custom-call(bf16[4,32,1024]{2,1,0:T(8,128)(2,1)S(1)} %shard_map.47.first, bf16[4,32,1024]{2,1,0:T(8,128)(2,1)S(1)} %collective-permute-done.3.second, bf16[1024,1664]{1,0:T(8,128)(2,1)S(1)} %shard_map.48.gate, bf16[1024,1664]{1,0:T(8,128)(2,1)S(1)} %shard_map.49.up), custom_call_target="tpu_custom_call" | custom-call | flops 1744830464 | bytes 9043968 | tf_op jit(solution)/shard_map/pallas_call | solution.py:59
  19.3 3.1 %collective-permute-start.6 = (bf16[4,2,32,1664]{3,2,1,0:T(8,128)(2,1)S(1)}, bf16[4,2,32,1664]{3,2,1,0:T(8,128)(2,1)S(1)}, u32[]{:S(2)}, u32[]{:S(2)}) collective-permute-start(bf16[4,2,32,1664]{3,2,1,0:T(8,128)(2,1)S(1)} %get-tuple-element.24.refs_0_), channel_id=1, source_target_pairs={{0,16},{16,0},{1,17},{17,1},{2,18},{18,2},{3,19},{19,3},{4,20},{20... | collective-permute-start | bytes 2555912 | tf_op jit(solution)/shard_map/ppermute | solution.py:32
  22.4 0.0 collective-permute-done.4.first
  22.4 0.2 collective-permute-done.5.second
  22.6 2.1 %shard_map.51 = (bf16[4,2,32,1664]{3,2,1,0:T(8,128)(2,1)S(1)}, bf16[4,2,32,1664]{3,2,1,0:T(8,128)(2,1)S(1)}) custom-call(bf16[4,32,1024]{2,1,0:T(8,128)(2,1)S(1)} %collective-permute-done.4.first, bf16[4,32,1024]{2,1,0:T(8,128)(2,1)S(1)} %collective-permute-done.5.second, bf16[1024,1664]{1,0:T(8,128)(2,1)S(1)} %shard_map.48.gate, ...), custom_call_target="tpu_custom_call" | custom-call | flops 1744830464 | bytes 9895936 | tf_op jit(solution)/shard_map/pallas_call | solution.py:59
  24.7 3.5 %collective-permute-start.7 = (bf16[4,2,32,1664]{3,2,1,0:T(8,128)(2,1)S(1)}, bf16[4,2,32,1664]{3,2,1,0:T(8,128)(2,1)S(1)}, u32[]{:S(2)}, u32[]{:S(2)}) collective-permute-start(bf16[4,2,32,1664]{3,2,1,0:T(8,128)(2,1)S(1)} %get-tuple-element.26), channel_id=1, source_target_pairs={{0,16},{16,0},{1,17},{17,1},{2,18},{18,2},{3,19},{19,3},{4,20},{20... | collective-permute-start | bytes 2555912 | tf_op jit(solution)/shard_map/ppermute | solution.py:32
  28.1 0.0 collective-permute-done.6.t0
  28.1 2.0 %collective-permute-done.7.t1 = bf16[4,2,32,1664]{3,2,1,0:T(8,128)(2,1)S(1)} collective-permute-done((bf16[4,2,32,1664]{3,2,1,0:T(8,128)(2,1)S(1)}, bf16[4,2,32,1664]{3,2,1,0:T(8,128)(2,1)S(1)}, u32[]{:S(2)}, u32[]{:S(2)}) %collective-permute-start.7) | collective-permute-done | bytes 852000 | tf_op jit(solution)/shard_map/ppermute | solution.py:32
  30.1 0.4 shard_map.52
  30.6 5.7 %collective-permute-start.8 = (bf16[4,2,32,1664]{3,2,1,0:T(8,128)(2,1)S(1)}, bf16[4,2,32,1664]{3,2,1,0:T(8,128)(2,1)S(1)}, u32[]{:S(2)}, u32[]{:S(2)}) collective-permute-start(bf16[4,2,32,1664]{3,2,1,0:T(8,128)(2,1)S(1)} %get-tuple-element.27), channel_id=1, source_target_pairs={{0,32},{16,240},{32,0},{48,80},{64,96},{80,48},{96,64},{112,144},{... | collective-permute-start | bytes 2555912 | tf_op jit(solution)/shard_map/ppermute | solution.py:28
  36.2 2.0 %shard_map.53.refs_0_.weight = bf16[1664,1024]{1,0:T(8,128)(2,1)S(1)} custom-call(bf16[1664,1024]{1,0:T(8,128)(2,1)} %source.5), custom_call_target="tpu_custom_call" | custom-call | bytes 6815744 | tf_op jit(solution)/shard_map/pallas_call | solution.py:59
  38.2 8.1 %collective-permute-done.8.got = bf16[4,2,32,1664]{3,2,1,0:T(8,128)(2,1)S(1)} collective-permute-done((bf16[4,2,32,1664]{3,2,1,0:T(8,128)(2,1)S(1)}, bf16[4,2,32,1664]{3,2,1,0:T(8,128)(2,1)S(1)}, u32[]{:S(2)}, u32[]{:S(2)}) %collective-permute-start.8) | collective-permute-done | bytes 852000 | tf_op jit(solution)/shard_map/ppermute | solution.py:28
  46.3 0.1 shard_map.54
  46.4 0.1 collective-permute-start.9
  46.5 7.3 %collective-permute-done.9.got = bf16[2,2,32,1664]{3,2,1,0:T(8,128)(2,1)S(1)} collective-permute-done((bf16[2,2,32,1664]{3,2,1,0:T(8,128)(2,1)S(1)}, bf16[2,2,32,1664]{3,2,1,0:T(8,128)(2,1)S(1)}, u32[]{:S(2)}, u32[]{:S(2)}) %collective-permute-start.9) | collective-permute-done | bytes 426016 | tf_op jit(solution)/shard_map/ppermute | solution.py:28
  53.8 0.1 shard_map.55
  53.9 2.9 %collective-permute-start.10 = (bf16[1,2,32,1664]{3,2,1,0:T(8,128)(2,1)S(1)}, bf16[1,2,32,1664]{3,2,1,0:T(8,128)(2,1)S(1)}, u32[]{:S(2)}, u32[]{:S(2)}) collective-permute-start(bf16[1,2,32,1664]{3,2,1,0:T(8,128)(2,1)S(1)} %get-tuple-element.31), channel_id=1, source_target_pairs={{0,96},{16,176},{32,192},{48,144},{64,160},{80,240},{96,0},{112,20... | collective-permute-start | bytes 638984 | tf_op jit(solution)/shard_map/ppermute | solution.py:28
  56.8 9.5 %collective-permute-done.10.got = bf16[1,2,32,1664]{3,2,1,0:T(8,128)(2,1)S(1)} collective-permute-done((bf16[1,2,32,1664]{3,2,1,0:T(8,128)(2,1)S(1)}, bf16[1,2,32,1664]{3,2,1,0:T(8,128)(2,1)S(1)}, u32[]{:S(2)}, u32[]{:S(2)}) %collective-permute-start.10) | collective-permute-done | bytes 213024 | tf_op jit(solution)/shard_map/ppermute | solution.py:28
  66.3 0.1 shard_map.56.refs_0_
  66.4 0.1 collective-permute-start.11
  66.5 8.1 %collective-permute-done.11.refs_1_ = bf16[1,32,1664]{2,1,0:T(8,128)(2,1)S(1)} collective-permute-done((bf16[1,32,1664]{2,1,0:T(8,128)(2,1)S(1)}, bf16[1,32,1664]{2,1,0:T(8,128)(2,1)S(1)}, u32[]{:S(2)}, u32[]{:S(2)}) %collective-permute-start.11) | collective-permute-done | bytes 106528 | tf_op jit(solution)/shard_map/ppermute | solution.py:28
  74.7 0.1 collective-permute-start.12
  74.8 5.0 %collective-permute-done.12.refs_1_ = bf16[2,32,1664]{2,1,0:T(8,128)(2,1)S(1)} collective-permute-done((bf16[2,32,1664]{2,1,0:T(8,128)(2,1)S(1)}, bf16[2,32,1664]{2,1,0:T(8,128)(2,1)S(1)}, u32[]{:S(2)}, u32[]{:S(2)}) %collective-permute-start.12) | collective-permute-done | bytes 213024 | tf_op jit(solution)/shard_map/ppermute | solution.py:28
  79.8 2.1 %collective-permute-start.13 = (bf16[4,32,1664]{2,1,0:T(8,128)(2,1)S(1)}, bf16[4,32,1664]{2,1,0:T(8,128)(2,1)S(1)}, u32[]{:S(2)}, u32[]{:S(2)}) collective-permute-start(bf16[4,32,1664]{2,1,0:T(8,128)(2,1)S(1)} %shard_map.58.sent), channel_id=1, source_target_pairs={{0,32},{16,240},{32,0},{48,80},{64,96},{80,48},{96,64},{112,144},{... | collective-permute-start | bytes 1277960 | tf_op jit(solution)/shard_map/ppermute | solution.py:28
  81.9 6.3 %collective-permute-done.13.got = bf16[4,32,1664]{2,1,0:T(8,128)(2,1)S(1)} collective-permute-done((bf16[4,32,1664]{2,1,0:T(8,128)(2,1)S(1)}, bf16[4,32,1664]{2,1,0:T(8,128)(2,1)S(1)}, u32[]{:S(2)}, u32[]{:S(2)}) %collective-permute-start.13) | collective-permute-done | bytes 426016 | tf_op jit(solution)/shard_map/ppermute | solution.py:28
  88.3 0.1 shard_map.59.own
  88.3 2.6 %collective-permute-start.14 = (bf16[8,32,1664]{2,1,0:T(8,128)(2,1)S(1)}, bf16[8,32,1664]{2,1,0:T(8,128)(2,1)S(1)}, u32[]{:S(2)}, u32[]{:S(2)}) collective-permute-start(bf16[8,32,1664]{2,1,0:T(8,128)(2,1)S(1)} %shard_map.59.own), channel_id=1, source_target_pairs={{0,16},{16,0},{1,17},{17,1},{2,18},{18,2},{3,19},{19,3},{4,20},{20... | collective-permute-start | bytes 2555912 | tf_op jit(solution)/shard_map/ppermute | solution.py:32
  91.0 2.0 %collective-permute-done.14.other = bf16[8,32,1664]{2,1,0:T(8,128)(2,1)S(1)} collective-permute-done((bf16[8,32,1664]{2,1,0:T(8,128)(2,1)S(1)}, bf16[8,32,1664]{2,1,0:T(8,128)(2,1)S(1)}, u32[]{:S(2)}, u32[]{:S(2)}) %collective-permute-start.14) | collective-permute-done | bytes 852000 | tf_op jit(solution)/shard_map/ppermute | solution.py:32
  93.0 2.1 %shard_map.60 = (bf16[4,32,1024]{2,1,0:T(8,128)(2,1)S(1)}, bf16[4,32,1024]{2,1,0:T(8,128)(2,1)S(1)}, bf16[4,32,1024]{2,1,0:T(8,128)(2,1)S(1)}, bf16[4,32,1024]{2,1,0:T(8,128)(2,1)S(1)}) custom-call(bf16[8,32,1664]{2,1,0:T(8,128)(2,1)S(1)} %shard_map.59.own, bf16[8,32,1664]{2,1,0:T(8,128)(2,1)S(1)} %collective-permute-done.14.other, ...), custom_call_target="tpu_custom_call" | custom-call | flops 1744830464 | bytes 6160384 | tf_op jit(solution)/shard_map/pallas_call | solution.py:59
  95.0 0.1 collective-permute-start.15
  95.1 1.4 %collective-permute-start.16 = (bf16[4,32,1024]{2,1,0:T(8,128)(2,1)S(1)}, bf16[4,32,1024]{2,1,0:T(8,128)(2,1)S(1)}, u32[]{:S(2)}, u32[]{:S(2)}) collective-permute-start(bf16[4,32,1024]{2,1,0:T(8,128)(2,1)S(1)} %get-tuple-element.35), channel_id=1, source_target_pairs={{0,2},{16,24},{1,3},{17,25},{2,0},{18,26},{3,1},{19,27},{4,6},{20,... | collective-permute-start | bytes 786440 | tf_op jit(solution)/shard_map/ppermute | solution.py:41
  96.5 2.5 %collective-permute-start.17 = (bf16[4,32,1024]{2,1,0:T(8,128)(2,1)S(1)}, bf16[4,32,1024]{2,1,0:T(8,128)(2,1)S(1)}, u32[]{:S(2)}, u32[]{:S(2)}) collective-permute-start(bf16[4,32,1024]{2,1,0:T(8,128)(2,1)S(1)} %get-tuple-element.36), channel_id=1, source_target_pairs={{0,3},{16,28},{1,2},{17,29},{2,1},{18,30},{3,0},{19,31},{4,7},{20,... | collective-permute-start | bytes 786440 | tf_op jit(solution)/shard_map/ppermute | solution.py:41
  99.0 1.7 %collective-permute-done.15.b = bf16[4,32,1024]{2,1,0:T(8,128)(2,1)S(1)} collective-permute-done((bf16[4,32,1024]{2,1,0:T(8,128)(2,1)S(1)}, bf16[4,32,1024]{2,1,0:T(8,128)(2,1)S(1)}, u32[]{:S(2)}, u32[]{:S(2)}) %collective-permute-start.15) | collective-permute-done | bytes 262176 | tf_op jit(solution)/shard_map/ppermute | solution.py:41
  100.7 2.8 %collective-permute-done.16.c = bf16[4,32,1024]{2,1,0:T(8,128)(2,1)S(1)} collective-permute-done((bf16[4,32,1024]{2,1,0:T(8,128)(2,1)S(1)}, bf16[4,32,1024]{2,1,0:T(8,128)(2,1)S(1)}, u32[]{:S(2)}, u32[]{:S(2)}) %collective-permute-start.16) | collective-permute-done | bytes 262176 | tf_op jit(solution)/shard_map/ppermute | solution.py:41
  103.4 2.6 %collective-permute-done.17.d = bf16[4,32,1024]{2,1,0:T(8,128)(2,1)S(1)} collective-permute-done((bf16[4,32,1024]{2,1,0:T(8,128)(2,1)S(1)}, bf16[4,32,1024]{2,1,0:T(8,128)(2,1)S(1)}, u32[]{:S(2)}, u32[]{:S(2)}) %collective-permute-start.17) | collective-permute-done | bytes 262176 | tf_op jit(solution)/shard_map/ppermute | solution.py:41
  106.1 0.1 shard_map.61
  106.2 0.1 collective-permute-start.18
  106.3 1.1 collective-permute-start.19
  107.4 2.7 %collective-permute-start.20 = (bf16[32,1024]{1,0:T(8,128)(2,1)S(1)}, bf16[32,1024]{1,0:T(8,128)(2,1)S(1)}, u32[]{:S(2)}, u32[]{:S(2)}) collective-permute-start(bf16[32,1024]{1,0:T(8,128)(2,1)S(1)} %get-tuple-element.40), channel_id=1, source_target_pairs={{0,12},{16,19},{1,13},{17,18},{2,14},{18,17},{3,15},{19,16},{4,8},... | collective-permute-start | bytes 196616 | tf_op jit(solution)/shard_map/ppermute | solution.py:41
  110.1 0.0 collective-permute-done.18.b
  110.1 0.9 collective-permute-done.19.c
  111.0 0.8 collective-permute-done.20.d
  111.8 0.7 shard_map.62
  (3 shorter events, 0.1 us)
Async XLA Ops:
  0.0 5.7 %collective-permute-start = (bf16[1,32,1024]{2,1,0:T(8,128)(2,1)}, bf16[1,32,1024]{2,1,0:T(8,128)(2,1)S(1)}, u32[]{:S(2)}, u32[]{:S(2)}) collective-permute-start(bf16[1,32,1024]{2,1,0:T(8,128)(2,1)} %bitcast.1), channel_id=1, source_target_pairs={{0,4},{16,17},{1,5},{17,16},{2,6},{18,19},{3,7},{19,18},{4,0},{20,... | collective-permute-start | bytes 196616 | tf_op jit(solution)/shard_map/ppermute | solution.py:41
  2.1 5.2 %collective-permute-start.1 = (bf16[1,32,1024]{2,1,0:T(8,128)(2,1)}, bf16[1,32,1024]{2,1,0:T(8,128)(2,1)S(1)}, u32[]{:S(2)}, u32[]{:S(2)}) collective-permute-start(bf16[1,32,1024]{2,1,0:T(8,128)(2,1)} %bitcast.2), channel_id=1, source_target_pairs={{0,8},{16,18},{1,9},{17,19},{2,10},{18,16},{3,11},{19,17},{4,12},{... | collective-permute-start | bytes 196616 | tf_op jit(solution)/shard_map/ppermute | solution.py:41
  4.7 4.5 %collective-permute-start.2 = (bf16[1,32,1024]{2,1,0:T(8,128)(2,1)}, bf16[1,32,1024]{2,1,0:T(8,128)(2,1)S(1)}, u32[]{:S(2)}, u32[]{:S(2)}) collective-permute-start(bf16[1,32,1024]{2,1,0:T(8,128)(2,1)} %bitcast.3), channel_id=1, source_target_pairs={{0,12},{16,19},{1,13},{17,18},{2,14},{18,17},{3,15},{19,16},{4,8},... | collective-permute-start | bytes 196616 | tf_op jit(solution)/shard_map/ppermute | solution.py:41
  4.8 0.9 copy-start
  9.3 7.9 %collective-permute-start.3 = (bf16[4,32,1024]{2,1,0:T(8,128)(2,1)S(1)}, bf16[4,32,1024]{2,1,0:T(8,128)(2,1)S(1)}, u32[]{:S(2)}, u32[]{:S(2)}) collective-permute-start(bf16[4,32,1024]{2,1,0:T(8,128)(2,1)S(1)} %shard_map.47.first), channel_id=1, source_target_pairs={{0,1},{16,20},{1,0},{17,21},{2,3},{18,22},{3,2},{19,23},{4,5},{20,... | collective-permute-start | bytes 786440 | tf_op jit(solution)/shard_map/ppermute | solution.py:41
  10.7 11.7 %collective-permute-start.4 = (bf16[4,32,1024]{2,1,0:T(8,128)(2,1)S(1)}, bf16[4,32,1024]{2,1,0:T(8,128)(2,1)S(1)}, u32[]{:S(2)}, u32[]{:S(2)}) collective-permute-start(bf16[4,32,1024]{2,1,0:T(8,128)(2,1)S(1)} %shard_map.47.first), channel_id=1, source_target_pairs={{0,2},{16,24},{1,3},{17,25},{2,0},{18,26},{3,1},{19,27},{4,6},{20,... | collective-permute-start | bytes 786440 | tf_op jit(solution)/shard_map/ppermute | solution.py:41
  13.1 9.5 %collective-permute-start.5 = (bf16[4,32,1024]{2,1,0:T(8,128)(2,1)S(1)}, bf16[4,32,1024]{2,1,0:T(8,128)(2,1)S(1)}, u32[]{:S(2)}, u32[]{:S(2)}) collective-permute-start(bf16[4,32,1024]{2,1,0:T(8,128)(2,1)S(1)} %shard_map.47.first), channel_id=1, source_target_pairs={{0,3},{16,28},{1,2},{17,29},{2,1},{18,30},{3,0},{19,31},{4,7},{20,... | collective-permute-start | bytes 786440 | tf_op jit(solution)/shard_map/ppermute | solution.py:41
  19.3 8.8 %collective-permute-start.6 = (bf16[4,2,32,1664]{3,2,1,0:T(8,128)(2,1)S(1)}, bf16[4,2,32,1664]{3,2,1,0:T(8,128)(2,1)S(1)}, u32[]{:S(2)}, u32[]{:S(2)}) collective-permute-start(bf16[4,2,32,1664]{3,2,1,0:T(8,128)(2,1)S(1)} %get-tuple-element.24.refs_0_), channel_id=1, source_target_pairs={{0,16},{16,0},{1,17},{17,1},{2,18},{18,2},{3,19},{19,3},{4,20},{20... | collective-permute-start | bytes 2555912 | tf_op jit(solution)/shard_map/ppermute | solution.py:32
  24.7 5.5 %collective-permute-start.7 = (bf16[4,2,32,1664]{3,2,1,0:T(8,128)(2,1)S(1)}, bf16[4,2,32,1664]{3,2,1,0:T(8,128)(2,1)S(1)}, u32[]{:S(2)}, u32[]{:S(2)}) collective-permute-start(bf16[4,2,32,1664]{3,2,1,0:T(8,128)(2,1)S(1)} %get-tuple-element.26), channel_id=1, source_target_pairs={{0,16},{16,0},{1,17},{17,1},{2,18},{18,2},{3,19},{19,3},{4,20},{20... | collective-permute-start | bytes 2555912 | tf_op jit(solution)/shard_map/ppermute | solution.py:32
  30.6 15.7 %collective-permute-start.8 = (bf16[4,2,32,1664]{3,2,1,0:T(8,128)(2,1)S(1)}, bf16[4,2,32,1664]{3,2,1,0:T(8,128)(2,1)S(1)}, u32[]{:S(2)}, u32[]{:S(2)}) collective-permute-start(bf16[4,2,32,1664]{3,2,1,0:T(8,128)(2,1)S(1)} %get-tuple-element.27), channel_id=1, source_target_pairs={{0,32},{16,240},{32,0},{48,80},{64,96},{80,48},{96,64},{112,144},{... | collective-permute-start | bytes 2555912 | tf_op jit(solution)/shard_map/ppermute | solution.py:28
  46.4 7.4 %collective-permute-start.9 = (bf16[2,2,32,1664]{3,2,1,0:T(8,128)(2,1)S(1)}, bf16[2,2,32,1664]{3,2,1,0:T(8,128)(2,1)S(1)}, u32[]{:S(2)}, u32[]{:S(2)}) collective-permute-start(bf16[2,2,32,1664]{3,2,1,0:T(8,128)(2,1)S(1)} %get-tuple-element.29), channel_id=1, source_target_pairs={{0,224},{16,48},{32,64},{48,16},{64,32},{80,112},{96,128},{112,80}... | collective-permute-start | bytes 1277960 | tf_op jit(solution)/shard_map/ppermute | solution.py:28
  53.9 12.4 %collective-permute-start.10 = (bf16[1,2,32,1664]{3,2,1,0:T(8,128)(2,1)S(1)}, bf16[1,2,32,1664]{3,2,1,0:T(8,128)(2,1)S(1)}, u32[]{:S(2)}, u32[]{:S(2)}) collective-permute-start(bf16[1,2,32,1664]{3,2,1,0:T(8,128)(2,1)S(1)} %get-tuple-element.31), channel_id=1, source_target_pairs={{0,96},{16,176},{32,192},{48,144},{64,160},{80,240},{96,0},{112,20... | collective-permute-start | bytes 638984 | tf_op jit(solution)/shard_map/ppermute | solution.py:28
  66.4 8.2 %collective-permute-start.11 = (bf16[1,32,1664]{2,1,0:T(8,128)(2,1)S(1)}, bf16[1,32,1664]{2,1,0:T(8,128)(2,1)S(1)}, u32[]{:S(2)}, u32[]{:S(2)}) collective-permute-start(bf16[1,32,1664]{2,1,0:T(8,128)(2,1)S(1)} %shard_map.56.refs_0_), channel_id=1, source_target_pairs={{0,96},{16,176},{32,192},{48,144},{64,160},{80,240},{96,0},{112,20... | collective-permute-start | bytes 319496 | tf_op jit(solution)/shard_map/ppermute | solution.py:28
  74.7 5.1 %collective-permute-start.12 = (bf16[2,32,1664]{2,1,0:T(8,128)(2,1)S(1)}, bf16[2,32,1664]{2,1,0:T(8,128)(2,1)S(1)}, u32[]{:S(2)}, u32[]{:S(2)}) collective-permute-start(bf16[2,32,1664]{2,1,0:T(8,128)(2,1)S(1)} %shard_map.57.refs_0_), channel_id=1, source_target_pairs={{0,224},{16,48},{32,64},{48,16},{64,32},{80,112},{96,128},{112,80}... | collective-permute-start | bytes 638984 | tf_op jit(solution)/shard_map/ppermute | solution.py:28
  79.8 8.5 %collective-permute-start.13 = (bf16[4,32,1664]{2,1,0:T(8,128)(2,1)S(1)}, bf16[4,32,1664]{2,1,0:T(8,128)(2,1)S(1)}, u32[]{:S(2)}, u32[]{:S(2)}) collective-permute-start(bf16[4,32,1664]{2,1,0:T(8,128)(2,1)S(1)} %shard_map.58.sent), channel_id=1, source_target_pairs={{0,32},{16,240},{32,0},{48,80},{64,96},{80,48},{96,64},{112,144},{... | collective-permute-start | bytes 1277960 | tf_op jit(solution)/shard_map/ppermute | solution.py:28
  88.3 4.6 %collective-permute-start.14 = (bf16[8,32,1664]{2,1,0:T(8,128)(2,1)S(1)}, bf16[8,32,1664]{2,1,0:T(8,128)(2,1)S(1)}, u32[]{:S(2)}, u32[]{:S(2)}) collective-permute-start(bf16[8,32,1664]{2,1,0:T(8,128)(2,1)S(1)} %shard_map.59.own), channel_id=1, source_target_pairs={{0,16},{16,0},{1,17},{17,1},{2,18},{18,2},{3,19},{19,3},{4,20},{20... | collective-permute-start | bytes 2555912 | tf_op jit(solution)/shard_map/ppermute | solution.py:32
  95.0 5.6 %collective-permute-start.15 = (bf16[4,32,1024]{2,1,0:T(8,128)(2,1)S(1)}, bf16[4,32,1024]{2,1,0:T(8,128)(2,1)S(1)}, u32[]{:S(2)}, u32[]{:S(2)}) collective-permute-start(bf16[4,32,1024]{2,1,0:T(8,128)(2,1)S(1)} %get-tuple-element.34), channel_id=1, source_target_pairs={{0,1},{16,20},{1,0},{17,21},{2,3},{18,22},{3,2},{19,23},{4,5},{20,... | collective-permute-start | bytes 786440 | tf_op jit(solution)/shard_map/ppermute | solution.py:41
  95.1 8.3 %collective-permute-start.16 = (bf16[4,32,1024]{2,1,0:T(8,128)(2,1)S(1)}, bf16[4,32,1024]{2,1,0:T(8,128)(2,1)S(1)}, u32[]{:S(2)}, u32[]{:S(2)}) collective-permute-start(bf16[4,32,1024]{2,1,0:T(8,128)(2,1)S(1)} %get-tuple-element.35), channel_id=1, source_target_pairs={{0,2},{16,24},{1,3},{17,25},{2,0},{18,26},{3,1},{19,27},{4,6},{20,... | collective-permute-start | bytes 786440 | tf_op jit(solution)/shard_map/ppermute | solution.py:41
  96.5 9.5 %collective-permute-start.17 = (bf16[4,32,1024]{2,1,0:T(8,128)(2,1)S(1)}, bf16[4,32,1024]{2,1,0:T(8,128)(2,1)S(1)}, u32[]{:S(2)}, u32[]{:S(2)}) collective-permute-start(bf16[4,32,1024]{2,1,0:T(8,128)(2,1)S(1)} %get-tuple-element.36), channel_id=1, source_target_pairs={{0,3},{16,28},{1,2},{17,29},{2,1},{18,30},{3,0},{19,31},{4,7},{20,... | collective-permute-start | bytes 786440 | tf_op jit(solution)/shard_map/ppermute | solution.py:41
  106.2 3.9 %collective-permute-start.18 = (bf16[32,1024]{1,0:T(8,128)(2,1)S(1)}, bf16[32,1024]{1,0:T(8,128)(2,1)S(1)}, u32[]{:S(2)}, u32[]{:S(2)}) collective-permute-start(bf16[32,1024]{1,0:T(8,128)(2,1)S(1)} %get-tuple-element.38), channel_id=1, source_target_pairs={{0,4},{16,17},{1,5},{17,16},{2,6},{18,19},{3,7},{19,18},{4,0},{20,... | collective-permute-start | bytes 196616 | tf_op jit(solution)/shard_map/ppermute | solution.py:41
  106.3 4.7 %collective-permute-start.19 = (bf16[32,1024]{1,0:T(8,128)(2,1)S(1)}, bf16[32,1024]{1,0:T(8,128)(2,1)S(1)}, u32[]{:S(2)}, u32[]{:S(2)}) collective-permute-start(bf16[32,1024]{1,0:T(8,128)(2,1)S(1)} %get-tuple-element.39), channel_id=1, source_target_pairs={{0,8},{16,18},{1,9},{17,19},{2,10},{18,16},{3,11},{19,17},{4,12},{... | collective-permute-start | bytes 196616 | tf_op jit(solution)/shard_map/ppermute | solution.py:41
  107.4 4.4 %collective-permute-start.20 = (bf16[32,1024]{1,0:T(8,128)(2,1)S(1)}, bf16[32,1024]{1,0:T(8,128)(2,1)S(1)}, u32[]{:S(2)}, u32[]{:S(2)}) collective-permute-start(bf16[32,1024]{1,0:T(8,128)(2,1)S(1)} %get-tuple-element.40), channel_id=1, source_target_pairs={{0,12},{16,19},{1,13},{17,18},{2,14},{18,17},{3,15},{19,16},{4,8},... | collective-permute-start | bytes 196616 | tf_op jit(solution)/shard_map/ppermute | solution.py:41

commit v3 on v2

v3 whole, which is shorter than its diff:
```python
import jax
import jax.numpy as jnp
from jax import lax
from jax.experimental import pallas as pl
from jax.experimental.pallas import tpu as pltpu
from jax.sharding import Mesh, PartitionSpec as P

BF = jnp.bfloat16
F32 = jnp.float32
VMEM = pl.BlockSpec(memory_space=pltpu.VMEM)
ANY = pl.BlockSpec(memory_space=pl.ANY)
MIB = 2**20

OWNER = (0, 3, 4, 7, 1, 6, 2, 5)
POSITION = sum(t << (4 * z) for t, z in enumerate(OWNER))
STEPS = (1, -1, 3)


def partner(z, step):
    return (z + STEPS[step] * (1 - 2 * (z % 2)) + 8) % 8


def swap_z(v, step):
    pairs = []
    for z in range(8):
        pairs.append((2 * z, 2 * partner(z, step)))
        pairs.append((2 * z + 1, 2 * ((8 - partner((8 - z) % 8, step)) % 8) + 1))
    return lax.ppermute(v, ("z", "core"), pairs)


def swap_core(v):
    return lax.ppermute(v, "core", [(0, 1), (1, 0)])


def swap_grid(v, near, far):
    pairs = []
    for x in range(4):
        for y in range(4):
            pairs.append((4 * x + y, 4 * (x ^ near) + (y ^ far)))
            pairs.append((16 + 4 * x + y, 16 + 4 * (x ^ far) + (y ^ near)))
    return lax.ppermute(v, ("core", "x", "y"), pairs)


def own_z():
    z = lax.axis_index("z")
    return jnp.where(lax.axis_index("core") == 0, z, (8 - z) % 8)


def is_in(z, members):
    return ((sum(1 << m for m in members) >> z) & 1) == 1


def shape(*dims, dtype=BF):
    return jax.ShapeDtypeStruct(dims, dtype)


def call(body, outs, *ins, flops=0, spec=VMEM, scratch=(), limit=16, after=()):
    size = sum(v.size * v.dtype.itemsize for v in (*ins, *outs))
    n = len(ins)
    return pl.pallas_call(
        lambda *refs: body(*refs[len(after) :]),
        out_shape=outs,
        in_specs=[ANY] * len(after) + [spec] * n,
        out_specs=[VMEM] * len(outs),
        scratch_shapes=list(scratch),
        cost_estimate=pl.CostEstimate(flops=1, bytes_accessed=1, transcendentals=0),
        compiler_params=pltpu.CompilerParams(vmem_limit_bytes=limit * MIB),
    )(*after, *ins)


def load(weight):
    def body(source, out, sem):
        copy = pltpu.make_async_copy(source, out, sem)
        copy.start()
        copy.wait()

    sems = [pltpu.SemaphoreType.DMA(())]
    return call(body, [shape(*weight.shape)], weight, spec=ANY, scratch=sems, limit=48)[0]


def join(*parts, after=()):
    rows = [p.shape[0] for p in parts]

    def body(*refs):
        at = 0
        for ref, n in zip(refs, rows):
            refs[-1][at : at + n] = ref[...]
            at += n

    return call(body, [shape(sum(rows), *parts[0].shape[1:])], *parts, after=after)[0]


def tiles(start, stop, tile):
    return [(at, min(tile, stop - at)) for at in range(start, stop, tile)]


def project(part, columns, first, second, gate_weight, up_weight, after=()):
    _, rows, depth = first.shape
    half = 4 * rows
    widths = [stop - start for start, stop in columns]

    def body(first, second, gate, up, *refs):
        left = refs[-1]
        mine = 2 * (part ^ lax.axis_index("core"))
        for j, ref in enumerate((first, second)):
            for h in range(2):
                at = (2 * j + h) * rows
                left[at : at + rows] = ref[2 - mine + h]
                left[half + at : half + at + rows] = ref[mine + h]
        for n, (start, stop) in enumerate(columns):
            theirs, ours = refs[2 * n : 2 * n + 2]
            for at, size in tiles(start, stop, 256):
                to = slice(at - start, at - start + size)
                for i, weight in enumerate((gate, up)):
                    out = jnp.dot(left[...], weight[:, at : at + size], preferred_element_type=F32)
                    out = out.astype(BF)
                    theirs[:, i, :, to] = out[:half].reshape(4, rows, size)
                    ours[:, i, :, to] = out[half:].reshape(4, rows, size)

    outs = [shape(4, 2, rows, width) for width in widths for _ in range(2)]
    return call(
        body, outs, first, second, gate_weight, up_weight,
        flops=8 * half * depth * sum(widths), scratch=[pltpu.VMEM((2 * half, depth), BF)], after=after,
    )


def first_sums(ours, theirs, after=()):
    _, _, rows, width = ours[0].shape

    def body(o0, o1, t0, t1, send, keep):
        core = lax.axis_index("core")

        def total(t, i):
            p, j, k = t // 4, t // 2 % 2, t % 2
            o, r, s = ((o0, t0, t1), (o1, t1, t0))[p]
            got = jnp.where(core == 0, r[2 * k + j, i], s[2 * k + j, i])
            return o[t % 4, i].astype(F32) + got.astype(F32)

        def fill(kept, sent):
            for n in range(4):
                for i in range(2):
                    send[n, i] = total(sent + n, i).astype(BF)
                    keep[n, i] = total(kept + n, i)

        inside = is_in(own_z(), OWNER[:4])
        pl.when(inside)(lambda: fill(0, 4))
        pl.when(jnp.logical_not(inside))(lambda: fill(4, 0))

    outs = [shape(4, 2, rows, width), shape(4, 2, rows, width, dtype=F32)]
    return call(body, outs, *ours, *theirs, after=after)


def next_sums(got, kept, after=()):
    n, _, rows, width = got.shape
    m = n // 2
    firsts = OWNER[0:2] + OWNER[4:6] if m == 2 else OWNER[::2]

    def body(got, kept, send, keep):
        at = jnp.where(is_in(own_z(), firsts), 0, m)
        for i in range(m):
            send[i] = (got[m - at + i].astype(F32) + kept[m - at + i]).astype(BF)
            keep[i] = got[at + i].astype(F32) + kept[at + i]

    outs = [shape(m, 2, rows, width), shape(m, 2, rows, width, dtype=F32)]
    return call(body, outs, got, kept, after=after)


def activate(got, kept, after=()):
    _, _, rows, width = got.shape

    def body(got, kept, out):
        gate = got[0, 0].astype(F32) + kept[0, 0]
        up = got[0, 1].astype(F32) + kept[0, 1]
        out[0] = (gate / (1 + jnp.exp(-gate)) * up).astype(BF)

    return call(body, [shape(1, rows, width)], got, kept, after=after)[0]


def assemble(sent, got, after=()):
    _, rows, width = sent.shape

    def body(sent, got, out):
        me = own_z()
        for source, ref in ((me, sent), (partner(me, 0), got)):
            near = partner(source, 1)
            for i, owner in enumerate((source, partner(source, 2), near, partner(near, 2))):
                out[(POSITION >> (4 * owner)) & 7] = ref[i]

    return call(body, [shape(8, rows, width)], sent, got, after=after)[0]


def order(own, other, left):
    rows = own.shape[1]
    core = lax.axis_index("core")
    for j in range(4):
        for q in range(4):
            at = (4 * j + q) * rows
            if q < 2:
                left[at : at + rows] = own[2 * j + q]
            else:
                left[at : at + rows] = other[4 * ((j >> 1) ^ 1 ^ core) + 2 * (q - 2) + (j & 1)]


def expand(own, other, weight):
    _, rows, depth = own.shape
    columns = weight.shape[1]

    def body(own, other, weight, total, left):
        order(own, other, left)
        for at, n in tiles(0, columns, 256):
            right = weight[:depth, at : at + n]
            total[:, at : at + n] = jnp.dot(left[...], right, preferred_element_type=F32)

    return call(
        body, [shape(16 * rows, columns, dtype=F32)], own, other, weight,
        flops=32 * rows * depth * columns, scratch=[pltpu.VMEM((16 * rows, depth), BF)],
    )[0]


def expand_rest(own, other, weight, total):
    _, rows, depth = own.shape
    columns = weight.shape[1]
    start = weight.shape[0] - depth

    def body(own, other, weight, total, *refs):
        outs, left = refs[:4], refs[4]
        order(own, other, left)
        for at, n in tiles(0, columns, 256):
            right = weight[start:, at : at + n]
            out = jnp.dot(left[...], right, preferred_element_type=F32) + total[:, at : at + n]
            out = out.astype(BF).reshape(4, 4, rows, n)
            for j in range(4):
                outs[j][:, :, at : at + n] = out[j]

    return call(
        body, [shape(4, rows, columns)] * 4, own, other, weight, total,
        flops=32 * rows * depth * columns, scratch=[pltpu.VMEM((16 * rows, depth), BF)],
    )


def sum_far(*parts):
    _, rows, columns = parts[0].shape

    def body(a, c, b, d, keep, *sends):
        core = lax.axis_index("core")
        for k in range(4):
            low, high = k ^ (2 * core), k ^ 2 ^ (2 * core)
            total = (a[low].astype(F32) + b[low].astype(F32)) + (c[high].astype(F32) + d[high].astype(F32))
            if k == 0:
                keep[...] = total
            else:
                sends[k - 1][...] = total.astype(BF)

    outs = [shape(rows, columns, dtype=F32)] + [shape(rows, columns)] * 3
    return call(body, outs, *parts)


def sum_near(*parts):
    def body(a, b, c, d, out):
        total = (a[...] + b[...].astype(F32)) + (c[...].astype(F32) + d[...].astype(F32))
        out[...] = total.astype(BF)

    return call(body, [shape(*parts[0].shape)], *parts)[0]


def on_device(acts, gate_weight, up_weight, down_weight):
    own = acts[None]
    near = [swap_grid(own, k, 0) for k in (1, 2, 3)]
    gate_weight = load(gate_weight)
    piece = join(load(own), *near)
    far = [swap_grid(piece, 0, j) for j in (1, 2, 3)]
    up_weight = load(up_weight)
    width = gate_weight.shape[1]
    cut = 896
    low, high = (0, cut), (cut, width)
    theirs_a0, ours_a0, theirs_b0, ours_b0 = project(0, (low, high), piece, far[0], gate_weight, up_weight)
    theirs_a0, theirs_b0 = swap_core(theirs_a0), swap_core(theirs_b0)
    theirs_a1, ours_a1 = project(1, (low,), far[1], far[2], gate_weight, up_weight, after=(ours_a0,))
    theirs_a1 = swap_core(theirs_a1)
    send_a, keep_a = first_sums((ours_a0, ours_a1), (theirs_a0, theirs_a1))
    got_a = swap_z(send_a, 0)
    theirs_b1, ours_b1 = project(1, (high,), far[1], far[2], gate_weight, up_weight, after=(ours_a1,))
    theirs_b1 = swap_core(theirs_b1)
    send_b, keep_b = first_sums((ours_b0, ours_b1), (theirs_b0, theirs_b1), after=(send_a,))
    got_b = swap_z(send_b, 0)
    down_weight = load(down_weight)
    send_a, keep_a = next_sums(got_a, keep_a, after=(send_b,))
    got_a = swap_z(send_a, 1)
    send_b, keep_b = next_sums(got_b, keep_b, after=(send_a,))
    got_b = swap_z(send_b, 1)
    send_a, keep_a = next_sums(got_a, keep_a, after=(send_b, down_weight))
    got_a = swap_z(send_a, 2)
    send_b, keep_b = next_sums(got_b, keep_b, after=(send_a,))
    got_b = swap_z(send_b, 2)
    have_a = activate(got_a, keep_a, after=(send_b,))
    got_a = swap_z(have_a, 2)
    have_b = activate(got_b, keep_b, after=(have_a,))
    got_b = swap_z(have_b, 2)
    for step in (1, 0):
        have_a = join(have_a, got_a, after=(have_b,))
        got_a = swap_z(have_a, step)
        have_b = join(have_b, got_b, after=(have_a,))
        got_b = swap_z(have_b, step)
    hidden_a = assemble(have_a, got_a, after=(have_b,))
    other_a = swap_core(hidden_a)
    hidden_b = assemble(have_b, got_b, after=(hidden_a,))
    other_b = swap_core(hidden_b)
    total = expand(hidden_a, other_a, down_weight)
    terms = expand_rest(hidden_b, other_b, down_weight, total)
    sums = sum_far(terms[0], *[swap_grid(terms[j], 0, j) for j in (2, 1, 3)])
    return sum_near(sums[0], *[swap_grid(sums[k], k, 0) for k in (2, 1, 3)])


def solution(mesh):
    grid = Mesh(mesh.devices.reshape(8, 2, 4, 4), ("z", "core", "x", "y"))
    row, col = ("z", "core"), ("x", "y")
    in_specs = (P(col, row), P(row, col), P(row, col), P(col, row))
    return jax.shard_map(
        on_device, mesh=grid, in_specs=in_specs, out_specs=P(col, row), check_vma=False
    )
```

time: 114 us -> 103 us (0.904)
  waiting for transfers between devices: 60.9 us -> 32.4 us
  starting transfers between devices: 36.7 us -> 54.8 us
    ppermute x6 -> x12, waiting for transfers between devices: 44.4 us -> 18.8 us  [swap_z(): return lax.ppermute(v, ('z', 'core'), pairs)]
    ppermute x6 -> x12, starting transfers between devices: 11 us -> 27.8 us  [swap_z(): return lax.ppermute(v, ('z', 'core'), pairs)]
    ppermute x3 -> x6, waiting for transfers between devices: 4.01 us -> 0.1 us  [swap_core(): return lax.ppermute(v, 'core', [(0, 1), (1, 0)])]
    ppermute x3 -> x6, starting transfers between devices: 9.15 us -> 12.1 us  [swap_core(): return lax.ppermute(v, 'core', [(0, 1), (1, 0)])]
    ppermute x12, starting transfers between devices: 16.6 us -> 14.9 us  [swap_grid(): return lax.ppermute(v, ('core', 'x', 'y'), pairs)]
    pallas_call x17 -> x26, Pallas kernels: 13.8 us -> 14.3 us  [call(): pl.pallas_call(lambda *refs: body(*refs[len(after):]), out_shape=outs, in...]
  transfers between devices with their start and end apart: 21 -> 30, of which waited for: 16 -> 17; matrix products, arithmetic and copies ran while one was open for 0% -> 0% of each run, Pallas kernels for 9% -> 12%
where the time goes in v3:
time: 103 us; the launch traced here: 102 us
  starting transfers between devices  54.8 us (53%)
  waiting for transfers between devices  32.4 us (31%)
  Pallas kernels  14.3 us (14%)
    ppermute x12, starting transfers between devices, swap_z(): return lax.ppermute(v, ('z', 'core'), pairs)  27.8 us
    ppermute x12, waiting for transfers between devices, swap_z(): return lax.ppermute(v, ('z', 'core'), pairs)  18.8 us
    ppermute x12, starting transfers between devices, swap_grid(): return lax.ppermute(v, ('core', 'x', 'y'), pairs)  14.9 us
    pallas_call x26, Pallas kernels, call(): pl.pallas_call(lambda *refs: body(*refs[len(after):]), out_shape=outs, in...  14.3 us
    ppermute x12, waiting for transfers between devices, swap_grid(): return lax.ppermute(v, ('core', 'x', 'y'), pairs)  13.4 us
    ppermute x6, starting transfers between devices, swap_core(): return lax.ppermute(v, 'core', [(0, 1), (1, 0)])  12.1 us
  transfers between devices with their start and end apart: 30, of which 17 were waited for; matrix products, arithmetic and copies ran while one was open for 0% of the time, Pallas kernels for 12%

profile of v3, /device:TPU:1, one launch (start us, length us, event | category | flops | bytes accessed | tf_op | source)
XLA Modules:
  0.0 102.5 jit_solution(10778934380077331965)
XLA Ops:
  0.0 3.6 %collective-permute-start.2 = (bf16[1,32,1024]{2,1,0:T(8,128)(2,1)}, bf16[1,32,1024]{2,1,0:T(8,128)(2,1)S(1)}, u32[]{:S(2)}, u32[]{:S(2)}) collective-permute-start(bf16[1,32,1024]{2,1,0:T(8,128)(2,1)} %bitcast.1), channel_id=1, source_target_pairs={{0,12},{16,19},{1,13},{17,18},{2,14},{18,17},{3,15},{19,16},{4,8},... | collective-permute-start | bytes 196616 | tf_op jit(solution)/shard_map/ppermute | solution.py:41
  3.6 0.3 collective-permute-start.1
  3.9 0.2 collective-permute-start
  4.1 0.9 copy-done
  5.0 0.1 shard_map.46.refs_0_
  5.1 0.7 collective-permute-done.2.refs_3_
  5.8 2.6 %collective-permute-done.1.refs_2_ = bf16[1,32,1024]{2,1,0:T(8,128)(2,1)S(1)} collective-permute-done((bf16[1,32,1024]{2,1,0:T(8,128)(2,1)}, bf16[1,32,1024]{2,1,0:T(8,128)(2,1)S(1)}, u32[]{:S(2)}, u32[]{:S(2)}) %collective-permute-start.1) | collective-permute-done | bytes 65568 | tf_op jit(solution)/shard_map/ppermute | solution.py:41
  8.4 1.3 %collective-permute-start.3 = (bf16[4,32,1024]{2,1,0:T(8,128)(2,1)S(1)}, bf16[4,32,1024]{2,1,0:T(8,128)(2,1)S(1)}, u32[]{:S(2)}, u32[]{:S(2)}) collective-permute-start(bf16[4,32,1024]{2,1,0:T(8,128)(2,1)S(1)} %shard_map.47.refs_0_), channel_id=1, source_target_pairs={{0,1},{16,20},{1,0},{17,21},{2,3},{18,22},{3,2},{19,23},{4,5},{20,... | collective-permute-start | bytes 786440 | tf_op jit(solution)/shard_map/ppermute | solution.py:41
  9.7 1.8 %collective-permute-start.5 = (bf16[4,32,1024]{2,1,0:T(8,128)(2,1)S(1)}, bf16[4,32,1024]{2,1,0:T(8,128)(2,1)S(1)}, u32[]{:S(2)}, u32[]{:S(2)}) collective-permute-start(bf16[4,32,1024]{2,1,0:T(8,128)(2,1)S(1)} %shard_map.47.refs_0_), channel_id=1, source_target_pairs={{0,3},{16,28},{1,2},{17,29},{2,1},{18,30},{3,0},{19,31},{4,7},{20,... | collective-permute-start | bytes 786440 | tf_op jit(solution)/shard_map/ppermute | solution.py:41
  11.5 0.9 collective-permute-start.4
  12.5 2.0 %shard_map.48.refs_2_.refs_3_ = bf16[1024,1664]{1,0:T(8,128)(2,1)S(1)} custom-call(bf16[1024,1664]{1,0:T(8,128)(2,1)} %refs_0_.3), custom_call_target="tpu_custom_call" | custom-call | flops 1 | bytes 1 | tf_op jit(solution)/shard_map/pallas_call | solution.py:60
  14.4 2.0 %shard_map.49.refs_3_.refs_4_ = bf16[1024,1664]{1,0:T(8,128)(2,1)S(1)} custom-call(bf16[1024,1664]{1,0:T(8,128)(2,1)} %refs_0_.4), custom_call_target="tpu_custom_call" | custom-call | flops 1 | bytes 1 | tf_op jit(solution)/shard_map/pallas_call | solution.py:60
  16.4 2.1 %shard_map.50 = (bf16[4,2,32,896]{3,2,1,0:T(8,128)(2,1)S(1)}, bf16[4,2,32,896]{3,2,1,0:T(8,128)(2,1)S(1)}, bf16[4,2,32,768]{3,2,1,0:T(8,128)(2,1)S(1)}, bf16[4,2,32,768]{3,2,1,0:T(8,128)(2,1)S(1)}) custom-call(bf16[4,32,1024]{2,1,0:T(8,128)(2,1)S(1)} %shard_map.47.refs_0_, bf16[4,32,1024]{2,1,0:T(8,128)(2,1)S(1)} %collective-permute-done.3.refs_1_, ...), custom_call_target="tpu_custom_call" | custom-call | flops 1 | bytes 1 | tf_op jit(solution)/shard_map/pallas_call | solution.py:60
  18.5 2.5 %collective-permute-start.6 = (bf16[4,2,32,896]{3,2,1,0:T(8,128)(2,1)S(1)}, bf16[4,2,32,896]{3,2,1,0:T(8,128)(2,1)S(1)}, u32[]{:S(2)}, u32[]{:S(2)}) collective-permute-start(bf16[4,2,32,896]{3,2,1,0:T(8,128)(2,1)S(1)} %get-tuple-element.35), channel_id=1, source_target_pairs={{0,16},{16,0},{1,17},{17,1},{2,18},{18,2},{3,19},{19,3},{4,20},{20... | collective-permute-start | bytes 1376264 | tf_op jit(solution)/shard_map/ppermute | solution.py:32
  21.0 1.3 %shard_map.51 = (bf16[4,2,32,896]{3,2,1,0:T(8,128)(2,1)S(1)}, bf16[4,2,32,896]{3,2,1,0:T(8,128)(2,1)S(1)}) custom-call(bf16[4,2,32,896]{3,2,1,0:T(8,128)(2,1)S(1)} %get-tuple-element.33.refs_0_, bf16[4,32,1024]{2,1,0:T(8,128)(2,1)S(1)} %collective-permute-done.4.refs_1_, bf16[4,32,1024]{2,1,0:T(8,128)(2,1)S(1)} %collective-permute-done.5.refs_2_, ...), custom_call_target="tpu_custom_call" | custom-call | flops 1 | bytes 1 | tf_op jit(solution)/shard_map/pallas_call | solution.py:60
  22.2 1.4 %collective-permute-start.7 = (bf16[4,2,32,896]{3,2,1,0:T(8,128)(2,1)S(1)}, bf16[4,2,32,896]{3,2,1,0:T(8,128)(2,1)S(1)}, u32[]{:S(2)}, u32[]{:S(2)}) collective-permute-start(bf16[4,2,32,896]{3,2,1,0:T(8,128)(2,1)S(1)} %get-tuple-element.36), channel_id=1, source_target_pairs={{0,16},{16,0},{1,17},{17,1},{2,18},{18,2},{3,19},{19,3},{4,20},{20... | collective-permute-start | bytes 1376264 | tf_op jit(solution)/shard_map/ppermute | solution.py:32
  23.7 0.1 collective-permute-start.8
  23.8 1.0 shard_map.53
  24.8 0.5 collective-permute-start.9
  25.3 0.2 shard_map.52
  25.5 5.7 %collective-permute-start.10 = (bf16[4,2,32,896]{3,2,1,0:T(8,128)(2,1)S(1)}, bf16[4,2,32,896]{3,2,1,0:T(8,128)(2,1)S(1)}, u32[]{:S(2)}, u32[]{:S(2)}) collective-permute-start(bf16[4,2,32,896]{3,2,1,0:T(8,128)(2,1)S(1)} %get-tuple-element.37.refs_0_), channel_id=1, source_target_pairs={{0,32},{16,240},{32,0},{48,80},{64,96},{80,48},{96,64},{112,144},{... | collective-permute-start | bytes 1376264 | tf_op jit(solution)/shard_map/ppermute | solution.py:28
  31.2 0.2 shard_map.54
  31.4 1.1 %collective-permute-start.11 = (bf16[4,2,32,768]{3,2,1,0:T(8,128)(2,1)S(1)}, bf16[4,2,32,768]{3,2,1,0:T(8,128)(2,1)S(1)}, u32[]{:S(2)}, u32[]{:S(2)}) collective-permute-start(bf16[4,2,32,768]{3,2,1,0:T(8,128)(2,1)S(1)} %get-tuple-element.42.refs_0_), channel_id=1, source_target_pairs={{0,32},{16,240},{32,0},{48,80},{64,96},{80,48},{96,64},{112,144},{... | collective-permute-start | bytes 1179656 | tf_op jit(solution)/shard_map/ppermute | solution.py:28
  32.5 4.6 %collective-permute-done.10.refs_1_ = bf16[4,2,32,896]{3,2,1,0:T(8,128)(2,1)S(1)} collective-permute-done((bf16[4,2,32,896]{3,2,1,0:T(8,128)(2,1)S(1)}, bf16[4,2,32,896]{3,2,1,0:T(8,128)(2,1)S(1)}, u32[]{:S(2)}, u32[]{:S(2)}) %collective-permute-start.10) | collective-permute-done | bytes 458784 | tf_op jit(solution)/shard_map/ppermute | solution.py:28
  37.0 0.1 shard_map.55
  37.1 0.1 collective-permute-start.12
  37.2 4.3 %collective-permute-done.11.refs_1_ = bf16[4,2,32,768]{3,2,1,0:T(8,128)(2,1)S(1)} collective-permute-done((bf16[4,2,32,768]{3,2,1,0:T(8,128)(2,1)S(1)}, bf16[4,2,32,768]{3,2,1,0:T(8,128)(2,1)S(1)}, u32[]{:S(2)}, u32[]{:S(2)}) %collective-permute-start.11) | collective-permute-done | bytes 393248 | tf_op jit(solution)/shard_map/ppermute | solution.py:28
  41.6 0.1 shard_map.56
  41.6 0.3 collective-permute-start.13
  41.9 2.0 %shard_map.57.refs_1_.refs_2_ = bf16[1664,1024]{1,0:T(8,128)(2,1)S(1)} custom-call(bf16[1664,1024]{1,0:T(8,128)(2,1)} %refs_0_.5), custom_call_target="tpu_custom_call" | custom-call | flops 1 | bytes 1 | tf_op jit(solution)/shard_map/pallas_call | solution.py:60
  44.0 4.1 %collective-permute-start.14 = (bf16[1,2,32,896]{3,2,1,0:T(8,128)(2,1)S(1)}, bf16[1,2,32,896]{3,2,1,0:T(8,128)(2,1)S(1)}, u32[]{:S(2)}, u32[]{:S(2)}) collective-permute-start(bf16[1,2,32,896]{3,2,1,0:T(8,128)(2,1)S(1)} %get-tuple-element.48.refs_0_), channel_id=1, source_target_pairs={{0,96},{16,176},{32,192},{48,144},{64,160},{80,240},{96,0},{112,20... | collective-permute-start | bytes 344072 | tf_op jit(solution)/shard_map/ppermute | solution.py:28
  48.1 1.0 collective-permute-start.15
  49.1 2.9 %collective-permute-done.14.refs_1_ = bf16[1,2,32,896]{3,2,1,0:T(8,128)(2,1)S(1)} collective-permute-done((bf16[1,2,32,896]{3,2,1,0:T(8,128)(2,1)S(1)}, bf16[1,2,32,896]{3,2,1,0:T(8,128)(2,1)S(1)}, u32[]{:S(2)}, u32[]{:S(2)}) %collective-permute-start.14) | collective-permute-done | bytes 114720 | tf_op jit(solution)/shard_map/ppermute | solution.py:28
  52.0 4.2 %collective-permute-start.16 = (bf16[1,32,896]{2,1,0:T(8,128)(2,1)S(1)}, bf16[1,32,896]{2,1,0:T(8,128)(2,1)S(1)}, u32[]{:S(2)}, u32[]{:S(2)}) collective-permute-start(bf16[1,32,896]{2,1,0:T(8,128)(2,1)S(1)} %shard_map.60.refs_0_.refs_1_), channel_id=1, source_target_pairs={{0,96},{16,176},{32,192},{48,144},{64,160},{80,240},{96,0},{112,20... | collective-permute-start | bytes 172040 | tf_op jit(solution)/shard_map/ppermute | solution.py:28
  56.2 0.6 collective-permute-done.15.refs_1_
  56.9 1.3 %collective-permute-done.16.refs_2_ = bf16[1,32,896]{2,1,0:T(8,128)(2,1)S(1)} collective-permute-done((bf16[1,32,896]{2,1,0:T(8,128)(2,1)S(1)}, bf16[1,32,896]{2,1,0:T(8,128)(2,1)S(1)}, u32[]{:S(2)}, u32[]{:S(2)}) %collective-permute-start.16) | collective-permute-done | bytes 57376 | tf_op jit(solution)/shard_map/ppermute | solution.py:28
  58.2 3.1 %collective-permute-start.18 = (bf16[2,32,896]{2,1,0:T(8,128)(2,1)S(1)}, bf16[2,32,896]{2,1,0:T(8,128)(2,1)S(1)}, u32[]{:S(2)}, u32[]{:S(2)}) collective-permute-start(bf16[2,32,896]{2,1,0:T(8,128)(2,1)S(1)} %shard_map.62.refs_0_.refs_1_), channel_id=1, source_target_pairs={{0,224},{16,48},{32,64},{48,16},{64,32},{80,112},{96,128},{112,80}... | collective-permute-start | bytes 344072 | tf_op jit(solution)/shard_map/ppermute | solution.py:28
  61.3 1.9 %collective-permute-start.17 = (bf16[1,32,768]{2,1,0:T(8,128)(2,1)S(1)}, bf16[1,32,768]{2,1,0:T(8,128)(2,1)S(1)}, u32[]{:S(2)}, u32[]{:S(2)}) collective-permute-start(bf16[1,32,768]{2,1,0:T(8,128)(2,1)S(1)} %shard_map.61.refs_0_.refs_1_), channel_id=1, source_target_pairs={{0,96},{16,176},{32,192},{48,144},{64,160},{80,240},{96,0},{112,20... | collective-permute-start | bytes 147464 | tf_op jit(solution)/shard_map/ppermute | solution.py:28
  63.2 4.0 %collective-permute-done.17.refs_2_ = bf16[1,32,768]{2,1,0:T(8,128)(2,1)S(1)} collective-permute-done((bf16[1,32,768]{2,1,0:T(8,128)(2,1)S(1)}, bf16[1,32,768]{2,1,0:T(8,128)(2,1)S(1)}, u32[]{:S(2)}, u32[]{:S(2)}) %collective-permute-start.17) | collective-permute-done | bytes 49184 | tf_op jit(solution)/shard_map/ppermute | solution.py:28
  67.3 0.6 collective-permute-start.19
  67.9 2.8 %collective-permute-start.20 = (bf16[4,32,896]{2,1,0:T(8,128)(2,1)S(1)}, bf16[4,32,896]{2,1,0:T(8,128)(2,1)S(1)}, u32[]{:S(2)}, u32[]{:S(2)}) collective-permute-start(bf16[4,32,896]{2,1,0:T(8,128)(2,1)S(1)} %shard_map.64.refs_0_.refs_1_), channel_id=1, source_target_pairs={{0,32},{16,240},{32,0},{48,80},{64,96},{80,48},{96,64},{112,144},{... | collective-permute-start | bytes 688136 | tf_op jit(solution)/shard_map/ppermute | solution.py:28
  70.7 0.1 collective-permute-done.19.refs_2_
  70.8 3.1 %collective-permute-start.21 = (bf16[4,32,768]{2,1,0:T(8,128)(2,1)S(1)}, bf16[4,32,768]{2,1,0:T(8,128)(2,1)S(1)}, u32[]{:S(2)}, u32[]{:S(2)}) collective-permute-start(bf16[4,32,768]{2,1,0:T(8,128)(2,1)S(1)} %shard_map.65.refs_0_.refs_1_), channel_id=1, source_target_pairs={{0,32},{16,240},{32,0},{48,80},{64,96},{80,48},{96,64},{112,144},{... | collective-permute-start | bytes 589832 | tf_op jit(solution)/shard_map/ppermute | solution.py:28
  73.9 0.9 collective-permute-done.20.refs_2_
  74.8 0.1 shard_map.66.refs_0_
  74.9 5.2 %collective-permute-start.23 = (bf16[8,32,896]{2,1,0:T(8,128)(2,1)S(1)}, bf16[8,32,896]{2,1,0:T(8,128)(2,1)S(1)}, u32[]{:S(2)}, u32[]{:S(2)}) collective-permute-start(bf16[8,32,896]{2,1,0:T(8,128)(2,1)S(1)} %shard_map.66.refs_0_), channel_id=1, source_target_pairs={{0,16},{16,0},{1,17},{17,1},{2,18},{18,2},{3,19},{19,3},{4,20},{20... | collective-permute-start | bytes 1376264 | tf_op jit(solution)/shard_map/ppermute | solution.py:32
  80.1 0.1 shard_map.67.refs_0_
  80.2 2.4 %collective-permute-start.22 = (bf16[8,32,768]{2,1,0:T(8,128)(2,1)S(1)}, bf16[8,32,768]{2,1,0:T(8,128)(2,1)S(1)}, u32[]{:S(2)}, u32[]{:S(2)}) collective-permute-start(bf16[8,32,768]{2,1,0:T(8,128)(2,1)S(1)} %shard_map.67.refs_0_), channel_id=1, source_target_pairs={{0,16},{16,0},{1,17},{17,1},{2,18},{18,2},{3,19},{19,3},{4,20},{20... | collective-permute-start | bytes 1179656 | tf_op jit(solution)/shard_map/ppermute | solution.py:32
  82.5 1.3 %shard_map.68.refs_3_ = f32[512,1024]{1,0:T(8,128)S(1)} custom-call(bf16[8,32,896]{2,1,0:T(8,128)(2,1)S(1)} %shard_map.66.refs_0_, bf16[8,32,896]{2,1,0:T(8,128)(2,1)S(1)} %collective-permute-done.23.refs_1_, bf16[1664,1024]{1,0:T(8,128)(2,1)S(1)} %shard_map.57.refs_1_.refs_2_), custom_call_target="tpu_custom_call" | custom-call | flops 1 | bytes 1 | tf_op jit(solution)/shard_map/pallas_call | solution.py:60
  83.8 0.1 collective-permute-done.22.refs_1_
  83.9 1.0 shard_map.69
  84.9 1.8 %collective-permute-start.24 = (bf16[4,32,1024]{2,1,0:T(8,128)(2,1)S(1)}, bf16[4,32,1024]{2,1,0:T(8,128)(2,1)S(1)}, u32[]{:S(2)}, u32[]{:S(2)}) collective-permute-start(bf16[4,32,1024]{2,1,0:T(8,128)(2,1)S(1)} %get-tuple-element.54), channel_id=1, source_target_pairs={{0,2},{16,24},{1,3},{17,25},{2,0},{18,26},{3,1},{19,27},{4,6},{20,... | collective-permute-start | bytes 786440 | tf_op jit(solution)/shard_map/ppermute | solution.py:41
  86.7 1.5 %collective-permute-start.26 = (bf16[4,32,1024]{2,1,0:T(8,128)(2,1)S(1)}, bf16[4,32,1024]{2,1,0:T(8,128)(2,1)S(1)}, u32[]{:S(2)}, u32[]{:S(2)}) collective-permute-start(bf16[4,32,1024]{2,1,0:T(8,128)(2,1)S(1)} %get-tuple-element.56), channel_id=1, source_target_pairs={{0,3},{16,28},{1,2},{17,29},{2,1},{18,30},{3,0},{19,31},{4,7},{20,... | collective-permute-start | bytes 786440 | tf_op jit(solution)/shard_map/ppermute | solution.py:41
  88.2 3.8 %collective-permute-done.24.refs_1_ = bf16[4,32,1024]{2,1,0:T(8,128)(2,1)S(1)} collective-permute-done((bf16[4,32,1024]{2,1,0:T(8,128)(2,1)S(1)}, bf16[4,32,1024]{2,1,0:T(8,128)(2,1)S(1)}, u32[]{:S(2)}, u32[]{:S(2)}) %collective-permute-start.24) | collective-permute-done | bytes 262176 | tf_op jit(solution)/shard_map/ppermute | solution.py:41
  92.0 1.5 %collective-permute-done.25.refs_2_ = bf16[4,32,1024]{2,1,0:T(8,128)(2,1)S(1)} collective-permute-done((bf16[4,32,1024]{2,1,0:T(8,128)(2,1)S(1)}, bf16[4,32,1024]{2,1,0:T(8,128)(2,1)S(1)}, u32[]{:S(2)}, u32[]{:S(2)}) %collective-permute-start.25) | collective-permute-done | bytes 262176 | tf_op jit(solution)/shard_map/ppermute | solution.py:41
  93.5 1.3 %collective-permute-done.26.refs_3_ = bf16[4,32,1024]{2,1,0:T(8,128)(2,1)S(1)} collective-permute-done((bf16[4,32,1024]{2,1,0:T(8,128)(2,1)S(1)}, bf16[4,32,1024]{2,1,0:T(8,128)(2,1)S(1)}, u32[]{:S(2)}, u32[]{:S(2)}) %collective-permute-start.26) | collective-permute-done | bytes 262176 | tf_op jit(solution)/shard_map/ppermute | solution.py:41
  94.8 0.1 shard_map.70
  94.9 0.5 collective-permute-start.27
  95.4 2.1 %collective-permute-start.28 = (bf16[32,1024]{1,0:T(8,128)(2,1)S(1)}, bf16[32,1024]{1,0:T(8,128)(2,1)S(1)}, u32[]{:S(2)}, u32[]{:S(2)}) collective-permute-start(bf16[32,1024]{1,0:T(8,128)(2,1)S(1)} %get-tuple-element.59), channel_id=1, source_target_pairs={{0,4},{16,17},{1,5},{17,16},{2,6},{18,19},{3,7},{19,18},{4,0},{20,... | collective-permute-start | bytes 196616 | tf_op jit(solution)/shard_map/ppermute | solution.py:41
  97.5 0.8 collective-permute-start.29
  98.3 1.4 %collective-permute-done.27.refs_1_ = bf16[32,1024]{1,0:T(8,128)(2,1)S(1)} collective-permute-done((bf16[32,1024]{1,0:T(8,128)(2,1)S(1)}, bf16[32,1024]{1,0:T(8,128)(2,1)S(1)}, u32[]{:S(2)}, u32[]{:S(2)}) %collective-permute-start.27) | collective-permute-done | bytes 65568 | tf_op jit(solution)/shard_map/ppermute | solution.py:41
  99.6 0.2 collective-permute-done.28.refs_2_
  99.8 2.0 %collective-permute-done.29.refs_3_ = bf16[32,1024]{1,0:T(8,128)(2,1)S(1)} collective-permute-done((bf16[32,1024]{1,0:T(8,128)(2,1)S(1)}, bf16[32,1024]{1,0:T(8,128)(2,1)S(1)}, u32[]{:S(2)}, u32[]{:S(2)}) %collective-permute-start.29) | collective-permute-done | bytes 65568 | tf_op jit(solution)/shard_map/ppermute | solution.py:41
  101.8 0.7 shard_map.71
  (24 shorter events, 0.3 us)
Async XLA Ops:
  0.0 5.8 %collective-permute-start.2 = (bf16[1,32,1024]{2,1,0:T(8,128)(2,1)}, bf16[1,32,1024]{2,1,0:T(8,128)(2,1)S(1)}, u32[]{:S(2)}, u32[]{:S(2)}) collective-permute-start(bf16[1,32,1024]{2,1,0:T(8,128)(2,1)} %bitcast.1), channel_id=1, source_target_pairs={{0,12},{16,19},{1,13},{17,18},{2,14},{18,17},{3,15},{19,16},{4,8},... | collective-permute-start | bytes 196616 | tf_op jit(solution)/shard_map/ppermute | solution.py:41
  3.6 4.8 %collective-permute-start.1 = (bf16[1,32,1024]{2,1,0:T(8,128)(2,1)}, bf16[1,32,1024]{2,1,0:T(8,128)(2,1)S(1)}, u32[]{:S(2)}, u32[]{:S(2)}) collective-permute-start(bf16[1,32,1024]{2,1,0:T(8,128)(2,1)} %bitcast.2), channel_id=1, source_target_pairs={{0,8},{16,18},{1,9},{17,19},{2,10},{18,16},{3,11},{19,17},{4,12},{... | collective-permute-start | bytes 196616 | tf_op jit(solution)/shard_map/ppermute | solution.py:41
  3.9 4.5 %collective-permute-start = (bf16[1,32,1024]{2,1,0:T(8,128)(2,1)}, bf16[1,32,1024]{2,1,0:T(8,128)(2,1)S(1)}, u32[]{:S(2)}, u32[]{:S(2)}) collective-permute-start(bf16[1,32,1024]{2,1,0:T(8,128)(2,1)} %bitcast.3), channel_id=1, source_target_pairs={{0,4},{16,17},{1,5},{17,16},{2,6},{18,19},{3,7},{19,18},{4,0},{20,... | collective-permute-start | bytes 196616 | tf_op jit(solution)/shard_map/ppermute | solution.py:41
  4.1 0.9 copy-start
  8.4 8.0 %collective-permute-start.3 = (bf16[4,32,1024]{2,1,0:T(8,128)(2,1)S(1)}, bf16[4,32,1024]{2,1,0:T(8,128)(2,1)S(1)}, u32[]{:S(2)}, u32[]{:S(2)}) collective-permute-start(bf16[4,32,1024]{2,1,0:T(8,128)(2,1)S(1)} %shard_map.47.refs_0_), channel_id=1, source_target_pairs={{0,1},{16,20},{1,0},{17,21},{2,3},{18,22},{3,2},{19,23},{4,5},{20,... | collective-permute-start | bytes 786440 | tf_op jit(solution)/shard_map/ppermute | solution.py:41
  9.7 11.3 %collective-permute-start.5 = (bf16[4,32,1024]{2,1,0:T(8,128)(2,1)S(1)}, bf16[4,32,1024]{2,1,0:T(8,128)(2,1)S(1)}, u32[]{:S(2)}, u32[]{:S(2)}) collective-permute-start(bf16[4,32,1024]{2,1,0:T(8,128)(2,1)S(1)} %shard_map.47.refs_0_), channel_id=1, source_target_pairs={{0,3},{16,28},{1,2},{17,29},{2,1},{18,30},{3,0},{19,31},{4,7},{20,... | collective-permute-start | bytes 786440 | tf_op jit(solution)/shard_map/ppermute | solution.py:41
  11.5 9.4 %collective-permute-start.4 = (bf16[4,32,1024]{2,1,0:T(8,128)(2,1)S(1)}, bf16[4,32,1024]{2,1,0:T(8,128)(2,1)S(1)}, u32[]{:S(2)}, u32[]{:S(2)}) collective-permute-start(bf16[4,32,1024]{2,1,0:T(8,128)(2,1)S(1)} %shard_map.47.refs_0_), channel_id=1, source_target_pairs={{0,2},{16,24},{1,3},{17,25},{2,0},{18,26},{3,1},{19,27},{4,6},{20,... | collective-permute-start | bytes 786440 | tf_op jit(solution)/shard_map/ppermute | solution.py:41
  18.5 6.7 %collective-permute-start.6 = (bf16[4,2,32,896]{3,2,1,0:T(8,128)(2,1)S(1)}, bf16[4,2,32,896]{3,2,1,0:T(8,128)(2,1)S(1)}, u32[]{:S(2)}, u32[]{:S(2)}) collective-permute-start(bf16[4,2,32,896]{3,2,1,0:T(8,128)(2,1)S(1)} %get-tuple-element.35), channel_id=1, source_target_pairs={{0,16},{16,0},{1,17},{17,1},{2,18},{18,2},{3,19},{19,3},{4,20},{20... | collective-permute-start | bytes 1376264 | tf_op jit(solution)/shard_map/ppermute | solution.py:32
  22.2 3.0 %collective-permute-start.7 = (bf16[4,2,32,896]{3,2,1,0:T(8,128)(2,1)S(1)}, bf16[4,2,32,896]{3,2,1,0:T(8,128)(2,1)S(1)}, u32[]{:S(2)}, u32[]{:S(2)}) collective-permute-start(bf16[4,2,32,896]{3,2,1,0:T(8,128)(2,1)S(1)} %get-tuple-element.36), channel_id=1, source_target_pairs={{0,16},{16,0},{1,17},{17,1},{2,18},{18,2},{3,19},{19,3},{4,20},{20... | collective-permute-start | bytes 1376264 | tf_op jit(solution)/shard_map/ppermute | solution.py:32
  23.7 7.5 %collective-permute-start.8 = (bf16[4,2,32,768]{3,2,1,0:T(8,128)(2,1)S(1)}, bf16[4,2,32,768]{3,2,1,0:T(8,128)(2,1)S(1)}, u32[]{:S(2)}, u32[]{:S(2)}) collective-permute-start(bf16[4,2,32,768]{3,2,1,0:T(8,128)(2,1)S(1)} %get-tuple-element.40), channel_id=1, source_target_pairs={{0,16},{16,0},{1,17},{17,1},{2,18},{18,2},{3,19},{19,3},{4,20},{20... | collective-permute-start | bytes 1179656 | tf_op jit(solution)/shard_map/ppermute | solution.py:32
  24.8 6.4 %collective-permute-start.9 = (bf16[4,2,32,768]{3,2,1,0:T(8,128)(2,1)S(1)}, bf16[4,2,32,768]{3,2,1,0:T(8,128)(2,1)S(1)}, u32[]{:S(2)}, u32[]{:S(2)}) collective-permute-start(bf16[4,2,32,768]{3,2,1,0:T(8,128)(2,1)S(1)} %get-tuple-element.41), channel_id=1, source_target_pairs={{0,16},{16,0},{1,17},{17,1},{2,18},{18,2},{3,19},{19,3},{4,20},{20... | collective-permute-start | bytes 1179656 | tf_op jit(solution)/shard_map/ppermute | solution.py:32
  25.5 11.5 %collective-permute-start.10 = (bf16[4,2,32,896]{3,2,1,0:T(8,128)(2,1)S(1)}, bf16[4,2,32,896]{3,2,1,0:T(8,128)(2,1)S(1)}, u32[]{:S(2)}, u32[]{:S(2)}) collective-permute-start(bf16[4,2,32,896]{3,2,1,0:T(8,128)(2,1)S(1)} %get-tuple-element.37.refs_0_), channel_id=1, source_target_pairs={{0,32},{16,240},{32,0},{48,80},{64,96},{80,48},{96,64},{112,144},{... | collective-permute-start | bytes 1376264 | tf_op jit(solution)/shard_map/ppermute | solution.py:28
  31.4 10.2 %collective-permute-start.11 = (bf16[4,2,32,768]{3,2,1,0:T(8,128)(2,1)S(1)}, bf16[4,2,32,768]{3,2,1,0:T(8,128)(2,1)S(1)}, u32[]{:S(2)}, u32[]{:S(2)}) collective-permute-start(bf16[4,2,32,768]{3,2,1,0:T(8,128)(2,1)S(1)} %get-tuple-element.42.refs_0_), channel_id=1, source_target_pairs={{0,32},{16,240},{32,0},{48,80},{64,96},{80,48},{96,64},{112,144},{... | collective-permute-start | bytes 1179656 | tf_op jit(solution)/shard_map/ppermute | solution.py:28
  37.1 6.8 %collective-permute-start.12 = (bf16[2,2,32,896]{3,2,1,0:T(8,128)(2,1)S(1)}, bf16[2,2,32,896]{3,2,1,0:T(8,128)(2,1)S(1)}, u32[]{:S(2)}, u32[]{:S(2)}) collective-permute-start(bf16[2,2,32,896]{3,2,1,0:T(8,128)(2,1)S(1)} %get-tuple-element.44.refs_0_), channel_id=1, source_target_pairs={{0,224},{16,48},{32,64},{48,16},{64,32},{80,112},{96,128},{112,80}... | collective-permute-start | bytes 688136 | tf_op jit(solution)/shard_map/ppermute | solution.py:28
  41.6 6.4 %collective-permute-start.13 = (bf16[2,2,32,768]{3,2,1,0:T(8,128)(2,1)S(1)}, bf16[2,2,32,768]{3,2,1,0:T(8,128)(2,1)S(1)}, u32[]{:S(2)}, u32[]{:S(2)}) collective-permute-start(bf16[2,2,32,768]{3,2,1,0:T(8,128)(2,1)S(1)} %get-tuple-element.46.refs_0_), channel_id=1, source_target_pairs={{0,224},{16,48},{32,64},{48,16},{64,32},{80,112},{96,128},{112,80}... | collective-permute-start | bytes 589832 | tf_op jit(solution)/shard_map/ppermute | solution.py:28
  44.0 8.0 %collective-permute-start.14 = (bf16[1,2,32,896]{3,2,1,0:T(8,128)(2,1)S(1)}, bf16[1,2,32,896]{3,2,1,0:T(8,128)(2,1)S(1)}, u32[]{:S(2)}, u32[]{:S(2)}) collective-permute-start(bf16[1,2,32,896]{3,2,1,0:T(8,128)(2,1)S(1)} %get-tuple-element.48.refs_0_), channel_id=1, source_target_pairs={{0,96},{16,176},{32,192},{48,144},{64,160},{80,240},{96,0},{112,20... | collective-permute-start | bytes 344072 | tf_op jit(solution)/shard_map/ppermute | solution.py:28
  48.1 8.7 %collective-permute-start.15 = (bf16[1,2,32,768]{3,2,1,0:T(8,128)(2,1)S(1)}, bf16[1,2,32,768]{3,2,1,0:T(8,128)(2,1)S(1)}, u32[]{:S(2)}, u32[]{:S(2)}) collective-permute-start(bf16[1,2,32,768]{3,2,1,0:T(8,128)(2,1)S(1)} %get-tuple-element.50.refs_0_), channel_id=1, source_target_pairs={{0,96},{16,176},{32,192},{48,144},{64,160},{80,240},{96,0},{112,20... | collective-permute-start | bytes 294920 | tf_op jit(solution)/shard_map/ppermute | solution.py:28
  52.0 6.2 %collective-permute-start.16 = (bf16[1,32,896]{2,1,0:T(8,128)(2,1)S(1)}, bf16[1,32,896]{2,1,0:T(8,128)(2,1)S(1)}, u32[]{:S(2)}, u32[]{:S(2)}) collective-permute-start(bf16[1,32,896]{2,1,0:T(8,128)(2,1)S(1)} %shard_map.60.refs_0_.refs_1_), channel_id=1, source_target_pairs={{0,96},{16,176},{32,192},{48,144},{64,160},{80,240},{96,0},{112,20... | collective-permute-start | bytes 172040 | tf_op jit(solution)/shard_map/ppermute | solution.py:28
  58.2 9.7 %collective-permute-start.18 = (bf16[2,32,896]{2,1,0:T(8,128)(2,1)S(1)}, bf16[2,32,896]{2,1,0:T(8,128)(2,1)S(1)}, u32[]{:S(2)}, u32[]{:S(2)}) collective-permute-start(bf16[2,32,896]{2,1,0:T(8,128)(2,1)S(1)} %shard_map.62.refs_0_.refs_1_), channel_id=1, source_target_pairs={{0,224},{16,48},{32,64},{48,16},{64,32},{80,112},{96,128},{112,80}... | collective-permute-start | bytes 344072 | tf_op jit(solution)/shard_map/ppermute | solution.py:28
  61.3 5.9 %collective-permute-start.17 = (bf16[1,32,768]{2,1,0:T(8,128)(2,1)S(1)}, bf16[1,32,768]{2,1,0:T(8,128)(2,1)S(1)}, u32[]{:S(2)}, u32[]{:S(2)}) collective-permute-start(bf16[1,32,768]{2,1,0:T(8,128)(2,1)S(1)} %shard_map.61.refs_0_.refs_1_), channel_id=1, source_target_pairs={{0,96},{16,176},{32,192},{48,144},{64,160},{80,240},{96,0},{112,20... | collective-permute-start | bytes 147464 | tf_op jit(solution)/shard_map/ppermute | solution.py:28
  67.3 3.6 %collective-permute-start.19 = (bf16[2,32,768]{2,1,0:T(8,128)(2,1)S(1)}, bf16[2,32,768]{2,1,0:T(8,128)(2,1)S(1)}, u32[]{:S(2)}, u32[]{:S(2)}) collective-permute-start(bf16[2,32,768]{2,1,0:T(8,128)(2,1)S(1)} %shard_map.63.refs_0_.refs_1_), channel_id=1, source_target_pairs={{0,224},{16,48},{32,64},{48,16},{64,32},{80,112},{96,128},{112,80}... | collective-permute-start | bytes 294920 | tf_op jit(solution)/shard_map/ppermute | solution.py:28
  67.9 6.9 %collective-permute-start.20 = (bf16[4,32,896]{2,1,0:T(8,128)(2,1)S(1)}, bf16[4,32,896]{2,1,0:T(8,128)(2,1)S(1)}, u32[]{:S(2)}, u32[]{:S(2)}) collective-permute-start(bf16[4,32,896]{2,1,0:T(8,128)(2,1)S(1)} %shard_map.64.refs_0_.refs_1_), channel_id=1, source_target_pairs={{0,32},{16,240},{32,0},{48,80},{64,96},{80,48},{96,64},{112,144},{... | collective-permute-start | bytes 688136 | tf_op jit(solution)/shard_map/ppermute | solution.py:28
  70.8 9.3 %collective-permute-start.21 = (bf16[4,32,768]{2,1,0:T(8,128)(2,1)S(1)}, bf16[4,32,768]{2,1,0:T(8,128)(2,1)S(1)}, u32[]{:S(2)}, u32[]{:S(2)}) collective-permute-start(bf16[4,32,768]{2,1,0:T(8,128)(2,1)S(1)} %shard_map.65.refs_0_.refs_1_), channel_id=1, source_target_pairs={{0,32},{16,240},{32,0},{48,80},{64,96},{80,48},{96,64},{112,144},{... | collective-permute-start | bytes 589832 | tf_op jit(solution)/shard_map/ppermute | solution.py:28
  74.9 7.6 %collective-permute-start.23 = (bf16[8,32,896]{2,1,0:T(8,128)(2,1)S(1)}, bf16[8,32,896]{2,1,0:T(8,128)(2,1)S(1)}, u32[]{:S(2)}, u32[]{:S(2)}) collective-permute-start(bf16[8,32,896]{2,1,0:T(8,128)(2,1)S(1)} %shard_map.66.refs_0_), channel_id=1, source_target_pairs={{0,16},{16,0},{1,17},{17,1},{2,18},{18,2},{3,19},{19,3},{4,20},{20... | collective-permute-start | bytes 1376264 | tf_op jit(solution)/shard_map/ppermute | solution.py:32
  80.2 3.7 %collective-permute-start.22 = (bf16[8,32,768]{2,1,0:T(8,128)(2,1)S(1)}, bf16[8,32,768]{2,1,0:T(8,128)(2,1)S(1)}, u32[]{:S(2)}, u32[]{:S(2)}) collective-permute-start(bf16[8,32,768]{2,1,0:T(8,128)(2,1)S(1)} %shard_map.67.refs_0_), channel_id=1, source_target_pairs={{0,16},{16,0},{1,17},{17,1},{2,18},{18,2},{3,19},{19,3},{4,20},{20... | collective-permute-start | bytes 1179656 | tf_op jit(solution)/shard_map/ppermute | solution.py:32
  84.9 7.1 %collective-permute-start.24 = (bf16[4,32,1024]{2,1,0:T(8,128)(2,1)S(1)}, bf16[4,32,1024]{2,1,0:T(8,128)(2,1)S(1)}, u32[]{:S(2)}, u32[]{:S(2)}) collective-permute-start(bf16[4,32,1024]{2,1,0:T(8,128)(2,1)S(1)} %get-tuple-element.54), channel_id=1, source_target_pairs={{0,2},{16,24},{1,3},{17,25},{2,0},{18,26},{3,1},{19,27},{4,6},{20,... | collective-permute-start | bytes 786440 | tf_op jit(solution)/shard_map/ppermute | solution.py:41
  86.7 6.8 %collective-permute-start.25 = (bf16[4,32,1024]{2,1,0:T(8,128)(2,1)S(1)}, bf16[4,32,1024]{2,1,0:T(8,128)(2,1)S(1)}, u32[]{:S(2)}, u32[]{:S(2)}) collective-permute-start(bf16[4,32,1024]{2,1,0:T(8,128)(2,1)S(1)} %get-tuple-element.55), channel_id=1, source_target_pairs={{0,1},{16,20},{1,0},{17,21},{2,3},{18,22},{3,2},{19,23},{4,5},{20,... | collective-permute-start | bytes 786440 | tf_op jit(solution)/shard_map/ppermute | solution.py:41
  86.7 8.1 %collective-permute-start.26 = (bf16[4,32,1024]{2,1,0:T(8,128)(2,1)S(1)}, bf16[4,32,1024]{2,1,0:T(8,128)(2,1)S(1)}, u32[]{:S(2)}, u32[]{:S(2)}) collective-permute-start(bf16[4,32,1024]{2,1,0:T(8,128)(2,1)S(1)} %get-tuple-element.56), channel_id=1, source_target_pairs={{0,3},{16,28},{1,2},{17,29},{2,1},{18,30},{3,0},{19,31},{4,7},{20,... | collective-permute-start | bytes 786440 | tf_op jit(solution)/shard_map/ppermute | solution.py:41
  94.9 4.7 %collective-permute-start.27 = (bf16[32,1024]{1,0:T(8,128)(2,1)S(1)}, bf16[32,1024]{1,0:T(8,128)(2,1)S(1)}, u32[]{:S(2)}, u32[]{:S(2)}) collective-permute-start(bf16[32,1024]{1,0:T(8,128)(2,1)S(1)} %get-tuple-element.58), channel_id=1, source_target_pairs={{0,8},{16,18},{1,9},{17,19},{2,10},{18,16},{3,11},{19,17},{4,12},{... | collective-permute-start | bytes 196616 | tf_op jit(solution)/shard_map/ppermute | solution.py:41
  95.4 4.4 %collective-permute-start.28 = (bf16[32,1024]{1,0:T(8,128)(2,1)S(1)}, bf16[32,1024]{1,0:T(8,128)(2,1)S(1)}, u32[]{:S(2)}, u32[]{:S(2)}) collective-permute-start(bf16[32,1024]{1,0:T(8,128)(2,1)S(1)} %get-tuple-element.59), channel_id=1, source_target_pairs={{0,4},{16,17},{1,5},{17,16},{2,6},{18,19},{3,7},{19,18},{4,0},{20,... | collective-permute-start | bytes 196616 | tf_op jit(solution)/shard_map/ppermute | solution.py:41
  97.5 4.3 %collective-permute-start.29 = (bf16[32,1024]{1,0:T(8,128)(2,1)S(1)}, bf16[32,1024]{1,0:T(8,128)(2,1)S(1)}, u32[]{:S(2)}, u32[]{:S(2)}) collective-permute-start(bf16[32,1024]{1,0:T(8,128)(2,1)S(1)} %get-tuple-element.60), channel_id=1, source_target_pairs={{0,12},{16,19},{1,13},{17,18},{2,14},{18,17},{3,15},{19,16},{4,8},... | collective-permute-start | bytes 196616 | tf_op jit(solution)/shard_map/ppermute | solution.py:41

commit v4 on v3

--- a/solution.py
+++ b/solution.py
@@ -14,6 +14,7 @@
 OWNER = (0, 3, 4, 7, 1, 6, 2, 5)
 POSITION = sum(t << (4 * z) for t, z in enumerate(OWNER))
 STEPS = (1, -1, 3)
+FLIP = (0, 2, 1, 3)
 
 
 def partner(z, step):
@@ -78,12 +79,12 @@
     return call(body, [shape(*weight.shape)], weight, spec=ANY, scratch=sems, limit=48)[0]
 
 
-def join(*parts, after=()):
+def join(*parts, after=(), back=False):
     rows = [p.shape[0] for p in parts]
 
     def body(*refs):
         at = 0
-        for ref, n in zip(refs, rows):
+        for ref, n in list(zip(refs, rows))[:: -1 if back else 1]:
             refs[-1][at : at + n] = ref[...]
             at += n
 
@@ -241,7 +242,7 @@
 def sum_far(*parts):
     _, rows, columns = parts[0].shape
 
-    def body(a, c, b, d, keep, *sends):
+    def body(a, b, c, d, keep, *sends):
         core = lax.axis_index("core")
         for k in range(4):
             low, high = k ^ (2 * core), k ^ 2 ^ (2 * core)
@@ -265,10 +266,10 @@
 
 def on_device(acts, gate_weight, up_weight, down_weight):
     own = acts[None]
-    near = [swap_grid(own, k, 0) for k in (1, 2, 3)]
+    near = [swap_grid(own, FLIP[k], 0) for k in (3, 2, 1)]
     gate_weight = load(gate_weight)
-    piece = join(load(own), *near)
-    far = [swap_grid(piece, 0, j) for j in (1, 2, 3)]
+    piece = join(*near, load(own), back=True)
+    far = [swap_grid(piece, 0, FLIP[j]) for j in (1, 2, 3)]
     up_weight = load(up_weight)
     width = gate_weight.shape[1]
     cut = 896
@@ -307,8 +308,8 @@
     other_b = swap_core(hidden_b)
     total = expand(hidden_a, other_a, down_weight)
     terms = expand_rest(hidden_b, other_b, down_weight, total)
-    sums = sum_far(terms[0], *[swap_grid(terms[j], 0, j) for j in (2, 1, 3)])
-    return sum_near(sums[0], *[swap_grid(sums[k], k, 0) for k in (2, 1, 3)])
+    sums = sum_far(terms[0], *[swap_grid(terms[j], 0, FLIP[j]) for j in (1, 2, 3)])
+    return sum_near(sums[0], *[swap_grid(sums[k], FLIP[k], 0) for k in (1, 2, 3)])
 
 
 def solution(mesh):

time: 103 us -> 103 us (level)
  transfers between devices with their start and end apart: 30 -> 30, of which waited for: 17 -> 18; matrix products, arithmetic and copies ran while one was open for 0% -> 0% of each run, Pallas kernels for 12% -> 12%
where the time goes in v4:
time: 103 us
  starting transfers between devices  54.4 us (53%)
  waiting for transfers between devices  33.1 us (32%)
  Pallas kernels  14.3 us (14%)
    ppermute x12, starting transfers between devices, swap_z(): return lax.ppermute(v, ('z', 'core'), pairs)  27.9 us
    ppermute x12, waiting for transfers between devices, swap_z(): return lax.ppermute(v, ('z', 'core'), pairs)  18.8 us
    ppermute x12, starting transfers between devices, swap_grid(): return lax.ppermute(v, ('core', 'x', 'y'), pairs)  14.7 us
    pallas_call x26, Pallas kernels, call(): pl.pallas_call(lambda *refs: body(*refs[len(after):]), out_shape=outs, in...  14.3 us
    ppermute x12, waiting for transfers between devices, swap_grid(): return lax.ppermute(v, ('core', 'x', 'y'), pairs)  14.2 us
    ppermute x6, starting transfers between devices, swap_core(): return lax.ppermute(v, 'core', [(0, 1), (1, 0)])  11.8 us
  transfers between devices with their start and end apart: 30, of which 18 were waited for; matrix products, arithmetic and copies ran while one was open for 0% of the time, Pallas kernels for 12%

profile of v4, /device:TPU:1, one launch (start us, length us, event | category | flops | bytes accessed | tf_op | source)
XLA Modules:
  0.0 102.9 jit_solution(7815894414731288914)
XLA Ops:
  0.0 3.7 %collective-permute-start.2 = (bf16[1,32,1024]{2,1,0:T(8,128)(2,1)}, bf16[1,32,1024]{2,1,0:T(8,128)(2,1)S(1)}, u32[]{:S(2)}, u32[]{:S(2)}) collective-permute-start(bf16[1,32,1024]{2,1,0:T(8,128)(2,1)} %bitcast.1), channel_id=1, source_target_pairs={{0,8},{16,18},{1,9},{17,19},{2,10},{18,16},{3,11},{19,17},{4,12},{... | collective-permute-start | bytes 196616 | tf_op jit(solution)/shard_map/ppermute | solution.py:42
  3.7 0.4 collective-permute-start.1
  4.1 0.4 collective-permute-start
  4.5 0.9 copy-done
  5.5 0.1 collective-permute-done.2.refs_2_
  5.6 1.5 %collective-permute-done.1.refs_1_ = bf16[1,32,1024]{2,1,0:T(8,128)(2,1)S(1)} collective-permute-done((bf16[1,32,1024]{2,1,0:T(8,128)(2,1)}, bf16[1,32,1024]{2,1,0:T(8,128)(2,1)S(1)}, u32[]{:S(2)}, u32[]{:S(2)}) %collective-permute-start.1) | collective-permute-done | bytes 65568 | tf_op jit(solution)/shard_map/ppermute | solution.py:42
  7.1 1.8 %collective-permute-done.refs_0_ = bf16[1,32,1024]{2,1,0:T(8,128)(2,1)S(1)} collective-permute-done((bf16[1,32,1024]{2,1,0:T(8,128)(2,1)}, bf16[1,32,1024]{2,1,0:T(8,128)(2,1)S(1)}, u32[]{:S(2)}, u32[]{:S(2)}) %collective-permute-start) | collective-permute-done | bytes 65568 | tf_op jit(solution)/shard_map/ppermute | solution.py:42
  8.8 2.7 %collective-permute-start.3 = (bf16[4,32,1024]{2,1,0:T(8,128)(2,1)S(1)}, bf16[4,32,1024]{2,1,0:T(8,128)(2,1)S(1)}, u32[]{:S(2)}, u32[]{:S(2)}) collective-permute-start(bf16[4,32,1024]{2,1,0:T(8,128)(2,1)S(1)} %shard_map.47.refs_0_), channel_id=1, source_target_pairs={{0,2},{16,24},{1,3},{17,25},{2,0},{18,26},{3,1},{19,27},{4,6},{20,... | collective-permute-start | bytes 786440 | tf_op jit(solution)/shard_map/ppermute | solution.py:42
  11.5 0.9 collective-permute-start.5
  12.4 2.0 %shard_map.48.refs_2_.refs_3_ = bf16[1024,1664]{1,0:T(8,128)(2,1)S(1)} custom-call(bf16[1024,1664]{1,0:T(8,128)(2,1)} %refs_0_.3), custom_call_target="tpu_custom_call" | custom-call | flops 1 | bytes 1 | tf_op jit(solution)/shard_map/pallas_call | solution.py:61
  14.4 2.0 %shard_map.49.refs_3_.refs_4_ = bf16[1024,1664]{1,0:T(8,128)(2,1)S(1)} custom-call(bf16[1024,1664]{1,0:T(8,128)(2,1)} %refs_0_.4), custom_call_target="tpu_custom_call" | custom-call | flops 1 | bytes 1 | tf_op jit(solution)/shard_map/pallas_call | solution.py:61
  16.4 2.1 %shard_map.50 = (bf16[4,2,32,896]{3,2,1,0:T(8,128)(2,1)S(1)}, bf16[4,2,32,896]{3,2,1,0:T(8,128)(2,1)S(1)}, bf16[4,2,32,768]{3,2,1,0:T(8,128)(2,1)S(1)}, bf16[4,2,32,768]{3,2,1,0:T(8,128)(2,1)S(1)}) custom-call(bf16[4,32,1024]{2,1,0:T(8,128)(2,1)S(1)} %shard_map.47.refs_0_, bf16[4,32,1024]{2,1,0:T(8,128)(2,1)S(1)} %collective-permute-done.3.refs_1_, ...), custom_call_target="tpu_custom_call" | custom-call | flops 1 | bytes 1 | tf_op jit(solution)/shard_map/pallas_call | solution.py:61
  18.4 2.9 %collective-permute-start.6 = (bf16[4,2,32,896]{3,2,1,0:T(8,128)(2,1)S(1)}, bf16[4,2,32,896]{3,2,1,0:T(8,128)(2,1)S(1)}, u32[]{:S(2)}, u32[]{:S(2)}) collective-permute-start(bf16[4,2,32,896]{3,2,1,0:T(8,128)(2,1)S(1)} %get-tuple-element.35), channel_id=1, source_target_pairs={{0,16},{16,0},{1,17},{17,1},{2,18},{18,2},{3,19},{19,3},{4,20},{20... | collective-permute-start | bytes 1376264 | tf_op jit(solution)/shard_map/ppermute | solution.py:33
  21.3 1.3 %shard_map.51 = (bf16[4,2,32,896]{3,2,1,0:T(8,128)(2,1)S(1)}, bf16[4,2,32,896]{3,2,1,0:T(8,128)(2,1)S(1)}) custom-call(bf16[4,2,32,896]{3,2,1,0:T(8,128)(2,1)S(1)} %get-tuple-element.33.refs_0_, bf16[4,32,1024]{2,1,0:T(8,128)(2,1)S(1)} %collective-permute-done.4.refs_1_, bf16[4,32,1024]{2,1,0:T(8,128)(2,1)S(1)} %collective-permute-done.5.refs_2_, ...), custom_call_target="tpu_custom_call" | custom-call | flops 1 | bytes 1 | tf_op jit(solution)/shard_map/pallas_call | solution.py:61
  22.6 0.8 collective-permute-start.7
  23.3 0.1 collective-permute-start.8
  23.4 1.0 shard_map.53
  24.4 0.5 collective-permute-start.9
  24.9 0.2 shard_map.52
  25.2 5.7 %collective-permute-start.10 = (bf16[4,2,32,896]{3,2,1,0:T(8,128)(2,1)S(1)}, bf16[4,2,32,896]{3,2,1,0:T(8,128)(2,1)S(1)}, u32[]{:S(2)}, u32[]{:S(2)}) collective-permute-start(bf16[4,2,32,896]{3,2,1,0:T(8,128)(2,1)S(1)} %get-tuple-element.37.refs_0_), channel_id=1, source_target_pairs={{0,32},{16,240},{32,0},{48,80},{64,96},{80,48},{96,64},{112,144},{... | collective-permute-start | bytes 1376264 | tf_op jit(solution)/shard_map/ppermute | solution.py:29
  30.8 0.2 shard_map.54
  31.0 1.1 %collective-permute-start.11 = (bf16[4,2,32,768]{3,2,1,0:T(8,128)(2,1)S(1)}, bf16[4,2,32,768]{3,2,1,0:T(8,128)(2,1)S(1)}, u32[]{:S(2)}, u32[]{:S(2)}) collective-permute-start(bf16[4,2,32,768]{3,2,1,0:T(8,128)(2,1)S(1)} %get-tuple-element.42.refs_0_), channel_id=1, source_target_pairs={{0,32},{16,240},{32,0},{48,80},{64,96},{80,48},{96,64},{112,144},{... | collective-permute-start | bytes 1179656 | tf_op jit(solution)/shard_map/ppermute | solution.py:29
  32.1 4.6 %collective-permute-done.10.refs_1_ = bf16[4,2,32,896]{3,2,1,0:T(8,128)(2,1)S(1)} collective-permute-done((bf16[4,2,32,896]{3,2,1,0:T(8,128)(2,1)S(1)}, bf16[4,2,32,896]{3,2,1,0:T(8,128)(2,1)S(1)}, u32[]{:S(2)}, u32[]{:S(2)}) %collective-permute-start.10) | collective-permute-done | bytes 458784 | tf_op jit(solution)/shard_map/ppermute | solution.py:29
  36.7 0.1 shard_map.55
  36.8 0.1 collective-permute-start.12
  36.9 4.3 %collective-permute-done.11.refs_1_ = bf16[4,2,32,768]{3,2,1,0:T(8,128)(2,1)S(1)} collective-permute-done((bf16[4,2,32,768]{3,2,1,0:T(8,128)(2,1)S(1)}, bf16[4,2,32,768]{3,2,1,0:T(8,128)(2,1)S(1)}, u32[]{:S(2)}, u32[]{:S(2)}) %collective-permute-start.11) | collective-permute-done | bytes 393248 | tf_op jit(solution)/shard_map/ppermute | solution.py:29
  41.2 0.1 shard_map.56
  41.3 0.3 collective-permute-start.13
  41.6 2.0 %shard_map.57.refs_1_.refs_2_ = bf16[1664,1024]{1,0:T(8,128)(2,1)S(1)} custom-call(bf16[1664,1024]{1,0:T(8,128)(2,1)} %refs_0_.5), custom_call_target="tpu_custom_call" | custom-call | flops 1 | bytes 1 | tf_op jit(solution)/shard_map/pallas_call | solution.py:61
  43.6 4.1 %collective-permute-start.14 = (bf16[1,2,32,896]{3,2,1,0:T(8,128)(2,1)S(1)}, bf16[1,2,32,896]{3,2,1,0:T(8,128)(2,1)S(1)}, u32[]{:S(2)}, u32[]{:S(2)}) collective-permute-start(bf16[1,2,32,896]{3,2,1,0:T(8,128)(2,1)S(1)} %get-tuple-element.48.refs_0_), channel_id=1, source_target_pairs={{0,96},{16,176},{32,192},{48,144},{64,160},{80,240},{96,0},{112,20... | collective-permute-start | bytes 344072 | tf_op jit(solution)/shard_map/ppermute | solution.py:29
  47.7 1.0 collective-permute-start.15
  48.7 2.9 %collective-permute-done.14.refs_1_ = bf16[1,2,32,896]{3,2,1,0:T(8,128)(2,1)S(1)} collective-permute-done((bf16[1,2,32,896]{3,2,1,0:T(8,128)(2,1)S(1)}, bf16[1,2,32,896]{3,2,1,0:T(8,128)(2,1)S(1)}, u32[]{:S(2)}, u32[]{:S(2)}) %collective-permute-start.14) | collective-permute-done | bytes 114720 | tf_op jit(solution)/shard_map/ppermute | solution.py:29
  51.7 4.2 %collective-permute-start.16 = (bf16[1,32,896]{2,1,0:T(8,128)(2,1)S(1)}, bf16[1,32,896]{2,1,0:T(8,128)(2,1)S(1)}, u32[]{:S(2)}, u32[]{:S(2)}) collective-permute-start(bf16[1,32,896]{2,1,0:T(8,128)(2,1)S(1)} %shard_map.60.refs_0_.refs_1_), channel_id=1, source_target_pairs={{0,96},{16,176},{32,192},{48,144},{64,160},{80,240},{96,0},{112,20... | collective-permute-start | bytes 172040 | tf_op jit(solution)/shard_map/ppermute | solution.py:29
  55.8 0.6 collective-permute-done.15.refs_1_
  56.5 1.3 %collective-permute-done.16.refs_2_ = bf16[1,32,896]{2,1,0:T(8,128)(2,1)S(1)} collective-permute-done((bf16[1,32,896]{2,1,0:T(8,128)(2,1)S(1)}, bf16[1,32,896]{2,1,0:T(8,128)(2,1)S(1)}, u32[]{:S(2)}, u32[]{:S(2)}) %collective-permute-start.16) | collective-permute-done | bytes 57376 | tf_op jit(solution)/shard_map/ppermute | solution.py:29
  57.8 3.1 %collective-permute-start.18 = (bf16[2,32,896]{2,1,0:T(8,128)(2,1)S(1)}, bf16[2,32,896]{2,1,0:T(8,128)(2,1)S(1)}, u32[]{:S(2)}, u32[]{:S(2)}) collective-permute-start(bf16[2,32,896]{2,1,0:T(8,128)(2,1)S(1)} %shard_map.62.refs_0_.refs_1_), channel_id=1, source_target_pairs={{0,224},{16,48},{32,64},{48,16},{64,32},{80,112},{96,128},{112,80}... | collective-permute-start | bytes 344072 | tf_op jit(solution)/shard_map/ppermute | solution.py:29
  60.9 1.9 %collective-permute-start.17 = (bf16[1,32,768]{2,1,0:T(8,128)(2,1)S(1)}, bf16[1,32,768]{2,1,0:T(8,128)(2,1)S(1)}, u32[]{:S(2)}, u32[]{:S(2)}) collective-permute-start(bf16[1,32,768]{2,1,0:T(8,128)(2,1)S(1)} %shard_map.61.refs_0_.refs_1_), channel_id=1, source_target_pairs={{0,96},{16,176},{32,192},{48,144},{64,160},{80,240},{96,0},{112,20... | collective-permute-start | bytes 147464 | tf_op jit(solution)/shard_map/ppermute | solution.py:29
  62.9 4.0 %collective-permute-done.17.refs_2_ = bf16[1,32,768]{2,1,0:T(8,128)(2,1)S(1)} collective-permute-done((bf16[1,32,768]{2,1,0:T(8,128)(2,1)S(1)}, bf16[1,32,768]{2,1,0:T(8,128)(2,1)S(1)}, u32[]{:S(2)}, u32[]{:S(2)}) %collective-permute-start.17) | collective-permute-done | bytes 49184 | tf_op jit(solution)/shard_map/ppermute | solution.py:29
  66.9 0.6 collective-permute-start.19
  67.6 2.8 %collective-permute-start.20 = (bf16[4,32,896]{2,1,0:T(8,128)(2,1)S(1)}, bf16[4,32,896]{2,1,0:T(8,128)(2,1)S(1)}, u32[]{:S(2)}, u32[]{:S(2)}) collective-permute-start(bf16[4,32,896]{2,1,0:T(8,128)(2,1)S(1)} %shard_map.64.refs_0_.refs_1_), channel_id=1, source_target_pairs={{0,32},{16,240},{32,0},{48,80},{64,96},{80,48},{96,64},{112,144},{... | collective-permute-start | bytes 688136 | tf_op jit(solution)/shard_map/ppermute | solution.py:29
  70.3 0.1 collective-permute-done.19.refs_2_
  70.5 3.1 %collective-permute-start.21 = (bf16[4,32,768]{2,1,0:T(8,128)(2,1)S(1)}, bf16[4,32,768]{2,1,0:T(8,128)(2,1)S(1)}, u32[]{:S(2)}, u32[]{:S(2)}) collective-permute-start(bf16[4,32,768]{2,1,0:T(8,128)(2,1)S(1)} %shard_map.65.refs_0_.refs_1_), channel_id=1, source_target_pairs={{0,32},{16,240},{32,0},{48,80},{64,96},{80,48},{96,64},{112,144},{... | collective-permute-start | bytes 589832 | tf_op jit(solution)/shard_map/ppermute | solution.py:29
  73.6 0.9 collective-permute-done.20.refs_2_
  74.5 0.1 shard_map.66.refs_0_
  74.5 5.2 %collective-permute-start.23 = (bf16[8,32,896]{2,1,0:T(8,128)(2,1)S(1)}, bf16[8,32,896]{2,1,0:T(8,128)(2,1)S(1)}, u32[]{:S(2)}, u32[]{:S(2)}) collective-permute-start(bf16[8,32,896]{2,1,0:T(8,128)(2,1)S(1)} %shard_map.66.refs_0_), channel_id=1, source_target_pairs={{0,16},{16,0},{1,17},{17,1},{2,18},{18,2},{3,19},{19,3},{4,20},{20... | collective-permute-start | bytes 1376264 | tf_op jit(solution)/shard_map/ppermute | solution.py:33
  79.7 0.1 shard_map.67.refs_0_
  79.8 2.4 %collective-permute-start.22 = (bf16[8,32,768]{2,1,0:T(8,128)(2,1)S(1)}, bf16[8,32,768]{2,1,0:T(8,128)(2,1)S(1)}, u32[]{:S(2)}, u32[]{:S(2)}) collective-permute-start(bf16[8,32,768]{2,1,0:T(8,128)(2,1)S(1)} %shard_map.67.refs_0_), channel_id=1, source_target_pairs={{0,16},{16,0},{1,17},{17,1},{2,18},{18,2},{3,19},{19,3},{4,20},{20... | collective-permute-start | bytes 1179656 | tf_op jit(solution)/shard_map/ppermute | solution.py:33
  82.2 1.2 %shard_map.68.refs_3_ = f32[512,1024]{1,0:T(8,128)S(1)} custom-call(bf16[8,32,896]{2,1,0:T(8,128)(2,1)S(1)} %shard_map.66.refs_0_, bf16[8,32,896]{2,1,0:T(8,128)(2,1)S(1)} %collective-permute-done.23.refs_1_, bf16[1664,1024]{1,0:T(8,128)(2,1)S(1)} %shard_map.57.refs_1_.refs_2_), custom_call_target="tpu_custom_call" | custom-call | flops 1 | bytes 1 | tf_op jit(solution)/shard_map/pallas_call | solution.py:61
  83.4 0.1 collective-permute-done.22.refs_1_
  83.5 1.0 shard_map.69
  84.5 0.6 collective-permute-start.24
  85.1 0.3 collective-permute-start.25
  85.5 2.4 %collective-permute-start.26 = (bf16[4,32,1024]{2,1,0:T(8,128)(2,1)S(1)}, bf16[4,32,1024]{2,1,0:T(8,128)(2,1)S(1)}, u32[]{:S(2)}, u32[]{:S(2)}) collective-permute-start(bf16[4,32,1024]{2,1,0:T(8,128)(2,1)S(1)} %get-tuple-element.56), channel_id=1, source_target_pairs={{0,3},{16,28},{1,2},{17,29},{2,1},{18,30},{3,0},{19,31},{4,7},{20,... | collective-permute-start | bytes 786440 | tf_op jit(solution)/shard_map/ppermute | solution.py:42
  87.9 3.8 %collective-permute-done.24.refs_1_ = bf16[4,32,1024]{2,1,0:T(8,128)(2,1)S(1)} collective-permute-done((bf16[4,32,1024]{2,1,0:T(8,128)(2,1)S(1)}, bf16[4,32,1024]{2,1,0:T(8,128)(2,1)S(1)}, u32[]{:S(2)}, u32[]{:S(2)}) %collective-permute-start.24) | collective-permute-done | bytes 262176 | tf_op jit(solution)/shard_map/ppermute | solution.py:42
  91.7 0.6 collective-permute-done.25.refs_2_
  92.3 2.1 %collective-permute-done.26.refs_3_ = bf16[4,32,1024]{2,1,0:T(8,128)(2,1)S(1)} collective-permute-done((bf16[4,32,1024]{2,1,0:T(8,128)(2,1)S(1)}, bf16[4,32,1024]{2,1,0:T(8,128)(2,1)S(1)}, u32[]{:S(2)}, u32[]{:S(2)}) %collective-permute-start.26) | collective-permute-done | bytes 262176 | tf_op jit(solution)/shard_map/ppermute | solution.py:42
  94.4 0.1 shard_map.70
  94.6 2.0 %collective-permute-start.27 = (bf16[32,1024]{1,0:T(8,128)(2,1)S(1)}, bf16[32,1024]{1,0:T(8,128)(2,1)S(1)}, u32[]{:S(2)}, u32[]{:S(2)}) collective-permute-start(bf16[32,1024]{1,0:T(8,128)(2,1)S(1)} %get-tuple-element.58), channel_id=1, source_target_pairs={{0,8},{16,18},{1,9},{17,19},{2,10},{18,16},{3,11},{19,17},{4,12},{... | collective-permute-start | bytes 196616 | tf_op jit(solution)/shard_map/ppermute | solution.py:42
  96.5 1.1 %collective-permute-start.28 = (bf16[32,1024]{1,0:T(8,128)(2,1)S(1)}, bf16[32,1024]{1,0:T(8,128)(2,1)S(1)}, u32[]{:S(2)}, u32[]{:S(2)}) collective-permute-start(bf16[32,1024]{1,0:T(8,128)(2,1)S(1)} %get-tuple-element.59), channel_id=1, source_target_pairs={{0,4},{16,17},{1,5},{17,16},{2,6},{18,19},{3,7},{19,18},{4,0},{20,... | collective-permute-start | bytes 196616 | tf_op jit(solution)/shard_map/ppermute | solution.py:42
  97.6 0.3 collective-permute-start.29
  97.9 1.4 %collective-permute-done.27.refs_1_ = bf16[32,1024]{1,0:T(8,128)(2,1)S(1)} collective-permute-done((bf16[32,1024]{1,0:T(8,128)(2,1)S(1)}, bf16[32,1024]{1,0:T(8,128)(2,1)S(1)}, u32[]{:S(2)}, u32[]{:S(2)}) %collective-permute-start.27) | collective-permute-done | bytes 65568 | tf_op jit(solution)/shard_map/ppermute | solution.py:42
  99.3 0.7 collective-permute-done.28.refs_2_
  99.9 2.3 %collective-permute-done.29.refs_3_ = bf16[32,1024]{1,0:T(8,128)(2,1)S(1)} collective-permute-done((bf16[32,1024]{1,0:T(8,128)(2,1)S(1)}, bf16[32,1024]{1,0:T(8,128)(2,1)S(1)}, u32[]{:S(2)}, u32[]{:S(2)}) %collective-permute-start.29) | collective-permute-done | bytes 65568 | tf_op jit(solution)/shard_map/ppermute | solution.py:42
  102.2 0.7 shard_map.71
  (24 shorter events, 0.4 us)
Async XLA Ops:
  0.0 5.6 %collective-permute-start.2 = (bf16[1,32,1024]{2,1,0:T(8,128)(2,1)}, bf16[1,32,1024]{2,1,0:T(8,128)(2,1)S(1)}, u32[]{:S(2)}, u32[]{:S(2)}) collective-permute-start(bf16[1,32,1024]{2,1,0:T(8,128)(2,1)} %bitcast.1), channel_id=1, source_target_pairs={{0,8},{16,18},{1,9},{17,19},{2,10},{18,16},{3,11},{19,17},{4,12},{... | collective-permute-start | bytes 196616 | tf_op jit(solution)/shard_map/ppermute | solution.py:42
  3.7 3.3 %collective-permute-start.1 = (bf16[1,32,1024]{2,1,0:T(8,128)(2,1)}, bf16[1,32,1024]{2,1,0:T(8,128)(2,1)S(1)}, u32[]{:S(2)}, u32[]{:S(2)}) collective-permute-start(bf16[1,32,1024]{2,1,0:T(8,128)(2,1)} %bitcast.2), channel_id=1, source_target_pairs={{0,4},{16,17},{1,5},{17,16},{2,6},{18,19},{3,7},{19,18},{4,0},{20,... | collective-permute-start | bytes 196616 | tf_op jit(solution)/shard_map/ppermute | solution.py:42
  4.1 4.7 %collective-permute-start = (bf16[1,32,1024]{2,1,0:T(8,128)(2,1)}, bf16[1,32,1024]{2,1,0:T(8,128)(2,1)S(1)}, u32[]{:S(2)}, u32[]{:S(2)}) collective-permute-start(bf16[1,32,1024]{2,1,0:T(8,128)(2,1)} %bitcast.3), channel_id=1, source_target_pairs={{0,12},{16,19},{1,13},{17,18},{2,14},{18,17},{3,15},{19,16},{4,8},... | collective-permute-start | bytes 196616 | tf_op jit(solution)/shard_map/ppermute | solution.py:42
  4.5 0.9 copy-start
  8.8 7.5 %collective-permute-start.3 = (bf16[4,32,1024]{2,1,0:T(8,128)(2,1)S(1)}, bf16[4,32,1024]{2,1,0:T(8,128)(2,1)S(1)}, u32[]{:S(2)}, u32[]{:S(2)}) collective-permute-start(bf16[4,32,1024]{2,1,0:T(8,128)(2,1)S(1)} %shard_map.47.refs_0_), channel_id=1, source_target_pairs={{0,2},{16,24},{1,3},{17,25},{2,0},{18,26},{3,1},{19,27},{4,6},{20,... | collective-permute-start | bytes 786440 | tf_op jit(solution)/shard_map/ppermute | solution.py:42
  11.5 9.8 %collective-permute-start.5 = (bf16[4,32,1024]{2,1,0:T(8,128)(2,1)S(1)}, bf16[4,32,1024]{2,1,0:T(8,128)(2,1)S(1)}, u32[]{:S(2)}, u32[]{:S(2)}) collective-permute-start(bf16[4,32,1024]{2,1,0:T(8,128)(2,1)S(1)} %shard_map.47.refs_0_), channel_id=1, source_target_pairs={{0,3},{16,28},{1,2},{17,29},{2,1},{18,30},{3,0},{19,31},{4,7},{20,... | collective-permute-start | bytes 786440 | tf_op jit(solution)/shard_map/ppermute | solution.py:42
  12.4 8.9 %collective-permute-start.4 = (bf16[4,32,1024]{2,1,0:T(8,128)(2,1)S(1)}, bf16[4,32,1024]{2,1,0:T(8,128)(2,1)S(1)}, u32[]{:S(2)}, u32[]{:S(2)}) collective-permute-start(bf16[4,32,1024]{2,1,0:T(8,128)(2,1)S(1)} %shard_map.47.refs_0_), channel_id=1, source_target_pairs={{0,1},{16,20},{1,0},{17,21},{2,3},{18,22},{3,2},{19,23},{4,5},{20,... | collective-permute-start | bytes 786440 | tf_op jit(solution)/shard_map/ppermute | solution.py:42
  18.4 6.5 %collective-permute-start.6 = (bf16[4,2,32,896]{3,2,1,0:T(8,128)(2,1)S(1)}, bf16[4,2,32,896]{3,2,1,0:T(8,128)(2,1)S(1)}, u32[]{:S(2)}, u32[]{:S(2)}) collective-permute-start(bf16[4,2,32,896]{3,2,1,0:T(8,128)(2,1)S(1)} %get-tuple-element.35), channel_id=1, source_target_pairs={{0,16},{16,0},{1,17},{17,1},{2,18},{18,2},{3,19},{19,3},{4,20},{20... | collective-permute-start | bytes 1376264 | tf_op jit(solution)/shard_map/ppermute | solution.py:33
  22.6 2.4 %collective-permute-start.7 = (bf16[4,2,32,896]{3,2,1,0:T(8,128)(2,1)S(1)}, bf16[4,2,32,896]{3,2,1,0:T(8,128)(2,1)S(1)}, u32[]{:S(2)}, u32[]{:S(2)}) collective-permute-start(bf16[4,2,32,896]{3,2,1,0:T(8,128)(2,1)S(1)} %get-tuple-element.36), channel_id=1, source_target_pairs={{0,16},{16,0},{1,17},{17,1},{2,18},{18,2},{3,19},{19,3},{4,20},{20... | collective-permute-start | bytes 1376264 | tf_op jit(solution)/shard_map/ppermute | solution.py:33
  23.3 7.5 %collective-permute-start.8 = (bf16[4,2,32,768]{3,2,1,0:T(8,128)(2,1)S(1)}, bf16[4,2,32,768]{3,2,1,0:T(8,128)(2,1)S(1)}, u32[]{:S(2)}, u32[]{:S(2)}) collective-permute-start(bf16[4,2,32,768]{3,2,1,0:T(8,128)(2,1)S(1)} %get-tuple-element.40), channel_id=1, source_target_pairs={{0,16},{16,0},{1,17},{17,1},{2,18},{18,2},{3,19},{19,3},{4,20},{20... | collective-permute-start | bytes 1179656 | tf_op jit(solution)/shard_map/ppermute | solution.py:33
  24.4 6.4 %collective-permute-start.9 = (bf16[4,2,32,768]{3,2,1,0:T(8,128)(2,1)S(1)}, bf16[4,2,32,768]{3,2,1,0:T(8,128)(2,1)S(1)}, u32[]{:S(2)}, u32[]{:S(2)}) collective-permute-start(bf16[4,2,32,768]{3,2,1,0:T(8,128)(2,1)S(1)} %get-tuple-element.41), channel_id=1, source_target_pairs={{0,16},{16,0},{1,17},{17,1},{2,18},{18,2},{3,19},{19,3},{4,20},{20... | collective-permute-start | bytes 1179656 | tf_op jit(solution)/shard_map/ppermute | solution.py:33
  25.2 11.5 %collective-permute-start.10 = (bf16[4,2,32,896]{3,2,1,0:T(8,128)(2,1)S(1)}, bf16[4,2,32,896]{3,2,1,0:T(8,128)(2,1)S(1)}, u32[]{:S(2)}, u32[]{:S(2)}) collective-permute-start(bf16[4,2,32,896]{3,2,1,0:T(8,128)(2,1)S(1)} %get-tuple-element.37.refs_0_), channel_id=1, source_target_pairs={{0,32},{16,240},{32,0},{48,80},{64,96},{80,48},{96,64},{112,144},{... | collective-permute-start | bytes 1376264 | tf_op jit(solution)/shard_map/ppermute | solution.py:29
  31.0 10.2 %collective-permute-start.11 = (bf16[4,2,32,768]{3,2,1,0:T(8,128)(2,1)S(1)}, bf16[4,2,32,768]{3,2,1,0:T(8,128)(2,1)S(1)}, u32[]{:S(2)}, u32[]{:S(2)}) collective-permute-start(bf16[4,2,32,768]{3,2,1,0:T(8,128)(2,1)S(1)} %get-tuple-element.42.refs_0_), channel_id=1, source_target_pairs={{0,32},{16,240},{32,0},{48,80},{64,96},{80,48},{96,64},{112,144},{... | collective-permute-start | bytes 1179656 | tf_op jit(solution)/shard_map/ppermute | solution.py:29
  36.8 6.8 %collective-permute-start.12 = (bf16[2,2,32,896]{3,2,1,0:T(8,128)(2,1)S(1)}, bf16[2,2,32,896]{3,2,1,0:T(8,128)(2,1)S(1)}, u32[]{:S(2)}, u32[]{:S(2)}) collective-permute-start(bf16[2,2,32,896]{3,2,1,0:T(8,128)(2,1)S(1)} %get-tuple-element.44.refs_0_), channel_id=1, source_target_pairs={{0,224},{16,48},{32,64},{48,16},{64,32},{80,112},{96,128},{112,80}... | collective-permute-start | bytes 688136 | tf_op jit(solution)/shard_map/ppermute | solution.py:29
  41.3 6.4 %collective-permute-start.13 = (bf16[2,2,32,768]{3,2,1,0:T(8,128)(2,1)S(1)}, bf16[2,2,32,768]{3,2,1,0:T(8,128)(2,1)S(1)}, u32[]{:S(2)}, u32[]{:S(2)}) collective-permute-start(bf16[2,2,32,768]{3,2,1,0:T(8,128)(2,1)S(1)} %get-tuple-element.46.refs_0_), channel_id=1, source_target_pairs={{0,224},{16,48},{32,64},{48,16},{64,32},{80,112},{96,128},{112,80}... | collective-permute-start | bytes 589832 | tf_op jit(solution)/shard_map/ppermute | solution.py:29
  43.6 8.0 %collective-permute-start.14 = (bf16[1,2,32,896]{3,2,1,0:T(8,128)(2,1)S(1)}, bf16[1,2,32,896]{3,2,1,0:T(8,128)(2,1)S(1)}, u32[]{:S(2)}, u32[]{:S(2)}) collective-permute-start(bf16[1,2,32,896]{3,2,1,0:T(8,128)(2,1)S(1)} %get-tuple-element.48.refs_0_), channel_id=1, source_target_pairs={{0,96},{16,176},{32,192},{48,144},{64,160},{80,240},{96,0},{112,20... | collective-permute-start | bytes 344072 | tf_op jit(solution)/shard_map/ppermute | solution.py:29
  47.7 8.7 %collective-permute-start.15 = (bf16[1,2,32,768]{3,2,1,0:T(8,128)(2,1)S(1)}, bf16[1,2,32,768]{3,2,1,0:T(8,128)(2,1)S(1)}, u32[]{:S(2)}, u32[]{:S(2)}) collective-permute-start(bf16[1,2,32,768]{3,2,1,0:T(8,128)(2,1)S(1)} %get-tuple-element.50.refs_0_), channel_id=1, source_target_pairs={{0,96},{16,176},{32,192},{48,144},{64,160},{80,240},{96,0},{112,20... | collective-permute-start | bytes 294920 | tf_op jit(solution)/shard_map/ppermute | solution.py:29
  51.7 6.2 %collective-permute-start.16 = (bf16[1,32,896]{2,1,0:T(8,128)(2,1)S(1)}, bf16[1,32,896]{2,1,0:T(8,128)(2,1)S(1)}, u32[]{:S(2)}, u32[]{:S(2)}) collective-permute-start(bf16[1,32,896]{2,1,0:T(8,128)(2,1)S(1)} %shard_map.60.refs_0_.refs_1_), channel_id=1, source_target_pairs={{0,96},{16,176},{32,192},{48,144},{64,160},{80,240},{96,0},{112,20... | collective-permute-start | bytes 172040 | tf_op jit(solution)/shard_map/ppermute | solution.py:29
  57.8 9.7 %collective-permute-start.18 = (bf16[2,32,896]{2,1,0:T(8,128)(2,1)S(1)}, bf16[2,32,896]{2,1,0:T(8,128)(2,1)S(1)}, u32[]{:S(2)}, u32[]{:S(2)}) collective-permute-start(bf16[2,32,896]{2,1,0:T(8,128)(2,1)S(1)} %shard_map.62.refs_0_.refs_1_), channel_id=1, source_target_pairs={{0,224},{16,48},{32,64},{48,16},{64,32},{80,112},{96,128},{112,80}... | collective-permute-start | bytes 344072 | tf_op jit(solution)/shard_map/ppermute | solution.py:29
  60.9 5.9 %collective-permute-start.17 = (bf16[1,32,768]{2,1,0:T(8,128)(2,1)S(1)}, bf16[1,32,768]{2,1,0:T(8,128)(2,1)S(1)}, u32[]{:S(2)}, u32[]{:S(2)}) collective-permute-start(bf16[1,32,768]{2,1,0:T(8,128)(2,1)S(1)} %shard_map.61.refs_0_.refs_1_), channel_id=1, source_target_pairs={{0,96},{16,176},{32,192},{48,144},{64,160},{80,240},{96,0},{112,20... | collective-permute-start | bytes 147464 | tf_op jit(solution)/shard_map/ppermute | solution.py:29
  66.9 3.6 %collective-permute-start.19 = (bf16[2,32,768]{2,1,0:T(8,128)(2,1)S(1)}, bf16[2,32,768]{2,1,0:T(8,128)(2,1)S(1)}, u32[]{:S(2)}, u32[]{:S(2)}) collective-permute-start(bf16[2,32,768]{2,1,0:T(8,128)(2,1)S(1)} %shard_map.63.refs_0_.refs_1_), channel_id=1, source_target_pairs={{0,224},{16,48},{32,64},{48,16},{64,32},{80,112},{96,128},{112,80}... | collective-permute-start | bytes 294920 | tf_op jit(solution)/shard_map/ppermute | solution.py:29
  67.6 6.9 %collective-permute-start.20 = (bf16[4,32,896]{2,1,0:T(8,128)(2,1)S(1)}, bf16[4,32,896]{2,1,0:T(8,128)(2,1)S(1)}, u32[]{:S(2)}, u32[]{:S(2)}) collective-permute-start(bf16[4,32,896]{2,1,0:T(8,128)(2,1)S(1)} %shard_map.64.refs_0_.refs_1_), channel_id=1, source_target_pairs={{0,32},{16,240},{32,0},{48,80},{64,96},{80,48},{96,64},{112,144},{... | collective-permute-start | bytes 688136 | tf_op jit(solution)/shard_map/ppermute | solution.py:29
  70.5 9.3 %collective-permute-start.21 = (bf16[4,32,768]{2,1,0:T(8,128)(2,1)S(1)}, bf16[4,32,768]{2,1,0:T(8,128)(2,1)S(1)}, u32[]{:S(2)}, u32[]{:S(2)}) collective-permute-start(bf16[4,32,768]{2,1,0:T(8,128)(2,1)S(1)} %shard_map.65.refs_0_.refs_1_), channel_id=1, source_target_pairs={{0,32},{16,240},{32,0},{48,80},{64,96},{80,48},{96,64},{112,144},{... | collective-permute-start | bytes 589832 | tf_op jit(solution)/shard_map/ppermute | solution.py:29
  74.5 7.7 %collective-permute-start.23 = (bf16[8,32,896]{2,1,0:T(8,128)(2,1)S(1)}, bf16[8,32,896]{2,1,0:T(8,128)(2,1)S(1)}, u32[]{:S(2)}, u32[]{:S(2)}) collective-permute-start(bf16[8,32,896]{2,1,0:T(8,128)(2,1)S(1)} %shard_map.66.refs_0_), channel_id=1, source_target_pairs={{0,16},{16,0},{1,17},{17,1},{2,18},{18,2},{3,19},{19,3},{4,20},{20... | collective-permute-start | bytes 1376264 | tf_op jit(solution)/shard_map/ppermute | solution.py:33
  79.8 3.7 %collective-permute-start.22 = (bf16[8,32,768]{2,1,0:T(8,128)(2,1)S(1)}, bf16[8,32,768]{2,1,0:T(8,128)(2,1)S(1)}, u32[]{:S(2)}, u32[]{:S(2)}) collective-permute-start(bf16[8,32,768]{2,1,0:T(8,128)(2,1)S(1)} %shard_map.67.refs_0_), channel_id=1, source_target_pairs={{0,16},{16,0},{1,17},{17,1},{2,18},{18,2},{3,19},{19,3},{4,20},{20... | collective-permute-start | bytes 1179656 | tf_op jit(solution)/shard_map/ppermute | solution.py:33
  84.5 7.2 %collective-permute-start.24 = (bf16[4,32,1024]{2,1,0:T(8,128)(2,1)S(1)}, bf16[4,32,1024]{2,1,0:T(8,128)(2,1)S(1)}, u32[]{:S(2)}, u32[]{:S(2)}) collective-permute-start(bf16[4,32,1024]{2,1,0:T(8,128)(2,1)S(1)} %get-tuple-element.54), channel_id=1, source_target_pairs={{0,2},{16,24},{1,3},{17,25},{2,0},{18,26},{3,1},{19,27},{4,6},{20,... | collective-permute-start | bytes 786440 | tf_op jit(solution)/shard_map/ppermute | solution.py:42
  85.1 7.2 %collective-permute-start.25 = (bf16[4,32,1024]{2,1,0:T(8,128)(2,1)S(1)}, bf16[4,32,1024]{2,1,0:T(8,128)(2,1)S(1)}, u32[]{:S(2)}, u32[]{:S(2)}) collective-permute-start(bf16[4,32,1024]{2,1,0:T(8,128)(2,1)S(1)} %get-tuple-element.55), channel_id=1, source_target_pairs={{0,1},{16,20},{1,0},{17,21},{2,3},{18,22},{3,2},{19,23},{4,5},{20,... | collective-permute-start | bytes 786440 | tf_op jit(solution)/shard_map/ppermute | solution.py:42
  85.5 9.0 %collective-permute-start.26 = (bf16[4,32,1024]{2,1,0:T(8,128)(2,1)S(1)}, bf16[4,32,1024]{2,1,0:T(8,128)(2,1)S(1)}, u32[]{:S(2)}, u32[]{:S(2)}) collective-permute-start(bf16[4,32,1024]{2,1,0:T(8,128)(2,1)S(1)} %get-tuple-element.56), channel_id=1, source_target_pairs={{0,3},{16,28},{1,2},{17,29},{2,1},{18,30},{3,0},{19,31},{4,7},{20,... | collective-permute-start | bytes 786440 | tf_op jit(solution)/shard_map/ppermute | solution.py:42
  94.6 4.7 %collective-permute-start.27 = (bf16[32,1024]{1,0:T(8,128)(2,1)S(1)}, bf16[32,1024]{1,0:T(8,128)(2,1)S(1)}, u32[]{:S(2)}, u32[]{:S(2)}) collective-permute-start(bf16[32,1024]{1,0:T(8,128)(2,1)S(1)} %get-tuple-element.58), channel_id=1, source_target_pairs={{0,8},{16,18},{1,9},{17,19},{2,10},{18,16},{3,11},{19,17},{4,12},{... | collective-permute-start | bytes 196616 | tf_op jit(solution)/shard_map/ppermute | solution.py:42
  96.5 3.4 %collective-permute-start.28 = (bf16[32,1024]{1,0:T(8,128)(2,1)S(1)}, bf16[32,1024]{1,0:T(8,128)(2,1)S(1)}, u32[]{:S(2)}, u32[]{:S(2)}) collective-permute-start(bf16[32,1024]{1,0:T(8,128)(2,1)S(1)} %get-tuple-element.59), channel_id=1, source_target_pairs={{0,4},{16,17},{1,5},{17,16},{2,6},{18,19},{3,7},{19,18},{4,0},{20,... | collective-permute-start | bytes 196616 | tf_op jit(solution)/shard_map/ppermute | solution.py:42
  97.6 4.6 %collective-permute-start.29 = (bf16[32,1024]{1,0:T(8,128)(2,1)S(1)}, bf16[32,1024]{1,0:T(8,128)(2,1)S(1)}, u32[]{:S(2)}, u32[]{:S(2)}) collective-permute-start(bf16[32,1024]{1,0:T(8,128)(2,1)S(1)} %get-tuple-element.60), channel_id=1, source_target_pairs={{0,12},{16,19},{1,13},{17,18},{2,14},{18,17},{3,15},{19,16},{4,8},... | collective-permute-start | bytes 196616 | tf_op jit(solution)/shard_map/ppermute | solution.py:42

commit v5 on v4

--- a/solution.py
+++ b/solution.py
@@ -298,7 +298,7 @@
     have_b = activate(got_b, keep_b, after=(have_a,))
     got_b = swap_z(have_b, 2)
     for step in (1, 0):
-        have_a = join(have_a, got_a, after=(have_b,))
+        have_a = join(have_a, got_a, after=(got_b,) if step else (have_b,))
         got_a = swap_z(have_a, step)
         have_b = join(have_b, got_b, after=(have_a,))
         got_b = swap_z(have_b, step)

time: 103 us -> 103 us (level)
  waiting for transfers between devices: 33.1 us -> 36.2 us
  starting transfers between devices: 54.4 us -> 51.4 us
    ppermute x12, starting transfers between devices: 27.9 us -> 24.1 us  [swap_z(): return lax.ppermute(v, ('z', 'core'), pairs)]
    ppermute x12, waiting for transfers between devices: 18.8 us -> 21.9 us  [swap_z(): return lax.ppermute(v, ('z', 'core'), pairs)]
  transfers between devices with their start and end apart: 30 -> 30, of which waited for: 18 -> 17; matrix products, arithmetic and copies ran while one was open for 0% -> 0% of each run, Pallas kernels for 12% -> 12%
where the time goes in v5:
time: 103 us
  starting transfers between devices  51.4 us (50%)
  waiting for transfers between devices  36.2 us (35%)
  Pallas kernels  14.3 us (14%)
    ppermute x12, starting transfers between devices, swap_z(): return lax.ppermute(v, ('z', 'core'), pairs)  24.1 us
    ppermute x12, waiting for transfers between devices, swap_z(): return lax.ppermute(v, ('z', 'core'), pairs)  21.9 us
    ppermute x12, starting transfers between devices, swap_grid(): return lax.ppermute(v, ('core', 'x', 'y'), pairs)  14.7 us
    pallas_call x26, Pallas kernels, call(): pl.pallas_call(lambda *refs: body(*refs[len(after):]), out_shape=outs, in...  14.3 us
    ppermute x12, waiting for transfers between devices, swap_grid(): return lax.ppermute(v, ('core', 'x', 'y'), pairs)  14.2 us
    ppermute x6, starting transfers between devices, swap_core(): return lax.ppermute(v, 'core', [(0, 1), (1, 0)])  12.5 us
  transfers between devices with their start and end apart: 30, of which 17 were waited for; matrix products, arithmetic and copies ran while one was open for 0% of the time, Pallas kernels for 12%

profile of v5, /device:TPU:1, one launch (start us, length us, event | category | flops | bytes accessed | tf_op | source)
XLA Modules:
  0.0 103.0 jit_solution(9317727206808651485)
XLA Ops:
  0.0 3.7 %collective-permute-start.2 = (bf16[1,32,1024]{2,1,0:T(8,128)(2,1)}, bf16[1,32,1024]{2,1,0:T(8,128)(2,1)S(1)}, u32[]{:S(2)}, u32[]{:S(2)}) collective-permute-start(bf16[1,32,1024]{2,1,0:T(8,128)(2,1)} %bitcast.1), channel_id=1, source_target_pairs={{0,8},{16,18},{1,9},{17,19},{2,10},{18,16},{3,11},{19,17},{4,12},{... | collective-permute-start | bytes 196616 | tf_op jit(solution)/shard_map/ppermute | solution.py:42
  3.7 0.4 collective-permute-start.1
  4.1 0.4 collective-permute-start
  4.5 0.9 copy-done
  5.4 0.1 shard_map.46.refs_3_
  5.5 0.1 collective-permute-done.2.refs_2_
  5.6 1.5 %collective-permute-done.1.refs_1_ = bf16[1,32,1024]{2,1,0:T(8,128)(2,1)S(1)} collective-permute-done((bf16[1,32,1024]{2,1,0:T(8,128)(2,1)}, bf16[1,32,1024]{2,1,0:T(8,128)(2,1)S(1)}, u32[]{:S(2)}, u32[]{:S(2)}) %collective-permute-start.1) | collective-permute-done | bytes 65568 | tf_op jit(solution)/shard_map/ppermute | solution.py:42
  7.1 1.8 %collective-permute-done.refs_0_ = bf16[1,32,1024]{2,1,0:T(8,128)(2,1)S(1)} collective-permute-done((bf16[1,32,1024]{2,1,0:T(8,128)(2,1)}, bf16[1,32,1024]{2,1,0:T(8,128)(2,1)S(1)}, u32[]{:S(2)}, u32[]{:S(2)}) %collective-permute-start) | collective-permute-done | bytes 65568 | tf_op jit(solution)/shard_map/ppermute | solution.py:42
  8.8 2.7 %collective-permute-start.3 = (bf16[4,32,1024]{2,1,0:T(8,128)(2,1)S(1)}, bf16[4,32,1024]{2,1,0:T(8,128)(2,1)S(1)}, u32[]{:S(2)}, u32[]{:S(2)}) collective-permute-start(bf16[4,32,1024]{2,1,0:T(8,128)(2,1)S(1)} %shard_map.47.refs_0_), channel_id=1, source_target_pairs={{0,2},{16,24},{1,3},{17,25},{2,0},{18,26},{3,1},{19,27},{4,6},{20,... | collective-permute-start | bytes 786440 | tf_op jit(solution)/shard_map/ppermute | solution.py:42
  11.5 0.9 collective-permute-start.5
  12.4 2.0 %shard_map.48.refs_2_.refs_3_ = bf16[1024,1664]{1,0:T(8,128)(2,1)S(1)} custom-call(bf16[1024,1664]{1,0:T(8,128)(2,1)} %refs_0_.3), custom_call_target="tpu_custom_call" | custom-call | flops 1 | bytes 1 | tf_op jit(solution)/shard_map/pallas_call | solution.py:61
  14.4 2.0 %shard_map.49.refs_3_.refs_4_ = bf16[1024,1664]{1,0:T(8,128)(2,1)S(1)} custom-call(bf16[1024,1664]{1,0:T(8,128)(2,1)} %refs_0_.4), custom_call_target="tpu_custom_call" | custom-call | flops 1 | bytes 1 | tf_op jit(solution)/shard_map/pallas_call | solution.py:61
  16.4 2.1 %shard_map.50 = (bf16[4,2,32,896]{3,2,1,0:T(8,128)(2,1)S(1)}, bf16[4,2,32,896]{3,2,1,0:T(8,128)(2,1)S(1)}, bf16[4,2,32,768]{3,2,1,0:T(8,128)(2,1)S(1)}, bf16[4,2,32,768]{3,2,1,0:T(8,128)(2,1)S(1)}) custom-call(bf16[4,32,1024]{2,1,0:T(8,128)(2,1)S(1)} %shard_map.47.refs_0_, bf16[4,32,1024]{2,1,0:T(8,128)(2,1)S(1)} %collective-permute-done.3.refs_1_, ...), custom_call_target="tpu_custom_call" | custom-call | flops 1 | bytes 1 | tf_op jit(solution)/shard_map/pallas_call | solution.py:61
  18.4 2.9 %collective-permute-start.6 = (bf16[4,2,32,896]{3,2,1,0:T(8,128)(2,1)S(1)}, bf16[4,2,32,896]{3,2,1,0:T(8,128)(2,1)S(1)}, u32[]{:S(2)}, u32[]{:S(2)}) collective-permute-start(bf16[4,2,32,896]{3,2,1,0:T(8,128)(2,1)S(1)} %get-tuple-element.35), channel_id=1, source_target_pairs={{0,16},{16,0},{1,17},{17,1},{2,18},{18,2},{3,19},{19,3},{4,20},{20... | collective-permute-start | bytes 1376264 | tf_op jit(solution)/shard_map/ppermute | solution.py:33
  21.3 1.3 %shard_map.51 = (bf16[4,2,32,896]{3,2,1,0:T(8,128)(2,1)S(1)}, bf16[4,2,32,896]{3,2,1,0:T(8,128)(2,1)S(1)}) custom-call(bf16[4,2,32,896]{3,2,1,0:T(8,128)(2,1)S(1)} %get-tuple-element.33.refs_0_, bf16[4,32,1024]{2,1,0:T(8,128)(2,1)S(1)} %collective-permute-done.4.refs_1_, bf16[4,32,1024]{2,1,0:T(8,128)(2,1)S(1)} %collective-permute-done.5.refs_2_, ...), custom_call_target="tpu_custom_call" | custom-call | flops 1 | bytes 1 | tf_op jit(solution)/shard_map/pallas_call | solution.py:61
  22.6 0.8 collective-permute-start.7
  23.3 0.1 collective-permute-start.8
  23.4 1.0 shard_map.53
  24.4 0.5 collective-permute-start.9
  24.9 0.2 shard_map.52
  25.2 5.7 %collective-permute-start.10 = (bf16[4,2,32,896]{3,2,1,0:T(8,128)(2,1)S(1)}, bf16[4,2,32,896]{3,2,1,0:T(8,128)(2,1)S(1)}, u32[]{:S(2)}, u32[]{:S(2)}) collective-permute-start(bf16[4,2,32,896]{3,2,1,0:T(8,128)(2,1)S(1)} %get-tuple-element.37.refs_0_), channel_id=1, source_target_pairs={{0,32},{16,240},{32,0},{48,80},{64,96},{80,48},{96,64},{112,144},{... | collective-permute-start | bytes 1376264 | tf_op jit(solution)/shard_map/ppermute | solution.py:29
  30.8 0.2 shard_map.54
  31.0 1.1 %collective-permute-start.11 = (bf16[4,2,32,768]{3,2,1,0:T(8,128)(2,1)S(1)}, bf16[4,2,32,768]{3,2,1,0:T(8,128)(2,1)S(1)}, u32[]{:S(2)}, u32[]{:S(2)}) collective-permute-start(bf16[4,2,32,768]{3,2,1,0:T(8,128)(2,1)S(1)} %get-tuple-element.42.refs_0_), channel_id=1, source_target_pairs={{0,32},{16,240},{32,0},{48,80},{64,96},{80,48},{96,64},{112,144},{... | collective-permute-start | bytes 1179656 | tf_op jit(solution)/shard_map/ppermute | solution.py:29
  32.1 4.6 %collective-permute-done.10.refs_1_ = bf16[4,2,32,896]{3,2,1,0:T(8,128)(2,1)S(1)} collective-permute-done((bf16[4,2,32,896]{3,2,1,0:T(8,128)(2,1)S(1)}, bf16[4,2,32,896]{3,2,1,0:T(8,128)(2,1)S(1)}, u32[]{:S(2)}, u32[]{:S(2)}) %collective-permute-start.10) | collective-permute-done | bytes 458784 | tf_op jit(solution)/shard_map/ppermute | solution.py:29
  36.7 0.1 shard_map.55
  36.8 0.1 collective-permute-start.12
  36.9 4.3 %collective-permute-done.11.refs_1_ = bf16[4,2,32,768]{3,2,1,0:T(8,128)(2,1)S(1)} collective-permute-done((bf16[4,2,32,768]{3,2,1,0:T(8,128)(2,1)S(1)}, bf16[4,2,32,768]{3,2,1,0:T(8,128)(2,1)S(1)}, u32[]{:S(2)}, u32[]{:S(2)}) %collective-permute-start.11) | collective-permute-done | bytes 393248 | tf_op jit(solution)/shard_map/ppermute | solution.py:29
  41.2 0.1 shard_map.56
  41.3 0.3 collective-permute-start.13
  41.6 2.0 %shard_map.57.refs_1_.refs_2_ = bf16[1664,1024]{1,0:T(8,128)(2,1)S(1)} custom-call(bf16[1664,1024]{1,0:T(8,128)(2,1)} %refs_0_.5), custom_call_target="tpu_custom_call" | custom-call | flops 1 | bytes 1 | tf_op jit(solution)/shard_map/pallas_call | solution.py:61
  43.6 4.1 %collective-permute-start.14 = (bf16[1,2,32,896]{3,2,1,0:T(8,128)(2,1)S(1)}, bf16[1,2,32,896]{3,2,1,0:T(8,128)(2,1)S(1)}, u32[]{:S(2)}, u32[]{:S(2)}) collective-permute-start(bf16[1,2,32,896]{3,2,1,0:T(8,128)(2,1)S(1)} %get-tuple-element.48.refs_0_), channel_id=1, source_target_pairs={{0,96},{16,176},{32,192},{48,144},{64,160},{80,240},{96,0},{112,20... | collective-permute-start | bytes 344072 | tf_op jit(solution)/shard_map/ppermute | solution.py:29
  47.7 1.0 collective-permute-start.15
  48.7 2.9 %collective-permute-done.14.refs_1_ = bf16[1,2,32,896]{3,2,1,0:T(8,128)(2,1)S(1)} collective-permute-done((bf16[1,2,32,896]{3,2,1,0:T(8,128)(2,1)S(1)}, bf16[1,2,32,896]{3,2,1,0:T(8,128)(2,1)S(1)}, u32[]{:S(2)}, u32[]{:S(2)}) %collective-permute-start.14) | collective-permute-done | bytes 114720 | tf_op jit(solution)/shard_map/ppermute | solution.py:29
  51.7 4.2 %collective-permute-start.17 = (bf16[1,32,896]{2,1,0:T(8,128)(2,1)S(1)}, bf16[1,32,896]{2,1,0:T(8,128)(2,1)S(1)}, u32[]{:S(2)}, u32[]{:S(2)}) collective-permute-start(bf16[1,32,896]{2,1,0:T(8,128)(2,1)S(1)} %shard_map.60.refs_0_.refs_1_), channel_id=1, source_target_pairs={{0,96},{16,176},{32,192},{48,144},{64,160},{80,240},{96,0},{112,20... | collective-permute-start | bytes 172040 | tf_op jit(solution)/shard_map/ppermute | solution.py:29
  55.8 0.6 collective-permute-done.15.refs_1_
  56.5 2.6 %collective-permute-start.16 = (bf16[1,32,768]{2,1,0:T(8,128)(2,1)S(1)}, bf16[1,32,768]{2,1,0:T(8,128)(2,1)S(1)}, u32[]{:S(2)}, u32[]{:S(2)}) collective-permute-start(bf16[1,32,768]{2,1,0:T(8,128)(2,1)S(1)} %shard_map.61.refs_1_), channel_id=1, source_target_pairs={{0,96},{16,176},{32,192},{48,144},{64,160},{80,240},{96,0},{112,20... | collective-permute-start | bytes 147464 | tf_op jit(solution)/shard_map/ppermute | solution.py:29
  59.2 3.7 %collective-permute-done.16.refs_0_.refs_2_ = bf16[1,32,768]{2,1,0:T(8,128)(2,1)S(1)} collective-permute-done((bf16[1,32,768]{2,1,0:T(8,128)(2,1)S(1)}, bf16[1,32,768]{2,1,0:T(8,128)(2,1)S(1)}, u32[]{:S(2)}, u32[]{:S(2)}) %collective-permute-start.16) | collective-permute-done | bytes 49184 | tf_op jit(solution)/shard_map/ppermute | solution.py:29
  62.9 0.1 collective-permute-start.18
  63.0 1.5 %collective-permute-start.19 = (bf16[2,32,768]{2,1,0:T(8,128)(2,1)S(1)}, bf16[2,32,768]{2,1,0:T(8,128)(2,1)S(1)}, u32[]{:S(2)}, u32[]{:S(2)}) collective-permute-start(bf16[2,32,768]{2,1,0:T(8,128)(2,1)S(1)} %shard_map.63.refs_0_.refs_1_), channel_id=1, source_target_pairs={{0,224},{16,48},{32,64},{48,16},{64,32},{80,112},{96,128},{112,80}... | collective-permute-start | bytes 294920 | tf_op jit(solution)/shard_map/ppermute | solution.py:29
  64.5 2.1 %collective-permute-done.18.refs_2_ = bf16[2,32,896]{2,1,0:T(8,128)(2,1)S(1)} collective-permute-done((bf16[2,32,896]{2,1,0:T(8,128)(2,1)S(1)}, bf16[2,32,896]{2,1,0:T(8,128)(2,1)S(1)}, u32[]{:S(2)}, u32[]{:S(2)}) %collective-permute-start.18) | collective-permute-done | bytes 114720 | tf_op jit(solution)/shard_map/ppermute | solution.py:29
  66.6 2.5 %collective-permute-start.20 = (bf16[4,32,896]{2,1,0:T(8,128)(2,1)S(1)}, bf16[4,32,896]{2,1,0:T(8,128)(2,1)S(1)}, u32[]{:S(2)}, u32[]{:S(2)}) collective-permute-start(bf16[4,32,896]{2,1,0:T(8,128)(2,1)S(1)} %shard_map.64.refs_0_.refs_1_), channel_id=1, source_target_pairs={{0,32},{16,240},{32,0},{48,80},{64,96},{80,48},{96,64},{112,144},{... | collective-permute-start | bytes 688136 | tf_op jit(solution)/shard_map/ppermute | solution.py:29
  69.1 1.0 collective-permute-start.21
  70.2 3.7 %collective-permute-done.20.refs_2_ = bf16[4,32,896]{2,1,0:T(8,128)(2,1)S(1)} collective-permute-done((bf16[4,32,896]{2,1,0:T(8,128)(2,1)S(1)}, bf16[4,32,896]{2,1,0:T(8,128)(2,1)S(1)}, u32[]{:S(2)}, u32[]{:S(2)}) %collective-permute-start.20) | collective-permute-done | bytes 229408 | tf_op jit(solution)/shard_map/ppermute | solution.py:29
  73.8 0.1 shard_map.66.refs_0_
  73.9 6.2 %collective-permute-start.23 = (bf16[8,32,896]{2,1,0:T(8,128)(2,1)S(1)}, bf16[8,32,896]{2,1,0:T(8,128)(2,1)S(1)}, u32[]{:S(2)}, u32[]{:S(2)}) collective-permute-start(bf16[8,32,896]{2,1,0:T(8,128)(2,1)S(1)} %shard_map.66.refs_0_), channel_id=1, source_target_pairs={{0,16},{16,0},{1,17},{17,1},{2,18},{18,2},{3,19},{19,3},{4,20},{20... | collective-permute-start | bytes 1376264 | tf_op jit(solution)/shard_map/ppermute | solution.py:33
  80.2 0.1 shard_map.67.refs_0_
  80.2 2.0 %collective-permute-start.22 = (bf16[8,32,768]{2,1,0:T(8,128)(2,1)S(1)}, bf16[8,32,768]{2,1,0:T(8,128)(2,1)S(1)}, u32[]{:S(2)}, u32[]{:S(2)}) collective-permute-start(bf16[8,32,768]{2,1,0:T(8,128)(2,1)S(1)} %shard_map.67.refs_0_), channel_id=1, source_target_pairs={{0,16},{16,0},{1,17},{17,1},{2,18},{18,2},{3,19},{19,3},{4,20},{20... | collective-permute-start | bytes 1179656 | tf_op jit(solution)/shard_map/ppermute | solution.py:33
  82.3 1.2 %shard_map.68.refs_3_ = f32[512,1024]{1,0:T(8,128)S(1)} custom-call(bf16[8,32,896]{2,1,0:T(8,128)(2,1)S(1)} %shard_map.66.refs_0_, bf16[8,32,896]{2,1,0:T(8,128)(2,1)S(1)} %collective-permute-done.23.refs_1_, bf16[1664,1024]{1,0:T(8,128)(2,1)S(1)} %shard_map.57.refs_1_.refs_2_), custom_call_target="tpu_custom_call" | custom-call | flops 1 | bytes 1 | tf_op jit(solution)/shard_map/pallas_call | solution.py:61
  83.5 0.1 collective-permute-done.22.refs_1_
  83.6 1.0 shard_map.69
  84.6 0.6 collective-permute-start.24
  85.2 0.3 collective-permute-start.25
  85.5 2.4 %collective-permute-start.26 = (bf16[4,32,1024]{2,1,0:T(8,128)(2,1)S(1)}, bf16[4,32,1024]{2,1,0:T(8,128)(2,1)S(1)}, u32[]{:S(2)}, u32[]{:S(2)}) collective-permute-start(bf16[4,32,1024]{2,1,0:T(8,128)(2,1)S(1)} %get-tuple-element.56), channel_id=1, source_target_pairs={{0,3},{16,28},{1,2},{17,29},{2,1},{18,30},{3,0},{19,31},{4,7},{20,... | collective-permute-start | bytes 786440 | tf_op jit(solution)/shard_map/ppermute | solution.py:42
  87.9 3.8 %collective-permute-done.24.refs_1_ = bf16[4,32,1024]{2,1,0:T(8,128)(2,1)S(1)} collective-permute-done((bf16[4,32,1024]{2,1,0:T(8,128)(2,1)S(1)}, bf16[4,32,1024]{2,1,0:T(8,128)(2,1)S(1)}, u32[]{:S(2)}, u32[]{:S(2)}) %collective-permute-start.24) | collective-permute-done | bytes 262176 | tf_op jit(solution)/shard_map/ppermute | solution.py:42
  91.7 0.6 collective-permute-done.25.refs_2_
  92.4 2.1 %collective-permute-done.26.refs_3_ = bf16[4,32,1024]{2,1,0:T(8,128)(2,1)S(1)} collective-permute-done((bf16[4,32,1024]{2,1,0:T(8,128)(2,1)S(1)}, bf16[4,32,1024]{2,1,0:T(8,128)(2,1)S(1)}, u32[]{:S(2)}, u32[]{:S(2)}) %collective-permute-start.26) | collective-permute-done | bytes 262176 | tf_op jit(solution)/shard_map/ppermute | solution.py:42
  94.5 0.1 shard_map.70
  94.6 1.0 collective-permute-start.27
  95.6 2.1 %collective-permute-start.28 = (bf16[32,1024]{1,0:T(8,128)(2,1)S(1)}, bf16[32,1024]{1,0:T(8,128)(2,1)S(1)}, u32[]{:S(2)}, u32[]{:S(2)}) collective-permute-start(bf16[32,1024]{1,0:T(8,128)(2,1)S(1)} %get-tuple-element.59), channel_id=1, source_target_pairs={{0,4},{16,17},{1,5},{17,16},{2,6},{18,19},{3,7},{19,18},{4,0},{20,... | collective-permute-start | bytes 196616 | tf_op jit(solution)/shard_map/ppermute | solution.py:42
  97.7 0.3 collective-permute-start.29
  98.0 1.4 %collective-permute-done.27.refs_1_ = bf16[32,1024]{1,0:T(8,128)(2,1)S(1)} collective-permute-done((bf16[32,1024]{1,0:T(8,128)(2,1)S(1)}, bf16[32,1024]{1,0:T(8,128)(2,1)S(1)}, u32[]{:S(2)}, u32[]{:S(2)}) %collective-permute-start.27) | collective-permute-done | bytes 65568 | tf_op jit(solution)/shard_map/ppermute | solution.py:42
  99.4 0.7 collective-permute-done.28.refs_2_
  100.0 2.3 %collective-permute-done.29.refs_3_ = bf16[32,1024]{1,0:T(8,128)(2,1)S(1)} collective-permute-done((bf16[32,1024]{1,0:T(8,128)(2,1)S(1)}, bf16[32,1024]{1,0:T(8,128)(2,1)S(1)}, u32[]{:S(2)}, u32[]{:S(2)}) %collective-permute-start.29) | collective-permute-done | bytes 65568 | tf_op jit(solution)/shard_map/ppermute | solution.py:42
  102.3 0.7 shard_map.71
  (24 shorter events, 0.3 us)
Async XLA Ops:
  0.0 5.6 %collective-permute-start.2 = (bf16[1,32,1024]{2,1,0:T(8,128)(2,1)}, bf16[1,32,1024]{2,1,0:T(8,128)(2,1)S(1)}, u32[]{:S(2)}, u32[]{:S(2)}) collective-permute-start(bf16[1,32,1024]{2,1,0:T(8,128)(2,1)} %bitcast.1), channel_id=1, source_target_pairs={{0,8},{16,18},{1,9},{17,19},{2,10},{18,16},{3,11},{19,17},{4,12},{... | collective-permute-start | bytes 196616 | tf_op jit(solution)/shard_map/ppermute | solution.py:42
  3.7 3.3 %collective-permute-start.1 = (bf16[1,32,1024]{2,1,0:T(8,128)(2,1)}, bf16[1,32,1024]{2,1,0:T(8,128)(2,1)S(1)}, u32[]{:S(2)}, u32[]{:S(2)}) collective-permute-start(bf16[1,32,1024]{2,1,0:T(8,128)(2,1)} %bitcast.2), channel_id=1, source_target_pairs={{0,4},{16,17},{1,5},{17,16},{2,6},{18,19},{3,7},{19,18},{4,0},{20,... | collective-permute-start | bytes 196616 | tf_op jit(solution)/shard_map/ppermute | solution.py:42
  4.1 4.7 %collective-permute-start = (bf16[1,32,1024]{2,1,0:T(8,128)(2,1)}, bf16[1,32,1024]{2,1,0:T(8,128)(2,1)S(1)}, u32[]{:S(2)}, u32[]{:S(2)}) collective-permute-start(bf16[1,32,1024]{2,1,0:T(8,128)(2,1)} %bitcast.3), channel_id=1, source_target_pairs={{0,12},{16,19},{1,13},{17,18},{2,14},{18,17},{3,15},{19,16},{4,8},... | collective-permute-start | bytes 196616 | tf_op jit(solution)/shard_map/ppermute | solution.py:42
  4.5 0.9 copy-start
  8.8 7.5 %collective-permute-start.3 = (bf16[4,32,1024]{2,1,0:T(8,128)(2,1)S(1)}, bf16[4,32,1024]{2,1,0:T(8,128)(2,1)S(1)}, u32[]{:S(2)}, u32[]{:S(2)}) collective-permute-start(bf16[4,32,1024]{2,1,0:T(8,128)(2,1)S(1)} %shard_map.47.refs_0_), channel_id=1, source_target_pairs={{0,2},{16,24},{1,3},{17,25},{2,0},{18,26},{3,1},{19,27},{4,6},{20,... | collective-permute-start | bytes 786440 | tf_op jit(solution)/shard_map/ppermute | solution.py:42
  11.5 9.8 %collective-permute-start.5 = (bf16[4,32,1024]{2,1,0:T(8,128)(2,1)S(1)}, bf16[4,32,1024]{2,1,0:T(8,128)(2,1)S(1)}, u32[]{:S(2)}, u32[]{:S(2)}) collective-permute-start(bf16[4,32,1024]{2,1,0:T(8,128)(2,1)S(1)} %shard_map.47.refs_0_), channel_id=1, source_target_pairs={{0,3},{16,28},{1,2},{17,29},{2,1},{18,30},{3,0},{19,31},{4,7},{20,... | collective-permute-start | bytes 786440 | tf_op jit(solution)/shard_map/ppermute | solution.py:42
  12.4 8.9 %collective-permute-start.4 = (bf16[4,32,1024]{2,1,0:T(8,128)(2,1)S(1)}, bf16[4,32,1024]{2,1,0:T(8,128)(2,1)S(1)}, u32[]{:S(2)}, u32[]{:S(2)}) collective-permute-start(bf16[4,32,1024]{2,1,0:T(8,128)(2,1)S(1)} %shard_map.47.refs_0_), channel_id=1, source_target_pairs={{0,1},{16,20},{1,0},{17,21},{2,3},{18,22},{3,2},{19,23},{4,5},{20,... | collective-permute-start | bytes 786440 | tf_op jit(solution)/shard_map/ppermute | solution.py:42
  18.4 6.5 %collective-permute-start.6 = (bf16[4,2,32,896]{3,2,1,0:T(8,128)(2,1)S(1)}, bf16[4,2,32,896]{3,2,1,0:T(8,128)(2,1)S(1)}, u32[]{:S(2)}, u32[]{:S(2)}) collective-permute-start(bf16[4,2,32,896]{3,2,1,0:T(8,128)(2,1)S(1)} %get-tuple-element.35), channel_id=1, source_target_pairs={{0,16},{16,0},{1,17},{17,1},{2,18},{18,2},{3,19},{19,3},{4,20},{20... | collective-permute-start | bytes 1376264 | tf_op jit(solution)/shard_map/ppermute | solution.py:33
  22.6 2.4 %collective-permute-start.7 = (bf16[4,2,32,896]{3,2,1,0:T(8,128)(2,1)S(1)}, bf16[4,2,32,896]{3,2,1,0:T(8,128)(2,1)S(1)}, u32[]{:S(2)}, u32[]{:S(2)}) collective-permute-start(bf16[4,2,32,896]{3,2,1,0:T(8,128)(2,1)S(1)} %get-tuple-element.36), channel_id=1, source_target_pairs={{0,16},{16,0},{1,17},{17,1},{2,18},{18,2},{3,19},{19,3},{4,20},{20... | collective-permute-start | bytes 1376264 | tf_op jit(solution)/shard_map/ppermute | solution.py:33
  23.3 7.5 %collective-permute-start.8 = (bf16[4,2,32,768]{3,2,1,0:T(8,128)(2,1)S(1)}, bf16[4,2,32,768]{3,2,1,0:T(8,128)(2,1)S(1)}, u32[]{:S(2)}, u32[]{:S(2)}) collective-permute-start(bf16[4,2,32,768]{3,2,1,0:T(8,128)(2,1)S(1)} %get-tuple-element.40), channel_id=1, source_target_pairs={{0,16},{16,0},{1,17},{17,1},{2,18},{18,2},{3,19},{19,3},{4,20},{20... | collective-permute-start | bytes 1179656 | tf_op jit(solution)/shard_map/ppermute | solution.py:33
  24.4 6.4 %collective-permute-start.9 = (bf16[4,2,32,768]{3,2,1,0:T(8,128)(2,1)S(1)}, bf16[4,2,32,768]{3,2,1,0:T(8,128)(2,1)S(1)}, u32[]{:S(2)}, u32[]{:S(2)}) collective-permute-start(bf16[4,2,32,768]{3,2,1,0:T(8,128)(2,1)S(1)} %get-tuple-element.41), channel_id=1, source_target_pairs={{0,16},{16,0},{1,17},{17,1},{2,18},{18,2},{3,19},{19,3},{4,20},{20... | collective-permute-start | bytes 1179656 | tf_op jit(solution)/shard_map/ppermute | solution.py:33
  25.2 11.5 %collective-permute-start.10 = (bf16[4,2,32,896]{3,2,1,0:T(8,128)(2,1)S(1)}, bf16[4,2,32,896]{3,2,1,0:T(8,128)(2,1)S(1)}, u32[]{:S(2)}, u32[]{:S(2)}) collective-permute-start(bf16[4,2,32,896]{3,2,1,0:T(8,128)(2,1)S(1)} %get-tuple-element.37.refs_0_), channel_id=1, source_target_pairs={{0,32},{16,240},{32,0},{48,80},{64,96},{80,48},{96,64},{112,144},{... | collective-permute-start | bytes 1376264 | tf_op jit(solution)/shard_map/ppermute | solution.py:29
  31.0 10.2 %collective-permute-start.11 = (bf16[4,2,32,768]{3,2,1,0:T(8,128)(2,1)S(1)}, bf16[4,2,32,768]{3,2,1,0:T(8,128)(2,1)S(1)}, u32[]{:S(2)}, u32[]{:S(2)}) collective-permute-start(bf16[4,2,32,768]{3,2,1,0:T(8,128)(2,1)S(1)} %get-tuple-element.42.refs_0_), channel_id=1, source_target_pairs={{0,32},{16,240},{32,0},{48,80},{64,96},{80,48},{96,64},{112,144},{... | collective-permute-start | bytes 1179656 | tf_op jit(solution)/shard_map/ppermute | solution.py:29
  36.8 6.8 %collective-permute-start.12 = (bf16[2,2,32,896]{3,2,1,0:T(8,128)(2,1)S(1)}, bf16[2,2,32,896]{3,2,1,0:T(8,128)(2,1)S(1)}, u32[]{:S(2)}, u32[]{:S(2)}) collective-permute-start(bf16[2,2,32,896]{3,2,1,0:T(8,128)(2,1)S(1)} %get-tuple-element.44.refs_0_), channel_id=1, source_target_pairs={{0,224},{16,48},{32,64},{48,16},{64,32},{80,112},{96,128},{112,80}... | collective-permute-start | bytes 688136 | tf_op jit(solution)/shard_map/ppermute | solution.py:29
  41.3 6.4 %collective-permute-start.13 = (bf16[2,2,32,768]{3,2,1,0:T(8,128)(2,1)S(1)}, bf16[2,2,32,768]{3,2,1,0:T(8,128)(2,1)S(1)}, u32[]{:S(2)}, u32[]{:S(2)}) collective-permute-start(bf16[2,2,32,768]{3,2,1,0:T(8,128)(2,1)S(1)} %get-tuple-element.46.refs_0_), channel_id=1, source_target_pairs={{0,224},{16,48},{32,64},{48,16},{64,32},{80,112},{96,128},{112,80}... | collective-permute-start | bytes 589832 | tf_op jit(solution)/shard_map/ppermute | solution.py:29
  43.6 8.0 %collective-permute-start.14 = (bf16[1,2,32,896]{3,2,1,0:T(8,128)(2,1)S(1)}, bf16[1,2,32,896]{3,2,1,0:T(8,128)(2,1)S(1)}, u32[]{:S(2)}, u32[]{:S(2)}) collective-permute-start(bf16[1,2,32,896]{3,2,1,0:T(8,128)(2,1)S(1)} %get-tuple-element.48.refs_0_), channel_id=1, source_target_pairs={{0,96},{16,176},{32,192},{48,144},{64,160},{80,240},{96,0},{112,20... | collective-permute-start | bytes 344072 | tf_op jit(solution)/shard_map/ppermute | solution.py:29
  47.7 8.7 %collective-permute-start.15 = (bf16[1,2,32,768]{3,2,1,0:T(8,128)(2,1)S(1)}, bf16[1,2,32,768]{3,2,1,0:T(8,128)(2,1)S(1)}, u32[]{:S(2)}, u32[]{:S(2)}) collective-permute-start(bf16[1,2,32,768]{3,2,1,0:T(8,128)(2,1)S(1)} %get-tuple-element.50.refs_0_), channel_id=1, source_target_pairs={{0,96},{16,176},{32,192},{48,144},{64,160},{80,240},{96,0},{112,20... | collective-permute-start | bytes 294920 | tf_op jit(solution)/shard_map/ppermute | solution.py:29
  51.7 11.2 %collective-permute-start.17 = (bf16[1,32,896]{2,1,0:T(8,128)(2,1)S(1)}, bf16[1,32,896]{2,1,0:T(8,128)(2,1)S(1)}, u32[]{:S(2)}, u32[]{:S(2)}) collective-permute-start(bf16[1,32,896]{2,1,0:T(8,128)(2,1)S(1)} %shard_map.60.refs_0_.refs_1_), channel_id=1, source_target_pairs={{0,96},{16,176},{32,192},{48,144},{64,160},{80,240},{96,0},{112,20... | collective-permute-start | bytes 172040 | tf_op jit(solution)/shard_map/ppermute | solution.py:29
  56.5 6.3 %collective-permute-start.16 = (bf16[1,32,768]{2,1,0:T(8,128)(2,1)S(1)}, bf16[1,32,768]{2,1,0:T(8,128)(2,1)S(1)}, u32[]{:S(2)}, u32[]{:S(2)}) collective-permute-start(bf16[1,32,768]{2,1,0:T(8,128)(2,1)S(1)} %shard_map.61.refs_1_), channel_id=1, source_target_pairs={{0,96},{16,176},{32,192},{48,144},{64,160},{80,240},{96,0},{112,20... | collective-permute-start | bytes 147464 | tf_op jit(solution)/shard_map/ppermute | solution.py:29
  62.9 3.7 %collective-permute-start.18 = (bf16[2,32,896]{2,1,0:T(8,128)(2,1)S(1)}, bf16[2,32,896]{2,1,0:T(8,128)(2,1)S(1)}, u32[]{:S(2)}, u32[]{:S(2)}) collective-permute-start(bf16[2,32,896]{2,1,0:T(8,128)(2,1)S(1)} %shard_map.62.refs_0_.refs_1_), channel_id=1, source_target_pairs={{0,224},{16,48},{32,64},{48,16},{64,32},{80,112},{96,128},{112,80}... | collective-permute-start | bytes 344072 | tf_op jit(solution)/shard_map/ppermute | solution.py:29
  63.0 6.1 %collective-permute-start.19 = (bf16[2,32,768]{2,1,0:T(8,128)(2,1)S(1)}, bf16[2,32,768]{2,1,0:T(8,128)(2,1)S(1)}, u32[]{:S(2)}, u32[]{:S(2)}) collective-permute-start(bf16[2,32,768]{2,1,0:T(8,128)(2,1)S(1)} %shard_map.63.refs_0_.refs_1_), channel_id=1, source_target_pairs={{0,224},{16,48},{32,64},{48,16},{64,32},{80,112},{96,128},{112,80}... | collective-permute-start | bytes 294920 | tf_op jit(solution)/shard_map/ppermute | solution.py:29
  66.6 7.2 %collective-permute-start.20 = (bf16[4,32,896]{2,1,0:T(8,128)(2,1)S(1)}, bf16[4,32,896]{2,1,0:T(8,128)(2,1)S(1)}, u32[]{:S(2)}, u32[]{:S(2)}) collective-permute-start(bf16[4,32,896]{2,1,0:T(8,128)(2,1)S(1)} %shard_map.64.refs_0_.refs_1_), channel_id=1, source_target_pairs={{0,32},{16,240},{32,0},{48,80},{64,96},{80,48},{96,64},{112,144},{... | collective-permute-start | bytes 688136 | tf_op jit(solution)/shard_map/ppermute | solution.py:29
  69.1 11.0 %collective-permute-start.21 = (bf16[4,32,768]{2,1,0:T(8,128)(2,1)S(1)}, bf16[4,32,768]{2,1,0:T(8,128)(2,1)S(1)}, u32[]{:S(2)}, u32[]{:S(2)}) collective-permute-start(bf16[4,32,768]{2,1,0:T(8,128)(2,1)S(1)} %shard_map.65.refs_0_.refs_1_), channel_id=1, source_target_pairs={{0,32},{16,240},{32,0},{48,80},{64,96},{80,48},{96,64},{112,144},{... | collective-permute-start | bytes 589832 | tf_op jit(solution)/shard_map/ppermute | solution.py:29
  73.9 8.4 %collective-permute-start.23 = (bf16[8,32,896]{2,1,0:T(8,128)(2,1)S(1)}, bf16[8,32,896]{2,1,0:T(8,128)(2,1)S(1)}, u32[]{:S(2)}, u32[]{:S(2)}) collective-permute-start(bf16[8,32,896]{2,1,0:T(8,128)(2,1)S(1)} %shard_map.66.refs_0_), channel_id=1, source_target_pairs={{0,16},{16,0},{1,17},{17,1},{2,18},{18,2},{3,19},{19,3},{4,20},{20... | collective-permute-start | bytes 1376264 | tf_op jit(solution)/shard_map/ppermute | solution.py:33
  80.2 3.4 %collective-permute-start.22 = (bf16[8,32,768]{2,1,0:T(8,128)(2,1)S(1)}, bf16[8,32,768]{2,1,0:T(8,128)(2,1)S(1)}, u32[]{:S(2)}, u32[]{:S(2)}) collective-permute-start(bf16[8,32,768]{2,1,0:T(8,128)(2,1)S(1)} %shard_map.67.refs_0_), channel_id=1, source_target_pairs={{0,16},{16,0},{1,17},{17,1},{2,18},{18,2},{3,19},{19,3},{4,20},{20... | collective-permute-start | bytes 1179656 | tf_op jit(solution)/shard_map/ppermute | solution.py:33
  84.6 7.2 %collective-permute-start.24 = (bf16[4,32,1024]{2,1,0:T(8,128)(2,1)S(1)}, bf16[4,32,1024]{2,1,0:T(8,128)(2,1)S(1)}, u32[]{:S(2)}, u32[]{:S(2)}) collective-permute-start(bf16[4,32,1024]{2,1,0:T(8,128)(2,1)S(1)} %get-tuple-element.54), channel_id=1, source_target_pairs={{0,2},{16,24},{1,3},{17,25},{2,0},{18,26},{3,1},{19,27},{4,6},{20,... | collective-permute-start | bytes 786440 | tf_op jit(solution)/shard_map/ppermute | solution.py:42
  85.2 7.2 %collective-permute-start.25 = (bf16[4,32,1024]{2,1,0:T(8,128)(2,1)S(1)}, bf16[4,32,1024]{2,1,0:T(8,128)(2,1)S(1)}, u32[]{:S(2)}, u32[]{:S(2)}) collective-permute-start(bf16[4,32,1024]{2,1,0:T(8,128)(2,1)S(1)} %get-tuple-element.55), channel_id=1, source_target_pairs={{0,1},{16,20},{1,0},{17,21},{2,3},{18,22},{3,2},{19,23},{4,5},{20,... | collective-permute-start | bytes 786440 | tf_op jit(solution)/shard_map/ppermute | solution.py:42
  85.5 9.0 %collective-permute-start.26 = (bf16[4,32,1024]{2,1,0:T(8,128)(2,1)S(1)}, bf16[4,32,1024]{2,1,0:T(8,128)(2,1)S(1)}, u32[]{:S(2)}, u32[]{:S(2)}) collective-permute-start(bf16[4,32,1024]{2,1,0:T(8,128)(2,1)S(1)} %get-tuple-element.56), channel_id=1, source_target_pairs={{0,3},{16,28},{1,2},{17,29},{2,1},{18,30},{3,0},{19,31},{4,7},{20,... | collective-permute-start | bytes 786440 | tf_op jit(solution)/shard_map/ppermute | solution.py:42
  94.6 4.7 %collective-permute-start.27 = (bf16[32,1024]{1,0:T(8,128)(2,1)S(1)}, bf16[32,1024]{1,0:T(8,128)(2,1)S(1)}, u32[]{:S(2)}, u32[]{:S(2)}) collective-permute-start(bf16[32,1024]{1,0:T(8,128)(2,1)S(1)} %get-tuple-element.58), channel_id=1, source_target_pairs={{0,8},{16,18},{1,9},{17,19},{2,10},{18,16},{3,11},{19,17},{4,12},{... | collective-permute-start | bytes 196616 | tf_op jit(solution)/shard_map/ppermute | solution.py:42
  95.6 4.4 %collective-permute-start.28 = (bf16[32,1024]{1,0:T(8,128)(2,1)S(1)}, bf16[32,1024]{1,0:T(8,128)(2,1)S(1)}, u32[]{:S(2)}, u32[]{:S(2)}) collective-permute-start(bf16[32,1024]{1,0:T(8,128)(2,1)S(1)} %get-tuple-element.59), channel_id=1, source_target_pairs={{0,4},{16,17},{1,5},{17,16},{2,6},{18,19},{3,7},{19,18},{4,0},{20,... | collective-permute-start | bytes 196616 | tf_op jit(solution)/shard_map/ppermute | solution.py:42
  97.7 4.6 %collective-permute-start.29 = (bf16[32,1024]{1,0:T(8,128)(2,1)S(1)}, bf16[32,1024]{1,0:T(8,128)(2,1)S(1)}, u32[]{:S(2)}, u32[]{:S(2)}) collective-permute-start(bf16[32,1024]{1,0:T(8,128)(2,1)S(1)} %get-tuple-element.60), channel_id=1, source_target_pairs={{0,12},{16,19},{1,13},{17,18},{2,14},{18,17},{3,15},{19,16},{4,8},... | collective-permute-start | bytes 196616 | tf_op jit(solution)/shard_map/ppermute | solution.py:42
